TPU v7x, 256 devices: a whole 4x4x8 slice. The times are simulated.
256 devices in a mesh: prow: 32 (over z, x), pcol: 8 (over y, core).
Axes of the slice: x: 4, y: 4, z: 8, core: 2. Of those that a mesh axis runs over, the one named last changes fastest.
Arguments:
- matrix: bfloat16 [1, 16384, 4, 4096], P(None, 'prow', None, 'pcol'), may hold values from -6 to 6
- upper_inverse: bfloat16 [4, 512, 512], replicated, may hold values from -1.8 to 1.8
- lower_inverse: bfloat16 [4, 512, 512], replicated, may hold values from -0.079549513 to 0.079549513
- structure: int32 [32, 32], replicated, may hold values 0 or 1
Outputs:
- factored: float32 [1, 16384, 4, 4096], P(None, 'prow', None, 'pcol')
All inputs are finite; a program needn't handle non-finite values.
Results may differ from a plain program's by a relative error of at most 0.012.
Values may be sent and summed in bfloat16 or wider, within the bound.
No kernel may reach another device: no remote copies, remote signals or barrier semaphores. Data moves between devices by JAX's collectives and lax.ppermute only.
A program may use at most 64 MiB of HBM per device.

v0:
```python
import jax
import jax.numpy as jnp
from jax import lax
from jax.sharding import PartitionSpec as P


def from_root(block, axis, source):
    block = jnp.where(lax.axis_index(axis) == source, block, jnp.zeros_like(block))
    return lax.psum(block, axis)


def on_device(matrix, upper_inverse, lower_inverse, structure):
    rows_axis = lax.axis_size("prow")
    cols_axis = lax.axis_size("pcol")
    my_row = lax.axis_index("prow")
    my_col = lax.axis_index("pcol")
    row_blocks = matrix.shape[0]
    col_blocks = matrix.shape[2]
    steps = upper_inverse.shape[0]
    nblocks = row_blocks * rows_axis
    row_ids = jnp.arange(row_blocks) * rows_axis + my_row
    col_ids = jnp.arange(col_blocks) * cols_axis + my_col
    every_id = jnp.arange(nblocks)
    onehot_rows = (row_ids[:, None] == every_id[None, :]).astype(jnp.float32)
    onehot_cols = (col_ids[:, None] == every_id[None, :]).astype(jnp.float32)
    shape_f = structure.astype(jnp.float32)
    local_shape = jnp.dot(jnp.dot(onehot_rows, shape_f), onehot_cols.T)
    state = matrix.astype(jnp.float32)
    for k in range(steps):
        column = state[:, :, k // cols_axis, :]
        row_now = state[k // rows_axis]
        below = jnp.dot(onehot_rows, shape_f[:, k]) * (row_ids > k).astype(jnp.float32)
        right = jnp.dot(onehot_cols, shape_f[k, :]) * (col_ids > k).astype(jnp.float32)
        panels_lower = jnp.einsum(
            "iab,bc->iac",
            column.astype(jnp.bfloat16),
            upper_inverse[k],
            preferred_element_type=jnp.float32,
        )
        panels_lower = (panels_lower * below[:, None, None]).astype(jnp.bfloat16)
        panels_lower = from_root(panels_lower, "pcol", k % cols_axis)
        panels_upper = jnp.einsum(
            "ab,bjc->ajc",
            lower_inverse[k],
            row_now.astype(jnp.bfloat16),
            preferred_element_type=jnp.float32,
        )
        panels_upper = (panels_upper * right[None, :, None]).astype(jnp.bfloat16)
        panels_upper = from_root(panels_upper, "prow", k % rows_axis)
        keep = (
            local_shape
            * (row_ids > k).astype(jnp.float32)[:, None]
            * (col_ids > k).astype(jnp.float32)[None, :]
        )
        product = jnp.einsum(
            "iab,bjc->iajc", panels_lower, panels_upper, preferred_element_type=jnp.float32
        )
        state = state - keep[:, None, :, None] * product
        place_state = state
        col_here = k // cols_axis
        row_here = k // rows_axis
        owns_col = my_col == k % cols_axis
        owns_row = my_row == k % rows_axis
        lower_f = panels_lower.astype(jnp.float32)
        upper_f = panels_upper.astype(jnp.float32)
        put_col = jnp.logical_and(owns_col, (row_ids > k)[:, None, None])
        place_state = place_state.at[:, :, col_here, :].set(
            jnp.where(put_col, lower_f, place_state[:, :, col_here, :])
        )
        put_row = jnp.logical_and(owns_row, (col_ids > k)[None, :, None])
        place_state = place_state.at[row_here].set(
            jnp.where(put_row, upper_f, place_state[row_here])
        )
        state = place_state
    return state


def solution(mesh):
    return jax.shard_map(
        on_device,
        mesh=mesh,
        in_specs=(P(None, "prow", None, "pcol"), P(), P(), P()),
        out_specs=P(None, "prow", None, "pcol"),
        check_vma=False,
    )
```

profile of v0, /device:TPU:16, one launch (start us, length us, event | category | flops | bytes accessed | tf_op | source)
XLA Modules:
  0.0 957.0 jit_solution(4498528561369175468)
XLA Ops:
  6.5 0.7 convert_element_type.139
  7.3 0.2 slice_reduce_fusion
  7.5 0.7 fusion.63
  8.2 3.3 copy.15
  12.3 2.5 fusion.15
  14.9 0.2 fusion.16
  15.1 3.7 broadcast_select_fusion
  18.8 0.0 all-reduce.15.cloned.1.call-start
  18.9 0.6 fusion.64
  20.0 0.2 fusion.17
  20.2 0.2 multiply_select_fusion
  20.4 59.4 %all-reduce.11.cloned.1.call-done = bf16[1,512,512]{2,1,0:T(8,128)(2,1)} async-done(((bf16[1,512,512]{2,1,0:T(8,128)(2,1)}), bf16[1,512,512]{2,1,0:T(8,128)(2,1)}) %all-reduce.11.cloned.1.call-update) | async-done | bytes 524304 | tf_op jit(solution)/shard_map/psum | solution.py:9
  79.8 161.5 %all-reduce.9.cloned.1.call-done = bf16[512,4,512]{2,0,1:T(8,128)(2,1)} async-done(((bf16[512,4,512]{2,0,1:T(8,128)(2,1)}), bf16[512,4,512]{2,0,1:T(8,128)(2,1)}) %all-reduce.9.cloned.1.call-update) | async-done | bytes 2097168 | tf_op jit(solution)/shard_map/psum | solution.py:9
  241.3 3.2 bitcast_subtract_fusion
  244.5 0.5 copy.45
  245.0 0.5 copy-done.8
  245.6 0.2 fusion.31
  245.7 1.4 copy-done.3
  247.2 0.9 fusion
  248.1 1.1 copy-done
  249.2 1.3 copy-done.9
  250.5 2.3 fusion.13
  252.8 0.0 all-reduce.13.cloned.1.call-start
  252.9 4.3 select_bitcast_fusion.3
  257.2 0.0 all-reduce.19.cloned.1.call-start
  257.3 0.6 fusion.65
  258.6 0.2 fusion.18
  258.8 53.0 %all-reduce.15.cloned.1.call-done = bf16[1,512,512]{2,1,0:T(8,128)(2,1)} async-done(((bf16[1,512,512]{2,1,0:T(8,128)(2,1)}), bf16[1,512,512]{2,1,0:T(8,128)(2,1)}) %all-reduce.15.cloned.1.call-update) | async-done | bytes 524304 | tf_op jit(solution)/shard_map/psum | solution.py:9
  311.8 161.4 %all-reduce.13.cloned.1.call-done = bf16[512,4,512]{2,0,1:T(8,128)(2,1)} async-done(((bf16[512,4,512]{2,0,1:T(8,128)(2,1)}), bf16[512,4,512]{2,0,1:T(8,128)(2,1)}) %all-reduce.13.cloned.1.call-update) | async-done | bytes 2097168 | tf_op jit(solution)/shard_map/psum | solution.py:9
  473.2 4.2 multiply_subtract_fusion.2
  477.5 0.5 copy.48
  478.0 0.5 copy-done.13
  478.5 0.2 fusion.28
  478.7 0.9 copy-done.4
  479.6 0.9 fusion.1
  480.5 1.1 copy-done.1
  481.6 1.3 copy-done.10
  483.0 2.3 fusion.11
  485.3 0.0 all-reduce.17.cloned.1.call-start
  485.3 4.3 select_bitcast_fusion.2
  489.7 0.2 all-reduce.23.cloned.1.call-start
  489.9 0.6 fusion.66
  491.2 0.2 fusion.19
  491.4 52.9 %all-reduce.19.cloned.1.call-done = bf16[1,512,512]{2,1,0:T(8,128)(2,1)} async-done(((bf16[1,512,512]{2,1,0:T(8,128)(2,1)}), bf16[1,512,512]{2,1,0:T(8,128)(2,1)}) %all-reduce.19.cloned.1.call-update) | async-done | bytes 524304 | tf_op jit(solution)/shard_map/psum | solution.py:9
  544.3 161.4 %all-reduce.17.cloned.1.call-done = bf16[512,4,512]{2,0,1:T(8,128)(2,1)} async-done(((bf16[512,4,512]{2,0,1:T(8,128)(2,1)}), bf16[512,4,512]{2,0,1:T(8,128)(2,1)}) %all-reduce.17.cloned.1.call-update) | async-done | bytes 2097168 | tf_op jit(solution)/shard_map/psum | solution.py:9
  705.7 4.2 multiply_subtract_fusion.1
  709.9 0.5 copy.51
  710.4 0.5 copy-done.12
  711.0 0.2 fusion.25
  711.1 0.9 copy-done.5
  712.1 0.9 fusion.2
  713.0 1.1 copy-done.2
  714.1 1.3 copy-done.11
  715.4 2.3 fusion.9
  717.8 4.3 select_bitcast_fusion.1
  722.2 54.6 %all-reduce.23.cloned.1.call-done = bf16[1,512,512]{2,1,0:T(8,128)(2,1)} async-done(((bf16[1,512,512]{2,1,0:T(8,128)(2,1)}), bf16[1,512,512]{2,1,0:T(8,128)(2,1)}) %all-reduce.23.cloned.1.call-update) | async-done | bytes 524304 | tf_op jit(solution)/shard_map/psum | solution.py:9
  776.7 161.5 %all-reduce.21.cloned.1.call-done = bf16[512,4,512]{2,0,1:T(8,128)(2,1)} async-done(((bf16[512,4,512]{2,0,1:T(8,128)(2,1)}), bf16[512,4,512]{2,0,1:T(8,128)(2,1)}) %all-reduce.21.cloned.1.call-update) | async-done | bytes 2097168 | tf_op jit(solution)/shard_map/psum | solution.py:9
  938.3 4.2 multiply_subtract_fusion
  942.5 0.5 copy.54
  943.0 0.5 copy-done.14
  943.6 0.2 fusion.22
  943.7 0.9 copy-done.7
  944.7 0.8 select_bitcast_fusion
  945.5 4.7 copy.23
  (34 shorter events, 0.3 us)
Async XLA Ops:
  6.5 73.2 %all-reduce.11.cloned.1.call-start = ((), (), s32[]{:S(2)}) async-start(), calls=%async_computation.1 | async-start | bytes 1048576 | tf_op jit(solution)/shard_map/psum | solution.py:9
  11.5 3.6 copy-start.6
  14.8 226.5 %all-reduce.9.cloned.1.call-start = ((), (), s32[]{:S(2)}) async-start(), calls=%async_computation | async-start | bytes 4194304 | tf_op jit(solution)/shard_map/psum | solution.py:9
  18.8 1.4 copy-start.15
  18.8 293.0 %all-reduce.15.cloned.1.call-start = ((), (), s32[]{:S(2)}) async-start(), calls=%async_computation.3 | async-start | bytes 1048576 | tf_op jit(solution)/shard_map/psum | solution.py:9
  244.5 1.0 copy-start.8
  245.6 1.6 copy-start.3
  247.2 2.0 copy-start
  249.2 1.4 copy-start.9
  252.8 220.4 %all-reduce.13.cloned.1.call-start = ((), (), s32[]{:S(2)}) async-start(), calls=%async_computation.2 | async-start | bytes 4194304 | tf_op jit(solution)/shard_map/psum | solution.py:9
  257.2 287.0 %all-reduce.19.cloned.1.call-start = ((), (), s32[]{:S(2)}) async-start(), calls=%async_computation.5 | async-start | bytes 1048576 | tf_op jit(solution)/shard_map/psum | solution.py:9
  477.5 1.0 copy-start.13
  478.0 1.6 copy-start.4
  479.6 2.0 copy-start.1
  481.6 1.4 copy-start.10
  485.3 220.4 %all-reduce.17.cloned.1.call-start = ((), (), s32[]{:S(2)}) async-start(), calls=%async_computation.4 | async-start | bytes 4194304 | tf_op jit(solution)/shard_map/psum | solution.py:9
  489.7 287.0 %all-reduce.23.cloned.1.call-start = ((), (), s32[]{:S(2)}) async-start(), calls=%async_computation.7 | async-start | bytes 1048576 | tf_op jit(solution)/shard_map/psum | solution.py:9
  709.9 1.0 copy-start.12
  710.4 1.6 copy-start.5
  712.1 2.0 copy-start.2
  714.1 1.4 copy-start.11
  717.8 220.5 %all-reduce.21.cloned.1.call-start = ((), (), s32[]{:S(2)}) async-start(), calls=%async_computation.6 | async-start | bytes 4194304 | tf_op jit(solution)/shard_map/psum | solution.py:9
  942.5 1.0 copy-start.14
  943.0 1.6 copy-start.7
Sparse Core Ops, SparseCore 0:
  14.9 64.7 all-reduce.10
  83.7 157.5 all-reduce.8
  253.0 58.8 all-reduce.14
  315.6 157.5 all-reduce.12
  485.4 58.8 all-reduce.18
  548.1 157.5 all-reduce.16
  717.9 58.8 all-reduce.22
  780.7 157.5 all-reduce.20
where the time goes:
time: 958 us; the launch traced here: 957 us
  waiting for transfers between devices  866 us (90%)
  matrix products  42.9 us (4%)
  local copies, waits for them, and re-layouts  23.8 us (2%)
  between operations  16.5 us (2%)
    psum x8, waiting for transfers between devices, from_root(): return lax.psum(block, axis)  866 us
  transfers between devices with their start and end apart: 8, of which 8 were waited for; matrix products, arithmetic and copies ran while one was open for 2% of the time, Pallas kernels for 0%

commit v1 on v0

v1 whole, which is shorter than its diff:
```python
import functools

import jax
import jax.numpy as jnp
from jax import lax
from jax.experimental import pallas as pl
from jax.experimental.pallas import tpu as pltpu
from jax.sharding import PartitionSpec as P

STEPS = 4
HALF = jnp.bfloat16
FULL = jnp.float32
VMEM_LIMIT = 56 * 1024 * 1024


def mm(a, b):
    return jnp.dot(a, b, preferred_element_type=FULL)


def factor_kernel(ids, shape, mine, other, row, v, w, low, left, up):
    n = v.shape[1]
    p = ids[0]
    core = ids[2]

    def raw(i, j):
        a = jnp.concatenate([mine[z * 4 + i, 4 + j % 2] for z in range(8)], axis=0)
        b = jnp.concatenate([other[z * 4 + i, j % 2] for z in range(8)], axis=0)
        return jnp.where(core == j // 2, a, b)

    def cut(k):
        return slice(k * n, (k + 1) * n)

    for k in range(3):
        for i in range(k + 1, 4):
            block = raw(i, k)
            if k:
                block = (block.astype(FULL) - mm(low[i - 1, :, 0 : k * n], up[0 : k * n, cut(k)])).astype(HALF)
            low[i - 1, :, cut(k)] = (mm(block, v[k]) * shape[i, k].astype(FULL)).astype(HALF)
        for j in range(k + 1, 4):
            block = raw(k, j)
            if k:
                block = (block.astype(FULL) - mm(low[k - 1, :, 0 : k * n], up[0 : k * n, cut(j)])).astype(HALF)
            up[cut(k), cut(j)] = (mm(w[k], block) * shape[k, j].astype(FULL)).astype(HALF)
    for k in range(4):
        block = row[k]
        if k:
            block = (block.astype(FULL) - mm(left[:, 0 : k * n], up[0 : k * n, cut(k)])).astype(HALF)
        scale = jnp.where(p > k, shape[p, k], 0).astype(FULL)
        left[:, cut(k)] = (mm(block, v[k]) * scale).astype(HALF)


def column_kernel(ids, shape, raw, own, low, left, w, out, upper):
    n = w.shape[1]
    p, q = ids[0], ids[1]
    c = pl.program_id(0)
    j = c * 8 + q
    for k in range(4):
        block = jnp.concatenate([raw[z * 4 + k, 0] for z in range(8)], axis=0)
        if k:
            block = (block.astype(FULL) - mm(low[k - 1, :, 0 : k * n], upper[0 : k * n, :])).astype(HALF)
        scale = jnp.where(j > k, shape[k, j], 0).astype(FULL)
        upper[k * n : (k + 1) * n, :] = (mm(w[k], block) * scale).astype(HALF)
    keep = shape[p, j].astype(FULL)
    out[0] = own[0].astype(FULL) - keep * mm(left[...], upper[...])

    @pl.when(jnp.logical_and(p < STEPS, j > p))
    def _():
        out[0] = upper[pl.ds(pl.multiple_of(jnp.minimum(p, 3) * n, n), n), :].astype(FULL)

    @pl.when(jnp.logical_and(j < STEPS, p > j))
    def _():
        out[0] = left[:, pl.ds(pl.multiple_of(jnp.minimum(j, 3) * n, n), n)].astype(FULL)


def factor(ids, shape, mine, other, row, v, w):
    n = v.shape[1]
    vmem = pl.BlockSpec(memory_space=pltpu.VMEM)
    smem = pl.BlockSpec(memory_space=pltpu.SMEM)
    return pl.pallas_call(
        factor_kernel,
        out_shape=(
            jax.ShapeDtypeStruct((3, n, 3 * n), HALF),
            jax.ShapeDtypeStruct((n, 4 * n), HALF),
        ),
        in_specs=[smem, smem, vmem, vmem, vmem, vmem, vmem],
        out_specs=(vmem, vmem),
        scratch_shapes=[pltpu.VMEM((3 * n, 4 * n), HALF)],
        compiler_params=pltpu.CompilerParams(vmem_limit_bytes=VMEM_LIMIT),
        cost_estimate=pl.CostEstimate(flops=60 * n**3, bytes_accessed=18 * 2**20, transcendentals=0),
    )(ids, shape, mine, other, row, v, w)


def columns(ids, shape, raw, own, low, left, w):
    n = w.shape[1]
    smem = pl.BlockSpec(memory_space=pltpu.SMEM)
    whole = lambda a: pl.BlockSpec(a.shape, lambda c: (0,) * a.ndim)
    return pl.pallas_call(
        column_kernel,
        grid=(4,),
        out_shape=jax.ShapeDtypeStruct((4, n, n), FULL),
        in_specs=[
            smem,
            smem,
            pl.BlockSpec((32, 1, n // 8, n), lambda c: (0, c, 0, 0)),
            pl.BlockSpec((1, n, n), lambda c: (c, 0, 0)),
            whole(low),
            whole(left),
            whole(w),
        ],
        out_specs=pl.BlockSpec((1, n, n), lambda c: (c, 0, 0)),
        scratch_shapes=[pltpu.VMEM((4 * n, n), HALF)],
        compiler_params=pltpu.CompilerParams(vmem_limit_bytes=VMEM_LIMIT),
        cost_estimate=pl.CostEstimate(flops=112 * n**3, bytes_accessed=24 * 2**20, transcendentals=0),
    )(ids, shape, raw, own, low, left, w)


def on_device(matrix, upper_inverse, lower_inverse, structure):
    p = lax.axis_index("prow")
    q = lax.axis_index("pcol")
    z = p // 4
    core = lax.rem(q, 2)
    n = matrix.shape[1]
    part = n // 8
    own = jnp.transpose(matrix[0], (1, 0, 2))
    ids = jnp.stack([p, q, core]).astype(jnp.int32)

    piece = own[:, :part]
    for s in range(1, 8):
        to = [(x, x + 4 * s) for x in range(4)]
        came = lax.ppermute(own[:, s * part : (s + 1) * part], "prow", to)
        piece = jnp.where(z == s, came, piece)

    row = lax.all_gather(own[0], "pcol")[:4]

    corner = lax.all_gather(piece[0], "pcol")
    corner = jnp.where(core == 0, corner[0:2], corner[2:4])

    raw = lax.all_gather(jnp.concatenate([piece, corner], axis=0), "prow")
    other = lax.ppermute(raw[:, 4:6], "pcol", [(i, i ^ 1) for i in range(8)])

    low, left = factor(ids, structure, raw, other, row, upper_inverse, lower_inverse)
    out = columns(ids, structure, raw, own, low, left, lower_inverse)
    return jnp.transpose(out, (1, 0, 2))[None]


def solution(mesh):
    return jax.shard_map(
        on_device,
        mesh=mesh,
        in_specs=(P(None, "prow", None, "pcol"), P(), P(), P()),
        out_specs=P(None, "prow", None, "pcol"),
        check_vma=False,
    )
```

time: 958 us -> 266 us (0.28)
  waiting for transfers between devices: 866 us -> 159 us
  matrix products: 42.9 us -> 0 us
  Pallas kernels: 0 us -> 40.5 us
  starting transfers between devices: 0.48 us -> 18.5 us
  blocking collectives: 0 us -> 11.9 us
    psum x8 -> x0, waiting for transfers between devices: 866 us -> none  [from_root(): return lax.psum(block, axis)]
    all_gather x0 -> x2, waiting for transfers between devices: none -> 147 us  [the longest x1 120 us: on_device(): raw = lax.all_gather(jnp.concatenate([piece, corner], axis=0), 'prow')]
    dot_general x17 -> x0, matrix products: 42.9 us -> none  [the longest x4 16.7 us: on_device(): jnp.einsum('ab,bjc->ajc', lower_inverse[k], row_now.astype(jnp.bfloat16),...]
    pallas_call x0 -> x2, Pallas kernels: none -> 40.5 us  [the longest x1 23 us: columns(): pl.pallas_call(column_kernel, grid=(4,), out_shape=jax.ShapeDtypeStruct((...]
    ppermute x0 -> x8, starting transfers between devices: none -> 18.5 us  [the longest x7 18.5 us: on_device(): came = lax.ppermute(own[:, s * part:(s + 1) * part], 'prow', to)]
    unnamed x37 -> x7, local copies, waits for them, and re-layouts: 18.9 us -> 2.01 us
    ppermute x0 -> x8, waiting for transfers between devices: none -> 12.1 us  [the longest x7 12.1 us: on_device(): came = lax.ppermute(own[:, s * part:(s + 1) * part], 'prow', to)]
    all_gather x0 -> x1, blocking collectives: none -> 11.9 us  [on_device(): corner = lax.all_gather(piece[0], 'pcol')]
  transfers between devices with their start and end apart: 8 -> 10, of which waited for: 8 -> 5; matrix products, arithmetic and copies ran while one was open for 2% -> 4% of each run, Pallas kernels for 0% -> 0%
where the time goes in v1:
time: 266 us; the launch traced here: 263 us
  waiting for transfers between devices  159 us (60%)
  Pallas kernels  40.5 us (15%)
  starting transfers between devices  18.5 us (7%)
  local copies, waits for them, and re-layouts  17.7 us (7%)
  between operations  13.5 us (5%)
  blocking collectives  11.9 us (4%)
    all_gather x1, waiting for transfers between devices, on_device(): raw = lax.all_gather(jnp.concatenate([piece, corner], axis=0), 'prow')  120 us
    all_gather x1, waiting for transfers between devices, on_device(): row = lax.all_gather(own[0], 'pcol')[:4]  27 us
    pallas_call x1, Pallas kernels, columns(): pl.pallas_call(column_kernel, grid=(4,), out_shape=jax.ShapeDtypeStruct((...  23 us
    ppermute x7, starting transfers between devices, on_device(): came = lax.ppermute(own[:, s * part:(s + 1) * part], 'prow', to)  18.5 us
    pallas_call x1, Pallas kernels, factor(): pl.pallas_call(factor_kernel, out_shape=(jax.ShapeDtypeStruct((3, n, 3 *...  17.5 us
    ppermute x7, waiting for transfers between devices, on_device(): came = lax.ppermute(own[:, s * part:(s + 1) * part], 'prow', to)  12.1 us
    all_gather x1, blocking collectives, on_device(): corner = lax.all_gather(piece[0], 'pcol')  11.9 us
    broadcast_in_dim x1, local copies, waits for them, and re-layouts, on_device(): return jnp.transpose(out, (1, 0, 2))[None]  6.9 us
  transfers between devices with their start and end apart: 10, of which 5 were waited for; matrix products, arithmetic and copies ran while one was open for 4% of the time, Pallas kernels for 0%

profile of v1, /device:TPU:16, one launch (start us, length us, event | category | flops | bytes accessed | tf_op | source)
XLA Modules:
  0.0 263.1 jit_solution(12959933918310303079)
XLA Ops:
  6.5 0.0 all-gather.6.cloned.1.call-start
  6.5 2.0 copy.10
  8.5 0.0 copy-start
  8.5 0.1 fusion.6
  8.7 3.8 %collective-permute-start.6 = (bf16[4,64,512]{2,1,0:T(8,128)(2,1)S(1)}, bf16[4,64,512]{2,1,0:T(8,128)(2,1)S(1)}, u32[]{:S(2)}, u32[]{:S(2)}) collective-permute-start(bf16[4,64,512]{2,1,0:T(8,128)(2,1)S(1)} %get-tuple-element.9), channel_id=1, source_target_pairs={{0,32},{8,40},{16,48},{24,56},{1,33},{9,41},{17,49},{25,57},{2,34}... | collective-permute-start | bytes 786440 | tf_op jit(solution)/shard_map/ppermute | solution.py:130
  12.5 2.0 collective-permute-start.5
  14.6 2.7 %collective-permute-start.4 = (bf16[4,64,512]{2,1,0:T(8,128)(2,1)S(1)}, bf16[4,64,512]{2,1,0:T(8,128)(2,1)}, u32[]{:S(2)}, u32[]{:S(2)}) collective-permute-start(bf16[4,64,512]{2,1,0:T(8,128)(2,1)S(1)} %get-tuple-element.11), channel_id=1, source_target_pairs={{0,96},{8,104},{16,112},{24,120},{1,97},{9,105},{17,113},{25,121},... | collective-permute-start | bytes 786440 | tf_op jit(solution)/shard_map/ppermute | solution.py:130
  17.3 3.9 %collective-permute-start.3 = (bf16[4,64,512]{2,1,0:T(8,128)(2,1)S(1)}, bf16[4,64,512]{2,1,0:T(8,128)(2,1)}, u32[]{:S(2)}, u32[]{:S(2)}) collective-permute-start(bf16[4,64,512]{2,1,0:T(8,128)(2,1)S(1)} %get-tuple-element.12), channel_id=1, source_target_pairs={{0,128},{8,136},{16,144},{24,152},{1,129},{9,137},{17,145},{25,153... | collective-permute-start | bytes 786440 | tf_op jit(solution)/shard_map/ppermute | solution.py:130
  21.2 2.0 collective-permute-start.2
  23.2 0.0 collective-permute-done.6
  23.2 0.0 copy-start.1
  23.2 2.0 collective-permute-start.1
  25.2 0.0 collective-permute-done.5
  25.2 0.0 copy-start.2
  25.2 2.0 collective-permute-start
  27.2 0.0 copy-done.1
  27.2 0.0 copy-done.2
  27.2 3.2 %collective-permute-done.4 = bf16[4,64,512]{2,1,0:T(8,128)(2,1)} collective-permute-done((bf16[4,64,512]{2,1,0:T(8,128)(2,1)S(1)}, bf16[4,64,512]{2,1,0:T(8,128)(2,1)}, u32[]{:S(2)}, u32[]{:S(2)}) %collective-permute-start.4) | collective-permute-done | bytes 262176 | tf_op jit(solution)/shard_map/ppermute | solution.py:130
  30.5 4.5 %collective-permute-done.3 = bf16[4,64,512]{2,1,0:T(8,128)(2,1)} collective-permute-done((bf16[4,64,512]{2,1,0:T(8,128)(2,1)S(1)}, bf16[4,64,512]{2,1,0:T(8,128)(2,1)}, u32[]{:S(2)}, u32[]{:S(2)}) %collective-permute-start.3) | collective-permute-done | bytes 262176 | tf_op jit(solution)/shard_map/ppermute | solution.py:130
  34.9 0.0 collective-permute-done.2
  34.9 0.0 collective-permute-done.1
  34.9 4.4 %collective-permute-done = bf16[4,64,512]{2,1,0:T(8,128)(2,1)} collective-permute-done((bf16[4,64,512]{2,1,0:T(8,128)(2,1)S(1)}, bf16[4,64,512]{2,1,0:T(8,128)(2,1)}, u32[]{:S(2)}, u32[]{:S(2)}) %collective-permute-start) | collective-permute-done | bytes 262176 | tf_op jit(solution)/shard_map/ppermute | solution.py:130
  39.3 0.1 fusion.5
  39.4 11.9 %all_gather.12 = bf16[8,64,512]{2,1,0:T(8,128)(2,1)S(1)} all-gather(bf16[1,64,512]{2,1,0:T(8,128)(2,1)S(1)} %slice.64), channel_id=1, replica_groups=mesh['prow'=32,'pcol'=8] {'pcol'}, dimensions={0}, use_global_device_ids=true | all-gather | bytes 589824 | tf_op jit(solution)/shard_map/all_gather | solution.py:135
  51.4 0.8 pad_maximum_fusion
  52.1 0.0 all-gather.6.cloned.1.call-update
  52.2 0.0 all-gather.4.cloned.1.call-start
  52.2 0.0 copy-done
  52.2 0.8 slice.68
  53.1 0.0 all-gather.4.cloned.1.call-update
  53.1 120.2 %all-gather.6.cloned.1.call-done = bf16[192,64,512]{2,1,0:T(8,128)(2,1)} async-done(((bf16[6,64,512]{2,1,0:T(8,128)(2,1)}), bf16[192,64,512]{2,1,0:T(8,128)(2,1)}) %all-gather.6.cloned.1.call-update) | async-done | bytes 12582928 | tf_op jit(solution)/shard_map/all_gather | solution.py:138
  173.3 4.7 %slice.67 = bf16[32,2,64,512]{3,2,1,0:T(8,128)(2,1)} slice(bf16[32,6,64,512]{3,2,1,0:T(8,128)(2,1)} %bitcast.17), slice={[0:32], [4:6], [0:64], [0:512]} | slice | bytes 8388608 | tf_op jit(solution)/shard_map/slice | solution.py:139
  178.0 0.0 collective-permute-start.7
  178.0 0.7 pad_add_fusion.ids
  178.7 27.0 %all-gather.4.cloned.1.call-done = bf16[8,512,512]{2,1,0:T(8,128)(2,1)} async-done(((bf16[1,512,512]{2,1,0:T(8,128)(2,1)}), bf16[8,512,512]{2,1,0:T(8,128)(2,1)}) %all-gather.4.cloned.1.call-update) | async-done | bytes 4194320 | tf_op jit(solution)/shard_map/all_gather | solution.py:133
  205.7 3.1 %slice.69.row = bf16[4,512,512]{2,1,0:T(8,128)(2,1)} slice(bf16[8,512,512]{2,1,0:T(8,128)(2,1)} %all-gather.4.cloned.1.call-done), slice={[0:4], [0:512], [0:512]} | slice | bytes 4194304 | tf_op jit(solution)/shard_map/slice | solution.py:133
  208.8 0.0 collective-permute-done.7.other
  208.8 17.5 %shard_map.46 = (bf16[3,512,1536]{2,1,0:T(8,128)(2,1)}, bf16[512,2048]{1,0:T(8,128)(2,1)}) custom-call(s32[3]{0:T(128)} %pad_add_fusion.ids, s32[32,32]{1,0:T(8,128)} %shape.3, bf16[32,6,64,512]{3,2,1,0:T(8,128)(2,1)} %bitcast.18, bf16[32,2,64,512]{3,2,1,0:T(8,128)(2,1)} %collective-permute-done.7.other, bf16[4,512,512]{2,1,0:T(8,128)(2,1)} %slice.69.row, ...), custom_call_target="tpu_custom_call" | custom-call | flops 8053063680 | bytes 18874368 | tf_op jit(solution)/shard_map/pallas_call | solution.py:79
  226.4 23.0 %shard_map.47 = f32[4,512,512]{2,1,0:T(8,128)} custom-call(s32[3]{0:T(128)} %pad_add_fusion.ids, s32[32,32]{1,0:T(8,128)} %shape.3, bf16[32,6,64,512]{3,2,1,0:T(8,128)(2,1)} %bitcast.19, bf16[4,512,512]{2,1,0:T(8,128)(2,1)} %bitcast.15, bf16[3,512,1536]{2,1,0:T(8,128)(2,1)} %get-tuple-element.7.low, bf16[512,2048]{1,0:T(8,128)(2,1)} %get-tuple-element.8.left, ...), custom_call_target="tpu_custom_call" | custom-call | flops 15032385536 | bytes 25165824 | tf_op jit(solution)/shard_map/pallas_call | solution.py:97
  249.4 6.9 %copy.8 = f32[1,512,4,512]{3,2,1,0:T(4,128)} copy(f32[1,512,4,512]{3,1,2,0:T(8,128)} %bitcast.16) | data formatting | bytes 8388608 | tf_op jit(solution)/shard_map/broadcast_in_dim | solution.py:143
  (2 shorter events, 0.0 us)
Async XLA Ops:
  6.5 166.8 %all-gather.6.cloned.1.call-start = ((), (), s32[]{:S(2)}) async-start(), calls=%async_computation.1 | async-start | bytes 12976128 | tf_op jit(solution)/shard_map/all_gather | solution.py:138
  8.5 43.7 %copy-start = (bf16[1,512,4,512]{3,1,2,0:T(8,128)(2,1)}, bf16[1,512,4,512]{3,1,2,0:T(8,128)(2,1)S(1)}, u32[]{:S(2)}) copy-start(bf16[1,512,4,512]{3,1,2,0:T(8,128)(2,1)S(1)} %copy.10) | copy-start | bytes 6291460
  8.7 14.5 %collective-permute-start.6 = (bf16[4,64,512]{2,1,0:T(8,128)(2,1)S(1)}, bf16[4,64,512]{2,1,0:T(8,128)(2,1)S(1)}, u32[]{:S(2)}, u32[]{:S(2)}) collective-permute-start(bf16[4,64,512]{2,1,0:T(8,128)(2,1)S(1)} %get-tuple-element.9), channel_id=1, source_target_pairs={{0,32},{8,40},{16,48},{24,56},{1,33},{9,41},{17,49},{25,57},{2,34}... | collective-permute-start | bytes 786440 | tf_op jit(solution)/shard_map/ppermute | solution.py:130
  12.5 12.7 %collective-permute-start.5 = (bf16[4,64,512]{2,1,0:T(8,128)(2,1)S(1)}, bf16[4,64,512]{2,1,0:T(8,128)(2,1)S(1)}, u32[]{:S(2)}, u32[]{:S(2)}) collective-permute-start(bf16[4,64,512]{2,1,0:T(8,128)(2,1)S(1)} %get-tuple-element.10), channel_id=1, source_target_pairs={{0,64},{8,72},{16,80},{24,88},{1,65},{9,73},{17,81},{25,89},{2,66}... | collective-permute-start | bytes 786440 | tf_op jit(solution)/shard_map/ppermute | solution.py:130
  14.6 15.9 %collective-permute-start.4 = (bf16[4,64,512]{2,1,0:T(8,128)(2,1)S(1)}, bf16[4,64,512]{2,1,0:T(8,128)(2,1)}, u32[]{:S(2)}, u32[]{:S(2)}) collective-permute-start(bf16[4,64,512]{2,1,0:T(8,128)(2,1)S(1)} %get-tuple-element.11), channel_id=1, source_target_pairs={{0,96},{8,104},{16,112},{24,120},{1,97},{9,105},{17,113},{25,121},... | collective-permute-start | bytes 786440 | tf_op jit(solution)/shard_map/ppermute | solution.py:130
  17.3 17.6 %collective-permute-start.3 = (bf16[4,64,512]{2,1,0:T(8,128)(2,1)S(1)}, bf16[4,64,512]{2,1,0:T(8,128)(2,1)}, u32[]{:S(2)}, u32[]{:S(2)}) collective-permute-start(bf16[4,64,512]{2,1,0:T(8,128)(2,1)S(1)} %get-tuple-element.12), channel_id=1, source_target_pairs={{0,128},{8,136},{16,144},{24,152},{1,129},{9,137},{17,145},{25,153... | collective-permute-start | bytes 786440 | tf_op jit(solution)/shard_map/ppermute | solution.py:130
  21.2 13.7 %collective-permute-start.2 = (bf16[4,64,512]{2,1,0:T(8,128)(2,1)S(1)}, bf16[4,64,512]{2,1,0:T(8,128)(2,1)}, u32[]{:S(2)}, u32[]{:S(2)}) collective-permute-start(bf16[4,64,512]{2,1,0:T(8,128)(2,1)S(1)} %get-tuple-element.13), channel_id=1, source_target_pairs={{0,160},{8,168},{16,176},{24,184},{1,161},{9,169},{17,177},{25,185... | collective-permute-start | bytes 786440 | tf_op jit(solution)/shard_map/ppermute | solution.py:130
  23.2 4.0 %copy-start.1 = (bf16[4,64,512]{2,1,0:T(8,128)(2,1)}, bf16[4,64,512]{2,1,0:T(8,128)(2,1)S(1)}, u32[]{:S(2)}) copy-start(bf16[4,64,512]{2,1,0:T(8,128)(2,1)S(1)} %collective-permute-done.6) | copy-start | bytes 786436
  23.2 11.7 %collective-permute-start.1 = (bf16[4,64,512]{2,1,0:T(8,128)(2,1)S(1)}, bf16[4,64,512]{2,1,0:T(8,128)(2,1)}, u32[]{:S(2)}, u32[]{:S(2)}) collective-permute-start(bf16[4,64,512]{2,1,0:T(8,128)(2,1)S(1)} %get-tuple-element.14), channel_id=1, source_target_pairs={{0,192},{8,200},{16,208},{24,216},{1,193},{9,201},{17,209},{25,217... | collective-permute-start | bytes 786440 | tf_op jit(solution)/shard_map/ppermute | solution.py:130
  25.2 2.0 copy-start.2
  25.2 14.1 %collective-permute-start = (bf16[4,64,512]{2,1,0:T(8,128)(2,1)S(1)}, bf16[4,64,512]{2,1,0:T(8,128)(2,1)}, u32[]{:S(2)}, u32[]{:S(2)}) collective-permute-start(bf16[4,64,512]{2,1,0:T(8,128)(2,1)S(1)} %get-tuple-element.15), channel_id=1, source_target_pairs={{0,224},{8,232},{16,240},{24,248},{1,225},{9,233},{17,241},{25,249... | collective-permute-start | bytes 786440 | tf_op jit(solution)/shard_map/ppermute | solution.py:130
  52.2 153.5 %all-gather.4.cloned.1.call-start = ((), (), s32[]{:S(2)}) async-start(), calls=%async_computation | async-start | bytes 4718592 | tf_op jit(solution)/shard_map/all_gather | solution.py:133
  178.0 30.8 %collective-permute-start.7 = (bf16[32,2,64,512]{3,2,1,0:T(8,128)(2,1)}, bf16[32,2,64,512]{3,2,1,0:T(8,128)(2,1)}, u32[]{:S(2)}, u32[]{:S(2)}) collective-permute-start(bf16[32,2,64,512]{3,2,1,0:T(8,128)(2,1)} %slice.67), channel_id=1, source_target_pairs={{0,1},{1,0},{2,3},{3,2},{4,5},{5,4},{6,7},{7,6},{8,9},{9,8},{10,11... | collective-permute-start | bytes 12582920 | tf_op jit(solution)/shard_map/ppermute | solution.py:139
Sparse Core Ops, SparseCore 0:
  52.3 121.0 all-gather.5
  175.2 30.4 all-gather.3

commit v2 on v1

v2 whole, which is shorter than its diff:
```python
import functools

import jax
import jax.numpy as jnp
from jax import lax
from jax.experimental import pallas as pl
from jax.experimental.pallas import tpu as pltpu
from jax.sharding import PartitionSpec as P

STEPS = 4
HALF = jnp.bfloat16
FULL = jnp.float32
VMEM_LIMIT = 56 * 1024 * 1024


def mm(a, b):
    return jnp.dot(a, b, preferred_element_type=FULL)


def shift(block, way):
    move = 1 if way[-1] == "+" else -1
    if way[0] == "z":
        return lax.ppermute(block, "prow", [(i, (i + 4 * move) % 32) for i in range(32)])
    if way[0] == "x":
        return lax.ppermute(block, "prow", [(i, i // 4 * 4 + (i + move) % 4) for i in range(32)])
    if way[0] == "y":
        return lax.ppermute(block, "pcol", [(i, (i + 2 * move) % 8) for i in range(8)])
    return lax.ppermute(block, "pcol", [(i, i ^ 1) for i in range(8)])


def around_four(block, axis):
    half = block.shape[0] // 2
    above = shift(block, axis + "-")
    below = shift(block, axis + "+")
    far = [shift(below[:half], axis + "+"), shift(above[half:], axis + "-")]
    return [block, above, jnp.concatenate(far, axis=0), below]


def around_eight(block):
    half = block.shape[1] // 2
    up, down = [block], [block]
    for _ in range(3):
        up.append(shift(up[-1], "z+"))
        down.append(shift(down[-1], "z-"))
    far = [shift(up[3][:, :half], "z+"), shift(down[3][:, half:], "z-")]
    return up + [jnp.concatenate(far, axis=1)] + down[:0:-1]


def kernel(ids, shape, mine, other, row_mine, row_other, v, w, raw, own, out, low, left, up, upper):
    n = v.shape[1]
    p, q = ids[0], ids[1]
    z, x, y, core = p // 4, lax.rem(p, 4), q // 2, lax.rem(q, 2)
    c = pl.program_id(0)
    j = c * 8 + q

    def cut(k):
        return slice(k * n, (k + 1) * n)

    def raw_corner(k, m):
        dx, dy, gap = lax.rem(k - x + 4, 4), lax.rem(m - y + 4, 4), lax.rem(m - x + 4, 4)
        at = jnp.where(dx < gap, dx, jnp.maximum(dx - 1, 0))
        parts = []
        for i in range(8):
            away = lax.rem(z - i + 8, 8)
            here, there = mine[dy, away, at], other[dy, away, at]
            parts += [jnp.where(core == 0, here, there), jnp.where(core == 0, there, here)]
        return jnp.concatenate(parts, axis=0)

    def raw_row(k):
        dy = lax.rem(k // 2 - y + 4, 4)
        return jnp.where(core == k % 2, row_mine[dy], row_other[dy])

    @pl.when(c == 0)
    def _():
        for k in range(3):
            for i in range(k + 1, 4):
                block = raw_corner(i, k)
                if k:
                    block = (block.astype(FULL) - mm(low[i - 1, :, 0 : k * n], up[0 : k * n, cut(k)])).astype(HALF)
                low[i - 1, :, cut(k)] = (mm(block, v[k]) * shape[i, k].astype(FULL)).astype(HALF)
            for i in range(k + 1, 4):
                block = raw_corner(k, i)
                if k:
                    block = (block.astype(FULL) - mm(low[k - 1, :, 0 : k * n], up[0 : k * n, cut(i)])).astype(HALF)
                up[cut(k), cut(i)] = (mm(w[k], block) * shape[k, i].astype(FULL)).astype(HALF)
        for k in range(4):
            block = raw_row(k)
            if k:
                block = (block.astype(FULL) - mm(left[:, 0 : k * n], up[0 : k * n, cut(k)])).astype(HALF)
            scale = jnp.where(p > k, shape[p, k], 0).astype(FULL)
            left[:, cut(k)] = (mm(block, v[k]) * scale).astype(HALF)

    for k in range(4):
        block = jnp.concatenate([raw[i * 4 + k, 0] for i in range(8)], axis=0)
        if k:
            block = (block.astype(FULL) - mm(low[k - 1, :, 0 : k * n], upper[0 : k * n, :])).astype(HALF)
        scale = jnp.where(j > k, shape[k, j], 0).astype(FULL)
        upper[cut(k), :] = (mm(w[k], block) * scale).astype(HALF)
    keep = shape[p, j].astype(FULL)
    out[0] = own[0].astype(FULL) - keep * mm(left[...], upper[...])

    @pl.when(jnp.logical_and(p < STEPS, j > p))
    def _():
        out[0] = upper[pl.ds(pl.multiple_of(jnp.minimum(p, 3) * n, n), n), :].astype(FULL)

    @pl.when(jnp.logical_and(j < STEPS, p > j))
    def _():
        out[0] = left[:, pl.ds(pl.multiple_of(jnp.minimum(j, 3) * n, n), n)].astype(FULL)


def factor_and_update(ids, shape, corner, row, v, w, raw, own):
    n = w.shape[1]
    smem = pl.BlockSpec(memory_space=pltpu.SMEM)
    whole = lambda a: pl.BlockSpec(a.shape, lambda c: (0,) * a.ndim, pipeline_mode=pl.Buffered(1))
    return pl.pallas_call(
        kernel,
        grid=(4,),
        out_shape=jax.ShapeDtypeStruct((4, n, n), FULL),
        in_specs=[smem, smem]
        + [whole(a) for a in (*corner, *row, v, w)]
        + [
            pl.BlockSpec((32, 1, n // 8, n), lambda c: (0, c, 0, 0)),
            pl.BlockSpec((1, n, n), lambda c: (c, 0, 0)),
        ],
        out_specs=pl.BlockSpec((1, n, n), lambda c: (c, 0, 0)),
        scratch_shapes=[
            pltpu.VMEM((3, n, 3 * n), HALF),
            pltpu.VMEM((n, 4 * n), HALF),
            pltpu.VMEM((3 * n, 4 * n), HALF),
            pltpu.VMEM((4 * n, n), HALF),
        ],
        compiler_params=pltpu.CompilerParams(vmem_limit_bytes=VMEM_LIMIT),
        cost_estimate=pl.CostEstimate(flops=172 * n**3, bytes_accessed=30 * 2**20, transcendentals=0),
    )(ids, shape, *corner, *row, v, w, raw, own)


def on_device(matrix, upper_inverse, lower_inverse, structure):
    p = lax.axis_index("prow")
    q = lax.axis_index("pcol")
    z, core = p // 4, lax.rem(q, 2)
    n = matrix.shape[1]
    part = n // 8
    own = jnp.transpose(matrix[0], (1, 0, 2))
    ids = jnp.stack([p, q]).astype(jnp.int32)

    piece = own[:, :part]
    came = {}
    for s in (1, 4, 5, 3, 6, 2, 7):
        to = [(i, i + 4 * s) for i in range(4)]
        came[s] = lax.ppermute(own[:, s * part : (s + 1) * part], "prow", to)
    row, came[1] = lax.optimization_barrier((own[0], came[1]))
    above, below = shift(row, "y-"), shift(row, "y+")
    for s in came:
        piece = jnp.where(z == s, came[s], piece)

    raw = lax.all_gather(piece, "prow")

    seed, above, below = lax.optimization_barrier((piece[0], above, below))
    first = lax.ppermute(seed[: part // 2], "pcol", [(i, 2 * i) for i in range(4)])
    second = lax.ppermute(seed[part // 2 :], "pcol", [(i, 2 * i + 1) for i in range(4)])
    corner = jnp.where(core == 0, first, second)
    corner = [corner, shift(corner, "x-"), shift(shift(corner, "x-"), "x-"), shift(corner, "x+")]
    gap = lax.rem(q // 2 - p % 4 + 4, 4)
    corner = jnp.stack([jnp.where(i < gap, corner[i], corner[i + 1]) for i in range(3)])
    far = [shift(below[: n // 2], "y+"), shift(above[n // 2 :], "y-")]
    row = jnp.stack([row, above, jnp.concatenate(far, axis=0), below])
    corner = jnp.stack(around_eight(corner))
    corner, row = lax.optimization_barrier((corner, row))
    row = [row, shift(row, "c")]
    corner = jnp.stack(around_four(corner, "y"))
    corner = [corner, shift(corner, "c")]

    out = factor_and_update(ids, structure, corner, row, upper_inverse, lower_inverse, raw, own)
    return jnp.transpose(out, (1, 0, 2))[None]


def solution(mesh):
    return jax.shard_map(
        on_device,
        mesh=mesh,
        in_specs=(P(None, "prow", None, "pcol"), P(), P(), P()),
        out_specs=P(None, "prow", None, "pcol"),
        check_vma=False,
    )
```

time: 266 us -> 186 us (0.70)
  waiting for transfers between devices: 159 us -> 68.8 us
  starting transfers between devices: 18.5 us -> 54.2 us
  blocking collectives: 11.9 us -> 0 us
  Pallas kernels: 40.5 us -> 33.2 us
  local copies, waits for them, and re-layouts: 17.7 us -> 12.4 us
    all_gather x2 -> x1, waiting for transfers between devices: 147 us -> 2.25 us  [on_device(): raw = lax.all_gather(piece, 'prow')]
    ppermute x8 -> x30, waiting for transfers between devices: 12.1 us -> 66.6 us  [the longest x8 33.9 us: shift(): lax.ppermute(block, 'pcol', [(i, (i + 2 * move) % 8) for i in range(8)])]
    ppermute x8 -> x30, starting transfers between devices: 18.5 us -> 54.2 us  [the longest x7 19.7 us: on_device(): came[s] = lax.ppermute(own[:, s * part:(s + 1) * part], 'prow', to)]
    all_gather x1 -> x0, blocking collectives: 11.9 us -> none  [on_device(): corner = lax.all_gather(piece[0], 'pcol')]
    slice x5 -> x8, local copies, waits for them, and re-layouts: 8.81 us -> 1.18 us  [the longest x1 1.07 us: on_device(): came[s] = lax.ppermute(own[:, s * part:(s + 1) * part], 'prow', to)]
    pallas_call x2 -> x1, Pallas kernels: 40.5 us -> 33.2 us  [factor_and_update(): pl.pallas_call(kernel, grid=(4,), out_shape=jax.ShapeDtypeStruct((4, n, n...]
  transfers between devices with their start and end apart: 10 -> 31, of which waited for: 5 -> 18; matrix products, arithmetic and copies ran while one was open for 4% -> 2% of each run, Pallas kernels for 0% -> 0%
where the time goes in v2:
time: 186 us; the launch traced here: 185 us
  waiting for transfers between devices  68.8 us (37%)
  starting transfers between devices  54.2 us (29%)
  Pallas kernels  33.2 us (18%)
  between operations  13.7 us (7%)
  local copies, waits for them, and re-layouts  12.4 us (7%)
  other arithmetic  2.68 us (1%)
    ppermute x8, waiting for transfers between devices, shift(): lax.ppermute(block, 'pcol', [(i, (i + 2 * move) % 8) for i in range(8)])  33.9 us
    pallas_call x1, Pallas kernels, factor_and_update(): pl.pallas_call(kernel, grid=(4,), out_shape=jax.ShapeDtypeStruct((4, n, n...  33.2 us
    ppermute x7, starting transfers between devices, on_device(): came[s] = lax.ppermute(own[:, s * part:(s + 1) * part], 'prow', to)  19.7 us
    ppermute x8, starting transfers between devices, shift(): lax.ppermute(block, 'prow', [(i, (i + 4 * move) % 32) for i in range(32)])  14.9 us
    ppermute x8, waiting for transfers between devices, shift(): lax.ppermute(block, 'prow', [(i, (i + 4 * move) % 32) for i in range(32)])  11.5 us
    ppermute x8, starting transfers between devices, shift(): lax.ppermute(block, 'pcol', [(i, (i + 2 * move) % 8) for i in range(8)])  10.7 us
    ppermute x7, waiting for transfers between devices, on_device(): came[s] = lax.ppermute(own[:, s * part:(s + 1) * part], 'prow', to)  8.27 us
    broadcast_in_dim x1, local copies, waits for them, and re-layouts, on_device(): return jnp.transpose(out, (1, 0, 2))[None]  6.9 us
  transfers between devices with their start and end apart: 31, of which 18 were waited for; matrix products, arithmetic and copies ran while one was open for 2% of the time, Pallas kernels for 0%

profile of v2, /device:TPU:16, one launch (start us, length us, event | category | flops | bytes accessed | tf_op | source)
XLA Modules:
  0.0 185.0 jit_solution(10085145282468818499)
XLA Ops:
  6.5 2.0 %copy.10 = bf16[1,512,4,512]{3,1,2,0:T(8,128)(2,1)S(1)} copy(bf16[1,512,4,512]{3,2,1,0:T(4,128)(2,1)} %param.4) | data formatting | bytes 4194304 | tf_op args[0]
  8.5 1.1 fusion.7
  9.6 3.8 %collective-permute-start.6 = (bf16[4,64,512]{2,1,0:T(8,128)(2,1)S(1)}, bf16[4,64,512]{2,1,0:T(8,128)(2,1)S(1)}, u32[]{:S(2)}, u32[]{:S(2)}) collective-permute-start(bf16[4,64,512]{2,1,0:T(8,128)(2,1)S(1)} %get-tuple-element.19), channel_id=1, source_target_pairs={{0,32},{8,40},{16,48},{24,56},{1,33},{9,41},{17,49},{25,57},{2,34}... | collective-permute-start | bytes 786440 | tf_op jit(solution)/shard_map/ppermute | solution.py:150
  13.5 5.9 %collective-permute-start.5 = (bf16[4,64,512]{2,1,0:T(8,128)(2,1)S(1)}, bf16[4,64,512]{2,1,0:T(8,128)(2,1)S(1)}, u32[]{:S(2)}, u32[]{:S(2)}) collective-permute-start(bf16[4,64,512]{2,1,0:T(8,128)(2,1)S(1)} %get-tuple-element.20), channel_id=1, source_target_pairs={{0,128},{8,136},{16,144},{24,152},{1,129},{9,137},{17,145},{25,153... | collective-permute-start | bytes 786440 | tf_op jit(solution)/shard_map/ppermute | solution.py:150
  19.4 2.0 %collective-permute-start.4 = (bf16[4,64,512]{2,1,0:T(8,128)(2,1)}, bf16[4,64,512]{2,1,0:T(8,128)(2,1)}, u32[]{:S(2)}, u32[]{:S(2)}) collective-permute-start(bf16[4,64,512]{2,1,0:T(8,128)(2,1)} %get-tuple-element.21), channel_id=1, source_target_pairs={{0,160},{8,168},{16,176},{24,184},{1,161},{9,169},{17,177},{25,185... | collective-permute-start | bytes 786440 | tf_op jit(solution)/shard_map/ppermute | solution.py:150
  21.4 2.0 %collective-permute-start.3 = (bf16[4,64,512]{2,1,0:T(8,128)(2,1)}, bf16[4,64,512]{2,1,0:T(8,128)(2,1)}, u32[]{:S(2)}, u32[]{:S(2)}) collective-permute-start(bf16[4,64,512]{2,1,0:T(8,128)(2,1)} %get-tuple-element.22), channel_id=1, source_target_pairs={{0,96},{8,104},{16,112},{24,120},{1,97},{9,105},{17,113},{25,121},... | collective-permute-start | bytes 786440 | tf_op jit(solution)/shard_map/ppermute | solution.py:150
  23.4 2.0 %collective-permute-start.2 = (bf16[4,64,512]{2,1,0:T(8,128)(2,1)S(1)}, bf16[4,64,512]{2,1,0:T(8,128)(2,1)}, u32[]{:S(2)}, u32[]{:S(2)}) collective-permute-start(bf16[4,64,512]{2,1,0:T(8,128)(2,1)S(1)} %get-tuple-element.23), channel_id=1, source_target_pairs={{0,192},{8,200},{16,208},{24,216},{1,193},{9,201},{17,209},{25,217... | collective-permute-start | bytes 786440 | tf_op jit(solution)/shard_map/ppermute | solution.py:150
  25.4 2.0 %collective-permute-start.1 = (bf16[4,64,512]{2,1,0:T(8,128)(2,1)S(1)}, bf16[4,64,512]{2,1,0:T(8,128)(2,1)}, u32[]{:S(2)}, u32[]{:S(2)}) collective-permute-start(bf16[4,64,512]{2,1,0:T(8,128)(2,1)S(1)} %get-tuple-element.24), channel_id=1, source_target_pairs={{0,64},{8,72},{16,80},{24,88},{1,65},{9,73},{17,81},{25,89},{2,66}... | collective-permute-start | bytes 786440 | tf_op jit(solution)/shard_map/ppermute | solution.py:150
  27.4 0.0 collective-permute-done.5
  27.4 2.0 %collective-permute-start = (bf16[4,64,512]{2,1,0:T(8,128)(2,1)S(1)}, bf16[4,64,512]{2,1,0:T(8,128)(2,1)}, u32[]{:S(2)}, u32[]{:S(2)}) collective-permute-start(bf16[4,64,512]{2,1,0:T(8,128)(2,1)S(1)} %get-tuple-element.25), channel_id=1, source_target_pairs={{0,224},{8,232},{16,240},{24,248},{1,225},{9,233},{17,241},{25,249... | collective-permute-start | bytes 786440 | tf_op jit(solution)/shard_map/ppermute | solution.py:150
  29.4 0.0 collective-permute-done.4
  29.4 2.4 %collective-permute-done.3 = bf16[4,64,512]{2,1,0:T(8,128)(2,1)} collective-permute-done((bf16[4,64,512]{2,1,0:T(8,128)(2,1)}, bf16[4,64,512]{2,1,0:T(8,128)(2,1)}, u32[]{:S(2)}, u32[]{:S(2)}) %collective-permute-start.3) | collective-permute-done | bytes 262176 | tf_op jit(solution)/shard_map/ppermute | solution.py:150
  31.8 1.4 collective-permute-done.2
  33.2 2.9 %collective-permute-done.1 = bf16[4,64,512]{2,1,0:T(8,128)(2,1)} collective-permute-done((bf16[4,64,512]{2,1,0:T(8,128)(2,1)S(1)}, bf16[4,64,512]{2,1,0:T(8,128)(2,1)}, u32[]{:S(2)}, u32[]{:S(2)}) %collective-permute-start.1) | collective-permute-done | bytes 262176 | tf_op jit(solution)/shard_map/ppermute | solution.py:150
  36.2 1.5 collective-permute-done
  37.7 0.9 fusion.5
  38.6 0.0 all-gather.3.cloned.1.call-update
  38.6 1.4 collective-permute-start.8
  39.9 0.7 collective-permute-start.7
  40.7 0.8 slice_bitcast_fusion.1
  41.5 9.9 %collective-permute-done.8 = bf16[512,512]{1,0:T(8,128)(2,1)S(1)} collective-permute-done((bf16[512,512]{1,0:T(8,128)(2,1)S(1)}, bf16[512,512]{1,0:T(8,128)(2,1)S(1)}, u32[]{:S(2)}, u32[]{:S(2)}) %collective-permute-start.8) | collective-permute-done | bytes 524320 | tf_op jit(solution)/shard_map/ppermute | solution.py:27
  51.5 1.0 collective-permute-done.7
  52.5 0.7 collective-permute-start.10
  53.1 1.3 collective-permute-start.9
  54.4 4.5 %collective-permute-done.9 = bf16[32,512]{1,0:T(8,128)(2,1)S(1)} collective-permute-done((bf16[32,512]{1,0:T(8,128)(2,1)S(1)}, bf16[32,512]{1,0:T(8,128)(2,1)S(1)}, u32[]{:S(2)}, u32[]{:S(2)}) %collective-permute-start.9) | collective-permute-done | bytes 32800 | tf_op jit(solution)/shard_map/ppermute | solution.py:159
  58.9 2.8 %collective-permute-start.11 = (bf16[32,512]{1,0:T(8,128)(2,1)S(1)}, bf16[32,512]{1,0:T(8,128)(2,1)S(1)}, u32[]{:S(2)}, u32[]{:S(2)}) collective-permute-start(bf16[32,512]{1,0:T(8,128)(2,1)S(1)} %broadcast_select_fusion), channel_id=1, source_target_pairs={{0,24},{8,0},{16,8},{24,16},{32,56},{40,32},{48,40},{56,48},{64,88... | collective-permute-start | bytes 98312 | tf_op jit(solution)/shard_map/ppermute | solution.py:25
  61.8 0.0 collective-permute-start.13
  61.8 1.6 collective-permute-done.11
  63.4 3.5 %collective-permute-start.12 = (bf16[32,512]{1,0:T(8,128)(2,1)S(1)}, bf16[32,512]{1,0:T(8,128)(2,1)S(1)}, u32[]{:S(2)}, u32[]{:S(2)}) collective-permute-start(bf16[32,512]{1,0:T(8,128)(2,1)S(1)} %collective-permute-done.11), channel_id=1, source_target_pairs={{0,24},{8,0},{16,8},{24,16},{32,56},{40,32},{48,40},{56,48},{64,88... | collective-permute-start | bytes 98312 | tf_op jit(solution)/shard_map/ppermute | solution.py:25
  66.9 3.0 %collective-permute-start.22 = (bf16[256,512]{1,0:T(8,128)(2,1)S(1)}, bf16[256,512]{1,0:T(8,128)(2,1)S(1)}, u32[]{:S(2)}, u32[]{:S(2)}) collective-permute-start(bf16[256,512]{1,0:T(8,128)(2,1)S(1)} %slice.68), channel_id=1, source_target_pairs={{0,2},{1,3},{2,4},{3,5},{4,6},{5,7},{6,0},{7,1},{8,10},{9,11},{10,... | collective-permute-start | bytes 786440 | tf_op jit(solution)/shard_map/ppermute | solution.py:27
  70.0 0.1 collective-permute-start.14
  70.1 4.9 %collective-permute-start.18 = (bf16[3,32,512]{2,1,0:T(8,128)(2,1)S(1)}, bf16[3,32,512]{2,1,0:T(8,128)(2,1)S(1)}, u32[]{:S(2)}, u32[]{:S(2)}) collective-permute-start(bf16[3,32,512]{2,1,0:T(8,128)(2,1)S(1)} %pad_maximum_fusion.2), channel_id=1, source_target_pairs={{0,224},{8,232},{16,240},{24,248},{32,0},{40,8},{48,16},{56,24},{6... | collective-permute-start | bytes 294920 | tf_op jit(solution)/shard_map/ppermute | solution.py:23
  75.1 3.2 %collective-permute-done.14 = bf16[3,32,512]{2,1,0:T(8,128)(2,1)S(1)} collective-permute-done((bf16[3,32,512]{2,1,0:T(8,128)(2,1)S(1)}, bf16[3,32,512]{2,1,0:T(8,128)(2,1)S(1)}, u32[]{:S(2)}, u32[]{:S(2)}) %collective-permute-start.14) | collective-permute-done | bytes 98336 | tf_op jit(solution)/shard_map/ppermute | solution.py:23
  78.3 3.2 %collective-permute-start.19 = (bf16[3,32,512]{2,1,0:T(8,128)(2,1)S(1)}, bf16[3,32,512]{2,1,0:T(8,128)(2,1)S(1)}, u32[]{:S(2)}, u32[]{:S(2)}) collective-permute-start(bf16[3,32,512]{2,1,0:T(8,128)(2,1)S(1)} %collective-permute-done.18), channel_id=1, source_target_pairs={{0,224},{8,232},{16,240},{24,248},{32,0},{40,8},{48,16},{56,24},{6... | collective-permute-start | bytes 294920 | tf_op jit(solution)/shard_map/ppermute | solution.py:23
  81.5 0.0 collective-permute-done.22
  81.5 0.0 collective-permute-done.23
  81.6 0.3 pad_maximum_fusion.1.row_mine
  81.9 3.0 %collective-permute-done.15 = bf16[3,32,512]{2,1,0:T(8,128)(2,1)S(1)} collective-permute-done((bf16[3,32,512]{2,1,0:T(8,128)(2,1)S(1)}, bf16[3,32,512]{2,1,0:T(8,128)(2,1)S(1)}, u32[]{:S(2)}, u32[]{:S(2)}) %collective-permute-start.15) | collective-permute-done | bytes 98336 | tf_op jit(solution)/shard_map/ppermute | solution.py:23
  84.9 0.0 collective-permute-start.16
  84.9 0.0 collective-permute-done.19
  84.9 3.3 %collective-permute-start.20 = (bf16[3,32,512]{2,1,0:T(8,128)(2,1)S(1)}, bf16[3,32,512]{2,1,0:T(8,128)(2,1)S(1)}, u32[]{:S(2)}, u32[]{:S(2)}) collective-permute-start(bf16[3,32,512]{2,1,0:T(8,128)(2,1)S(1)} %collective-permute-done.19), channel_id=1, source_target_pairs={{0,224},{8,232},{16,240},{24,248},{32,0},{40,8},{48,16},{56,24},{6... | collective-permute-start | bytes 294920 | tf_op jit(solution)/shard_map/ppermute | solution.py:23
  88.2 2.5 %collective-permute-done.16 = bf16[3,32,512]{2,1,0:T(8,128)(2,1)S(1)} collective-permute-done((bf16[3,32,512]{2,1,0:T(8,128)(2,1)S(1)}, bf16[3,32,512]{2,1,0:T(8,128)(2,1)S(1)}, u32[]{:S(2)}, u32[]{:S(2)}) %collective-permute-start.16) | collective-permute-done | bytes 98336 | tf_op jit(solution)/shard_map/ppermute | solution.py:23
  90.7 0.0 collective-permute-done.20
  90.7 3.4 %collective-permute-start.21 = (bf16[3,16,512]{2,1,0:T(8,128)(2,1)S(1)}, bf16[3,16,512]{2,1,0:T(8,128)(2,1)S(1)}, u32[]{:S(2)}, u32[]{:S(2)}) collective-permute-start(bf16[3,16,512]{2,1,0:T(8,128)(2,1)S(1)} %slice.83), channel_id=1, source_target_pairs={{0,224},{8,232},{16,240},{24,248},{32,0},{40,8},{48,16},{56,24},{6... | collective-permute-start | bytes 147464 | tf_op jit(solution)/shard_map/ppermute | solution.py:23
  94.1 2.8 %collective-permute-done.17 = bf16[3,16,512]{2,1,0:T(8,128)(2,1)S(1)} collective-permute-done((bf16[3,16,512]{2,1,0:T(8,128)(2,1)S(1)}, bf16[3,16,512]{2,1,0:T(8,128)(2,1)S(1)}, u32[]{:S(2)}, u32[]{:S(2)}) %collective-permute-start.17) | collective-permute-done | bytes 49184 | tf_op jit(solution)/shard_map/ppermute | solution.py:23
  97.0 2.9 %collective-permute-start.25 = (bf16[8,3,32,512]{3,2,1,0:T(8,128)(2,1)S(1)}, bf16[8,3,32,512]{3,2,1,0:T(8,128)(2,1)S(1)}, u32[]{:S(2)}, u32[]{:S(2)}) collective-permute-start(bf16[8,3,32,512]{3,2,1,0:T(8,128)(2,1)S(1)} %bitcast_dynamic-update-slice_fusion), channel_id=1, source_target_pairs={{0,2},{1,3},{2,4},{3,5},{4,6},{5,7},{6,0},{7,1},{8,10},{9,11},{10,... | collective-permute-start | bytes 2359304 | tf_op jit(solution)/shard_map/ppermute | solution.py:27
  99.9 0.0 collective-permute-start.24
  99.9 13.7 %collective-permute-done.25 = bf16[8,3,32,512]{3,2,1,0:T(8,128)(2,1)S(1)} collective-permute-done((bf16[8,3,32,512]{3,2,1,0:T(8,128)(2,1)S(1)}, bf16[8,3,32,512]{3,2,1,0:T(8,128)(2,1)S(1)}, u32[]{:S(2)}, u32[]{:S(2)}) %collective-permute-start.25) | collective-permute-done | bytes 786464 | tf_op jit(solution)/shard_map/ppermute | solution.py:27
  113.6 2.6 %collective-permute-start.26 = (bf16[4,3,32,512]{3,2,1,0:T(8,128)(2,1)S(1)}, bf16[4,3,32,512]{3,2,1,0:T(8,128)(2,1)S(1)}, u32[]{:S(2)}, u32[]{:S(2)}) collective-permute-start(bf16[4,3,32,512]{3,2,1,0:T(8,128)(2,1)S(1)} %slice.84), channel_id=1, source_target_pairs={{0,2},{1,3},{2,4},{3,5},{4,6},{5,7},{6,0},{7,1},{8,10},{9,11},{10,... | collective-permute-start | bytes 1179656 | tf_op jit(solution)/shard_map/ppermute | solution.py:27
  116.2 0.1 collective-permute-done.24
  116.3 0.1 collective-permute-start.27
  116.4 5.1 %collective-permute-done.26 = bf16[4,3,32,512]{3,2,1,0:T(8,128)(2,1)S(1)} collective-permute-done((bf16[4,3,32,512]{3,2,1,0:T(8,128)(2,1)S(1)}, bf16[4,3,32,512]{3,2,1,0:T(8,128)(2,1)S(1)}, u32[]{:S(2)}, u32[]{:S(2)}) %collective-permute-start.26) | collective-permute-done | bytes 393248 | tf_op jit(solution)/shard_map/ppermute | solution.py:27
  121.6 3.9 %collective-permute-done.27 = bf16[4,3,32,512]{3,2,1,0:T(8,128)(2,1)S(1)} collective-permute-done((bf16[4,3,32,512]{3,2,1,0:T(8,128)(2,1)S(1)}, bf16[4,3,32,512]{3,2,1,0:T(8,128)(2,1)S(1)}, u32[]{:S(2)}, u32[]{:S(2)}) %collective-permute-start.27) | collective-permute-done | bytes 393248 | tf_op jit(solution)/shard_map/ppermute | solution.py:27
  125.5 0.1 maximum_bitcast_fusion
  125.6 0.4 pad_maximum_fusion.mine
  126.0 0.0 copy-start.1
  126.1 0.1 collective-permute-start.28
  126.2 0.5 collective-permute-start.29
  126.7 1.0 pad_add_fusion.ids
  127.6 6.8 %collective-permute-done.29.row_other = bf16[4,512,512]{2,1,0:T(8,128)(2,1)S(1)} collective-permute-done((bf16[4,512,512]{2,1,0:T(8,128)(2,1)S(1)}, bf16[4,512,512]{2,1,0:T(8,128)(2,1)S(1)}, u32[]{:S(2)}, u32[]{:S(2)}) %collective-permute-start.29) | collective-permute-done | bytes 2097184 | tf_op jit(solution)/shard_map/ppermute | solution.py:28
  134.4 1.3 copy-done.5
  135.8 2.2 %all-gather.3.cloned.1.call-done = bf16[128,64,512]{2,1,0:T(8,128)(2,1)} async-done(((bf16[4,64,512]{2,1,0:T(8,128)(2,1)}), bf16[128,64,512]{2,1,0:T(8,128)(2,1)}) %all-gather.3.cloned.1.call-update) | async-done | bytes 8388624 | tf_op jit(solution)/shard_map/all_gather | solution.py:156
  138.0 33.2 %shard_map.46 = f32[4,512,512]{2,1,0:T(8,128)} custom-call(s32[2]{0:T(128)} %pad_add_fusion.ids, s32[32,32]{1,0:T(8,128)} %shape.1, bf16[4,8,3,32,512]{4,3,2,1,0:T(8,128)(2,1)} %copy-done.1, bf16[4,8,3,32,512]{4,3,2,1,0:T(8,128)(2,1)} %collective-permute-done.28.other, bf16[4,512,512]{2,1,0:T(8,128)(2,1)} %copy-done.2, bf16[4,512,512]{2,1,0:T(8,128)(2,1)} %copy-done.5, ...), custom_call_target="tpu_custom_call" | custom-call | flops 23085449216 | bytes 31457280 | tf_op jit(solution)/shard_map/pallas_call | solution.py:115
  171.2 6.9 %copy.8 = f32[1,512,4,512]{3,2,1,0:T(4,128)} copy(f32[1,512,4,512]{3,1,2,0:T(8,128)} %bitcast.53) | data formatting | bytes 8388608 | tf_op jit(solution)/shard_map/broadcast_in_dim | solution.py:174
  (41 shorter events, 0.3 us)
Async XLA Ops:
  6.5 131.5 %all-gather.3.cloned.1.call-start = ((), (), s32[]{:S(2)}) async-start(), calls=%async_computation | async-start | bytes 8650752 | tf_op jit(solution)/shard_map/all_gather | solution.py:156
  8.5 29.2 %copy-start = (bf16[1,512,4,512]{3,1,2,0:T(8,128)(2,1)}, bf16[1,512,4,512]{3,1,2,0:T(8,128)(2,1)S(1)}, u32[]{:S(2)}) copy-start(bf16[1,512,4,512]{3,1,2,0:T(8,128)(2,1)S(1)} %copy.10) | copy-start | bytes 6291460
  9.6 15.8 %collective-permute-start.6 = (bf16[4,64,512]{2,1,0:T(8,128)(2,1)S(1)}, bf16[4,64,512]{2,1,0:T(8,128)(2,1)S(1)}, u32[]{:S(2)}, u32[]{:S(2)}) collective-permute-start(bf16[4,64,512]{2,1,0:T(8,128)(2,1)S(1)} %get-tuple-element.19), channel_id=1, source_target_pairs={{0,32},{8,40},{16,48},{24,56},{1,33},{9,41},{17,49},{25,57},{2,34}... | collective-permute-start | bytes 786440 | tf_op jit(solution)/shard_map/ppermute | solution.py:150
  13.5 13.9 %collective-permute-start.5 = (bf16[4,64,512]{2,1,0:T(8,128)(2,1)S(1)}, bf16[4,64,512]{2,1,0:T(8,128)(2,1)S(1)}, u32[]{:S(2)}, u32[]{:S(2)}) collective-permute-start(bf16[4,64,512]{2,1,0:T(8,128)(2,1)S(1)} %get-tuple-element.20), channel_id=1, source_target_pairs={{0,128},{8,136},{16,144},{24,152},{1,129},{9,137},{17,145},{25,153... | collective-permute-start | bytes 786440 | tf_op jit(solution)/shard_map/ppermute | solution.py:150
  19.4 10.0 %collective-permute-start.4 = (bf16[4,64,512]{2,1,0:T(8,128)(2,1)}, bf16[4,64,512]{2,1,0:T(8,128)(2,1)}, u32[]{:S(2)}, u32[]{:S(2)}) collective-permute-start(bf16[4,64,512]{2,1,0:T(8,128)(2,1)} %get-tuple-element.21), channel_id=1, source_target_pairs={{0,160},{8,168},{16,176},{24,184},{1,161},{9,169},{17,177},{25,185... | collective-permute-start | bytes 786440 | tf_op jit(solution)/shard_map/ppermute | solution.py:150
  21.4 10.4 %collective-permute-start.3 = (bf16[4,64,512]{2,1,0:T(8,128)(2,1)}, bf16[4,64,512]{2,1,0:T(8,128)(2,1)}, u32[]{:S(2)}, u32[]{:S(2)}) collective-permute-start(bf16[4,64,512]{2,1,0:T(8,128)(2,1)} %get-tuple-element.22), channel_id=1, source_target_pairs={{0,96},{8,104},{16,112},{24,120},{1,97},{9,105},{17,113},{25,121},... | collective-permute-start | bytes 786440 | tf_op jit(solution)/shard_map/ppermute | solution.py:150
  23.4 9.8 %collective-permute-start.2 = (bf16[4,64,512]{2,1,0:T(8,128)(2,1)S(1)}, bf16[4,64,512]{2,1,0:T(8,128)(2,1)}, u32[]{:S(2)}, u32[]{:S(2)}) collective-permute-start(bf16[4,64,512]{2,1,0:T(8,128)(2,1)S(1)} %get-tuple-element.23), channel_id=1, source_target_pairs={{0,192},{8,200},{16,208},{24,216},{1,193},{9,201},{17,209},{25,217... | collective-permute-start | bytes 786440 | tf_op jit(solution)/shard_map/ppermute | solution.py:150
  25.4 4.0 %copy-start.3 = (bf16[4,64,512]{2,1,0:T(8,128)(2,1)}, bf16[4,64,512]{2,1,0:T(8,128)(2,1)S(1)}, u32[]{:S(2)}) copy-start(bf16[4,64,512]{2,1,0:T(8,128)(2,1)S(1)} %collective-permute-done.6) | copy-start | bytes 786436
  25.4 10.8 %collective-permute-start.1 = (bf16[4,64,512]{2,1,0:T(8,128)(2,1)S(1)}, bf16[4,64,512]{2,1,0:T(8,128)(2,1)}, u32[]{:S(2)}, u32[]{:S(2)}) collective-permute-start(bf16[4,64,512]{2,1,0:T(8,128)(2,1)S(1)} %get-tuple-element.24), channel_id=1, source_target_pairs={{0,64},{8,72},{16,80},{24,88},{1,65},{9,73},{17,81},{25,89},{2,66}... | collective-permute-start | bytes 786440 | tf_op jit(solution)/shard_map/ppermute | solution.py:150
  27.4 2.0 %copy-start.4 = (bf16[4,64,512]{2,1,0:T(8,128)(2,1)}, bf16[4,64,512]{2,1,0:T(8,128)(2,1)S(1)}, u32[]{:S(2)}) copy-start(bf16[4,64,512]{2,1,0:T(8,128)(2,1)S(1)} %collective-permute-done.5) | copy-start | bytes 786436
  27.4 10.3 %collective-permute-start = (bf16[4,64,512]{2,1,0:T(8,128)(2,1)S(1)}, bf16[4,64,512]{2,1,0:T(8,128)(2,1)}, u32[]{:S(2)}, u32[]{:S(2)}) collective-permute-start(bf16[4,64,512]{2,1,0:T(8,128)(2,1)S(1)} %get-tuple-element.25), channel_id=1, source_target_pairs={{0,224},{8,232},{16,240},{24,248},{1,225},{9,233},{17,241},{25,249... | collective-permute-start | bytes 786440 | tf_op jit(solution)/shard_map/ppermute | solution.py:150
  38.6 12.9 %collective-permute-start.8 = (bf16[512,512]{1,0:T(8,128)(2,1)S(1)}, bf16[512,512]{1,0:T(8,128)(2,1)S(1)}, u32[]{:S(2)}, u32[]{:S(2)}) collective-permute-start(bf16[512,512]{1,0:T(8,128)(2,1)S(1)} %slice_bitcast_fusion), channel_id=1, source_target_pairs={{0,2},{1,3},{2,4},{3,5},{4,6},{5,7},{6,0},{7,1},{8,10},{9,11},{10,... | collective-permute-start | bytes 1572872 | tf_op jit(solution)/shard_map/ppermute | solution.py:27
  39.9 12.5 %collective-permute-start.7 = (bf16[512,512]{1,0:T(8,128)(2,1)S(1)}, bf16[512,512]{1,0:T(8,128)(2,1)S(1)}, u32[]{:S(2)}, u32[]{:S(2)}) collective-permute-start(bf16[512,512]{1,0:T(8,128)(2,1)S(1)} %slice_bitcast_fusion), channel_id=1, source_target_pairs={{0,6},{1,7},{2,0},{3,1},{4,2},{5,3},{6,4},{7,5},{8,14},{9,15},{10,... | collective-permute-start | bytes 1572872 | tf_op jit(solution)/shard_map/ppermute | solution.py:27
  52.5 2.0 %collective-permute-start.10 = (bf16[32,512]{1,0:T(8,128)(2,1)S(1)}, bf16[32,512]{1,0:T(8,128)(2,1)S(1)}, u32[]{:S(2)}, u32[]{:S(2)}) collective-permute-start(bf16[32,512]{1,0:T(8,128)(2,1)S(1)} %get-tuple-element.26), channel_id=1, source_target_pairs={{0,1},{1,3},{2,5},{3,7},{8,9},{9,11},{10,13},{11,15},{16,17},{17,1... | collective-permute-start | bytes 98312 | tf_op jit(solution)/shard_map/ppermute | solution.py:160
  53.1 5.8 %collective-permute-start.9 = (bf16[32,512]{1,0:T(8,128)(2,1)S(1)}, bf16[32,512]{1,0:T(8,128)(2,1)S(1)}, u32[]{:S(2)}, u32[]{:S(2)}) collective-permute-start(bf16[32,512]{1,0:T(8,128)(2,1)S(1)} %get-tuple-element.27), channel_id=1, source_target_pairs={{0,0},{1,2},{2,4},{3,6},{8,8},{9,10},{10,12},{11,14},{16,16},{17,1... | collective-permute-start | bytes 98312 | tf_op jit(solution)/shard_map/ppermute | solution.py:159
  58.9 4.4 %collective-permute-start.11 = (bf16[32,512]{1,0:T(8,128)(2,1)S(1)}, bf16[32,512]{1,0:T(8,128)(2,1)S(1)}, u32[]{:S(2)}, u32[]{:S(2)}) collective-permute-start(bf16[32,512]{1,0:T(8,128)(2,1)S(1)} %broadcast_select_fusion), channel_id=1, source_target_pairs={{0,24},{8,0},{16,8},{24,16},{32,56},{40,32},{48,40},{56,48},{64,88... | collective-permute-start | bytes 98312 | tf_op jit(solution)/shard_map/ppermute | solution.py:25
  61.8 8.2 %collective-permute-start.13 = (bf16[32,512]{1,0:T(8,128)(2,1)S(1)}, bf16[32,512]{1,0:T(8,128)(2,1)S(1)}, u32[]{:S(2)}, u32[]{:S(2)}) collective-permute-start(bf16[32,512]{1,0:T(8,128)(2,1)S(1)} %broadcast_select_fusion), channel_id=1, source_target_pairs={{0,8},{8,16},{16,24},{24,0},{32,40},{40,48},{48,56},{56,32},{64,72... | collective-permute-start | bytes 98312 | tf_op jit(solution)/shard_map/ppermute | solution.py:25
  63.4 6.6 %collective-permute-start.12 = (bf16[32,512]{1,0:T(8,128)(2,1)S(1)}, bf16[32,512]{1,0:T(8,128)(2,1)S(1)}, u32[]{:S(2)}, u32[]{:S(2)}) collective-permute-start(bf16[32,512]{1,0:T(8,128)(2,1)S(1)} %collective-permute-done.11), channel_id=1, source_target_pairs={{0,24},{8,0},{16,8},{24,16},{32,56},{40,32},{48,40},{56,48},{64,88... | collective-permute-start | bytes 98312 | tf_op jit(solution)/shard_map/ppermute | solution.py:25
  66.9 14.6 %collective-permute-start.22 = (bf16[256,512]{1,0:T(8,128)(2,1)S(1)}, bf16[256,512]{1,0:T(8,128)(2,1)S(1)}, u32[]{:S(2)}, u32[]{:S(2)}) collective-permute-start(bf16[256,512]{1,0:T(8,128)(2,1)S(1)} %slice.68), channel_id=1, source_target_pairs={{0,2},{1,3},{2,4},{3,5},{4,6},{5,7},{6,0},{7,1},{8,10},{9,11},{10,... | collective-permute-start | bytes 786440 | tf_op jit(solution)/shard_map/ppermute | solution.py:27
  70.0 11.6 %collective-permute-start.23 = (bf16[256,512]{1,0:T(8,128)(2,1)S(1)}, bf16[256,512]{1,0:T(8,128)(2,1)S(1)}, u32[]{:S(2)}, u32[]{:S(2)}) collective-permute-start(bf16[256,512]{1,0:T(8,128)(2,1)S(1)} %slice.69), channel_id=1, source_target_pairs={{0,6},{1,7},{2,0},{3,1},{4,2},{5,3},{6,4},{7,5},{8,14},{9,15},{10,... | collective-permute-start | bytes 786440 | tf_op jit(solution)/shard_map/ppermute | solution.py:27
  70.0 8.2 %collective-permute-start.14 = (bf16[3,32,512]{2,1,0:T(8,128)(2,1)S(1)}, bf16[3,32,512]{2,1,0:T(8,128)(2,1)S(1)}, u32[]{:S(2)}, u32[]{:S(2)}) collective-permute-start(bf16[3,32,512]{2,1,0:T(8,128)(2,1)S(1)} %pad_maximum_fusion.2), channel_id=1, source_target_pairs={{0,32},{8,40},{16,48},{24,56},{32,64},{40,72},{48,80},{56,88},{64,... | collective-permute-start | bytes 294920 | tf_op jit(solution)/shard_map/ppermute | solution.py:23
  70.1 8.2 %collective-permute-start.18 = (bf16[3,32,512]{2,1,0:T(8,128)(2,1)S(1)}, bf16[3,32,512]{2,1,0:T(8,128)(2,1)S(1)}, u32[]{:S(2)}, u32[]{:S(2)}) collective-permute-start(bf16[3,32,512]{2,1,0:T(8,128)(2,1)S(1)} %pad_maximum_fusion.2), channel_id=1, source_target_pairs={{0,224},{8,232},{16,240},{24,248},{32,0},{40,8},{48,16},{56,24},{6... | collective-permute-start | bytes 294920 | tf_op jit(solution)/shard_map/ppermute | solution.py:23
  78.3 6.6 %collective-permute-start.15 = (bf16[3,32,512]{2,1,0:T(8,128)(2,1)S(1)}, bf16[3,32,512]{2,1,0:T(8,128)(2,1)S(1)}, u32[]{:S(2)}, u32[]{:S(2)}) collective-permute-start(bf16[3,32,512]{2,1,0:T(8,128)(2,1)S(1)} %collective-permute-done.14), channel_id=1, source_target_pairs={{0,32},{8,40},{16,48},{24,56},{32,64},{40,72},{48,80},{56,88},{64,... | collective-permute-start | bytes 294920 | tf_op jit(solution)/shard_map/ppermute | solution.py:23
  78.3 6.6 %collective-permute-start.19 = (bf16[3,32,512]{2,1,0:T(8,128)(2,1)S(1)}, bf16[3,32,512]{2,1,0:T(8,128)(2,1)S(1)}, u32[]{:S(2)}, u32[]{:S(2)}) collective-permute-start(bf16[3,32,512]{2,1,0:T(8,128)(2,1)S(1)} %collective-permute-done.18), channel_id=1, source_target_pairs={{0,224},{8,232},{16,240},{24,248},{32,0},{40,8},{48,16},{56,24},{6... | collective-permute-start | bytes 294920 | tf_op jit(solution)/shard_map/ppermute | solution.py:23
  81.9 44.3 %copy-start.2 = (bf16[4,512,512]{2,1,0:T(8,128)(2,1)}, bf16[4,512,512]{2,1,0:T(8,128)(2,1)S(1)}, u32[]{:S(2)}) copy-start(bf16[4,512,512]{2,1,0:T(8,128)(2,1)S(1)} %pad_maximum_fusion.1.row_mine) | copy-start | bytes 6291460
  84.9 5.8 %collective-permute-start.16 = (bf16[3,32,512]{2,1,0:T(8,128)(2,1)S(1)}, bf16[3,32,512]{2,1,0:T(8,128)(2,1)S(1)}, u32[]{:S(2)}, u32[]{:S(2)}) collective-permute-start(bf16[3,32,512]{2,1,0:T(8,128)(2,1)S(1)} %collective-permute-done.15), channel_id=1, source_target_pairs={{0,32},{8,40},{16,48},{24,56},{32,64},{40,72},{48,80},{56,88},{64,... | collective-permute-start | bytes 294920 | tf_op jit(solution)/shard_map/ppermute | solution.py:23
  84.9 5.8 %collective-permute-start.20 = (bf16[3,32,512]{2,1,0:T(8,128)(2,1)S(1)}, bf16[3,32,512]{2,1,0:T(8,128)(2,1)S(1)}, u32[]{:S(2)}, u32[]{:S(2)}) collective-permute-start(bf16[3,32,512]{2,1,0:T(8,128)(2,1)S(1)} %collective-permute-done.19), channel_id=1, source_target_pairs={{0,224},{8,232},{16,240},{24,248},{32,0},{40,8},{48,16},{56,24},{6... | collective-permute-start | bytes 294920 | tf_op jit(solution)/shard_map/ppermute | solution.py:23
  90.7 6.2 %collective-permute-start.17 = (bf16[3,16,512]{2,1,0:T(8,128)(2,1)S(1)}, bf16[3,16,512]{2,1,0:T(8,128)(2,1)S(1)}, u32[]{:S(2)}, u32[]{:S(2)}) collective-permute-start(bf16[3,16,512]{2,1,0:T(8,128)(2,1)S(1)} %slice.82), channel_id=1, source_target_pairs={{0,32},{8,40},{16,48},{24,56},{32,64},{40,72},{48,80},{56,88},{64,... | collective-permute-start | bytes 147464 | tf_op jit(solution)/shard_map/ppermute | solution.py:23
  90.7 6.1 %collective-permute-start.21 = (bf16[3,16,512]{2,1,0:T(8,128)(2,1)S(1)}, bf16[3,16,512]{2,1,0:T(8,128)(2,1)S(1)}, u32[]{:S(2)}, u32[]{:S(2)}) collective-permute-start(bf16[3,16,512]{2,1,0:T(8,128)(2,1)S(1)} %slice.83), channel_id=1, source_target_pairs={{0,224},{8,232},{16,240},{24,248},{32,0},{40,8},{48,16},{56,24},{6... | collective-permute-start | bytes 147464 | tf_op jit(solution)/shard_map/ppermute | solution.py:23
  97.0 16.6 %collective-permute-start.25 = (bf16[8,3,32,512]{3,2,1,0:T(8,128)(2,1)S(1)}, bf16[8,3,32,512]{3,2,1,0:T(8,128)(2,1)S(1)}, u32[]{:S(2)}, u32[]{:S(2)}) collective-permute-start(bf16[8,3,32,512]{3,2,1,0:T(8,128)(2,1)S(1)} %bitcast_dynamic-update-slice_fusion), channel_id=1, source_target_pairs={{0,2},{1,3},{2,4},{3,5},{4,6},{5,7},{6,0},{7,1},{8,10},{9,11},{10,... | collective-permute-start | bytes 2359304 | tf_op jit(solution)/shard_map/ppermute | solution.py:27
  99.9 16.5 %collective-permute-start.24 = (bf16[8,3,32,512]{3,2,1,0:T(8,128)(2,1)S(1)}, bf16[8,3,32,512]{3,2,1,0:T(8,128)(2,1)S(1)}, u32[]{:S(2)}, u32[]{:S(2)}) collective-permute-start(bf16[8,3,32,512]{3,2,1,0:T(8,128)(2,1)S(1)} %bitcast_dynamic-update-slice_fusion), channel_id=1, source_target_pairs={{0,6},{1,7},{2,0},{3,1},{4,2},{5,3},{6,4},{7,5},{8,14},{9,15},{10,... | collective-permute-start | bytes 2359304 | tf_op jit(solution)/shard_map/ppermute | solution.py:27
  113.6 8.0 %collective-permute-start.26 = (bf16[4,3,32,512]{3,2,1,0:T(8,128)(2,1)S(1)}, bf16[4,3,32,512]{3,2,1,0:T(8,128)(2,1)S(1)}, u32[]{:S(2)}, u32[]{:S(2)}) collective-permute-start(bf16[4,3,32,512]{3,2,1,0:T(8,128)(2,1)S(1)} %slice.84), channel_id=1, source_target_pairs={{0,2},{1,3},{2,4},{3,5},{4,6},{5,7},{6,0},{7,1},{8,10},{9,11},{10,... | collective-permute-start | bytes 1179656 | tf_op jit(solution)/shard_map/ppermute | solution.py:27
  116.3 9.2 %collective-permute-start.27 = (bf16[4,3,32,512]{3,2,1,0:T(8,128)(2,1)S(1)}, bf16[4,3,32,512]{3,2,1,0:T(8,128)(2,1)S(1)}, u32[]{:S(2)}, u32[]{:S(2)}) collective-permute-start(bf16[4,3,32,512]{3,2,1,0:T(8,128)(2,1)S(1)} %slice.85), channel_id=1, source_target_pairs={{0,6},{1,7},{2,0},{3,1},{4,2},{5,3},{6,4},{7,5},{8,14},{9,15},{10,... | collective-permute-start | bytes 1179656 | tf_op jit(solution)/shard_map/ppermute | solution.py:27
  126.0 12.0 %copy-start.1 = (bf16[4,8,3,32,512]{4,3,2,1,0:T(8,128)(2,1)}, bf16[4,8,3,32,512]{4,3,2,1,0:T(8,128)(2,1)S(1)}, u32[]{:S(2)}) copy-start(bf16[4,8,3,32,512]{4,3,2,1,0:T(8,128)(2,1)S(1)} %pad_maximum_fusion.mine) | copy-start | bytes 9437188
  126.1 9.7 %collective-permute-start.28 = (bf16[4,8,3,32,512]{4,3,2,1,0:T(8,128)(2,1)S(1)}, bf16[4,8,3,32,512]{4,3,2,1,0:T(8,128)(2,1)}, u32[]{:S(2)}, u32[]{:S(2)}) collective-permute-start(bf16[4,8,3,32,512]{4,3,2,1,0:T(8,128)(2,1)S(1)} %pad_maximum_fusion.mine), channel_id=1, source_target_pairs={{0,1},{1,0},{2,3},{3,2},{4,5},{5,4},{6,7},{7,6},{8,9},{9,8},{10,11... | collective-permute-start | bytes 9437192 | tf_op jit(solution)/shard_map/ppermute | solution.py:28
  126.2 8.3 %collective-permute-start.29 = (bf16[4,512,512]{2,1,0:T(8,128)(2,1)S(1)}, bf16[4,512,512]{2,1,0:T(8,128)(2,1)S(1)}, u32[]{:S(2)}, u32[]{:S(2)}) collective-permute-start(bf16[4,512,512]{2,1,0:T(8,128)(2,1)S(1)} %pad_maximum_fusion.1.row_mine), channel_id=1, source_target_pairs={{0,1},{1,0},{2,3},{3,2},{4,5},{5,4},{6,7},{7,6},{8,9},{9,8},{10,11... | collective-permute-start | bytes 6291464 | tf_op jit(solution)/shard_map/ppermute | solution.py:28
  134.4 1.3 copy-start.5
Sparse Core Ops, SparseCore 0:
  38.7 99.2 all-gather.2

commit v3 on v2

v3 whole, which is shorter than its diff:
```python
import functools

import jax
import jax.numpy as jnp
from jax import lax
from jax.experimental import pallas as pl
from jax.experimental.pallas import tpu as pltpu
from jax.sharding import PartitionSpec as P

STEPS = 4
HALF = jnp.bfloat16
FULL = jnp.float32
VMEM_LIMIT = 56 * 1024 * 1024


def mm(a, b):
    return jnp.dot(a, b, preferred_element_type=FULL)


def shift(block, way):
    move = 1 if way[-1] == "+" else -1
    if way[0] == "z":
        return lax.ppermute(block, "prow", [(i, (i + 4 * move) % 32) for i in range(32)])
    if way[0] == "x":
        return lax.ppermute(block, "prow", [(i, i // 4 * 4 + (i + move) % 4) for i in range(32)])
    if way[0] == "y":
        return lax.ppermute(block, "pcol", [(i, (i + 2 * move) % 8) for i in range(8)])
    return lax.ppermute(block, "pcol", [(i, i ^ 1) for i in range(8)])


def around_eight(block):
    half = block.shape[1] // 2
    up, down = [block], [block]
    for _ in range(3):
        up.append(shift(up[-1], "z+"))
        down.append(shift(down[-1], "z-"))
    far = [shift(up[3][:, :half], "z+"), shift(down[3][:, half:], "z-")]
    return up + [jnp.concatenate(far, axis=1)] + down[:0:-1]


def cut(k, n):
    return slice(k * n, (k + 1) * n)


def factor_kernel(ids, shape, *refs):
    mine, other, (row_mine, row_other, v, w, low, left, up) = refs[:4], refs[4:8], refs[8:]
    n = v.shape[1]
    p, q = ids[0], ids[1]
    z, x, y, core = p // 4, lax.rem(p, 4), q // 2, lax.rem(q, 2)

    def raw_corner(k, m):
        dx, dy, gap = lax.rem(k - x + 4, 4), lax.rem(m - y + 4, 4), lax.rem(m - x + 4, 4)
        at = jnp.where(dx < gap, dx, jnp.maximum(dx - 1, 0))
        odd, upper_half = lax.rem(dy, 2) == 1, dy >= 2

        def pick(four, away):
            low_pair = jnp.where(odd, four[1][away, at], four[0][away, at])
            return jnp.where(upper_half, jnp.where(odd, four[3][away, at], four[2][away, at]), low_pair)

        parts = []
        for i in range(8):
            away = lax.rem(z - i + 8, 8)
            here, there = pick(mine, away), pick(other, away)
            parts += [jnp.where(core == 0, here, there), jnp.where(core == 0, there, here)]
        return jnp.concatenate(parts, axis=0)

    def raw_row(k):
        dy = lax.rem(k // 2 - y + 4, 4)
        return jnp.where(core == k % 2, row_mine[dy], row_other[dy])

    def fill(ref, rows, cols, present, make):
        @pl.when(present)
        def _():
            ref[rows, cols] = make().astype(HALF)

        @pl.when(jnp.logical_not(present))
        def _():
            ref[rows, cols] = jnp.zeros((n, n), HALF)

    def less(block, a, b):
        return (block.astype(FULL) - mm(a, b)).astype(HALF)

    for k in range(3):
        for i in range(k + 1, 4):

            def make_low():
                block = raw_corner(i, k)
                if k:
                    block = less(block, low[i - 1, :, 0 : k * n], up[0 : k * n, cut(k, n)])
                return mm(block, v[k])

            def make_up():
                block = raw_corner(k, i)
                if k:
                    block = less(block, low[k - 1, :, 0 : k * n], up[0 : k * n, cut(i, n)])
                return mm(w[k], block)

            fill(low.at[i - 1], slice(None), cut(k, n), shape[i, k] != 0, make_low)
            fill(up, cut(k, n), cut(i, n), shape[k, i] != 0, make_up)
    for k in range(4):

        def make_left():
            block = raw_row(k)
            if k:
                block = less(block, left[:, 0 : k * n], up[0 : k * n, cut(k, n)])
            return mm(block, v[k])

        fill(left, slice(None), cut(k, n), jnp.logical_and(p > k, shape[p, k] != 0), make_left)


def column_kernel(ids, shape, raw, own, low, left, w, whole_out, upper, out):
    n = w.shape[1]
    p, q = ids[0], ids[1]
    c = pl.program_id(0)
    j = c * 8 + q
    for k in range(4):
        present = jnp.logical_and(j > k, shape[k, j] != 0)

        @pl.when(present)
        def _():
            block = jnp.concatenate([raw[i * 4 + k, 0] for i in range(8)], axis=0)
            if k:
                block = (block.astype(FULL) - mm(low[k - 1, :, 0 : k * n], upper[0 : k * n, :])).astype(HALF)
            upper[cut(k, n), :] = mm(w[k], block).astype(HALF)

        @pl.when(jnp.logical_not(present))
        def _():
            upper[cut(k, n), :] = jnp.zeros((n, n), HALF)

    @pl.when(shape[p, j] != 0)
    def _():
        out[...] = own[0].astype(FULL) - mm(left[...], upper[...])

    @pl.when(shape[p, j] == 0)
    def _():
        out[...] = own[0].astype(FULL)

    @pl.when(jnp.logical_and(p < STEPS, j > p))
    def _():
        out[...] = upper[pl.ds(pl.multiple_of(jnp.minimum(p, 3) * n, n), n), :].astype(FULL)

    @pl.when(jnp.logical_and(j < STEPS, p > j))
    def _():
        out[...] = left[:, pl.ds(pl.multiple_of(jnp.minimum(j, 3) * n, n), n)].astype(FULL)

    for i in range(4):

        @pl.when(c == i)
        def _():
            whole_out[:, i, :] = out[...]


def factor(ids, shape, corner, row, v, w):
    n = v.shape[1]
    vmem = pl.BlockSpec(memory_space=pltpu.VMEM)
    smem = pl.BlockSpec(memory_space=pltpu.SMEM)
    return pl.pallas_call(
        factor_kernel,
        out_shape=(
            jax.ShapeDtypeStruct((3, n, 3 * n), HALF),
            jax.ShapeDtypeStruct((n, 4 * n), HALF),
        ),
        in_specs=[smem, smem] + [vmem] * 12,
        out_specs=(vmem, vmem),
        scratch_shapes=[pltpu.VMEM((3 * n, 4 * n), HALF)],
        compiler_params=pltpu.CompilerParams(vmem_limit_bytes=VMEM_LIMIT),
        cost_estimate=pl.CostEstimate(flops=60 * n**3, bytes_accessed=18 * 2**20, transcendentals=0),
    )(ids, shape, *corner, *row, v, w)


def columns(ids, shape, raw, own, low, left, w):
    n = w.shape[1]
    smem = pl.BlockSpec(memory_space=pltpu.SMEM)
    whole = lambda a: pl.BlockSpec(a.shape, lambda c: (0,) * a.ndim, pipeline_mode=pl.Buffered(1))
    return pl.pallas_call(
        column_kernel,
        grid=(4,),
        out_shape=jax.ShapeDtypeStruct((n, 4, n), FULL),
        in_specs=[
            smem,
            smem,
            pl.BlockSpec((32, 1, n // 8, n), lambda c: (0, c, 0, 0)),
            pl.BlockSpec((1, n, n), lambda c: (c, 0, 0)),
            whole(low),
            whole(left),
            whole(w),
        ],
        out_specs=pl.BlockSpec((n, 4, n), lambda c: (0, 0, 0)),
        scratch_shapes=[pltpu.VMEM((4 * n, n), HALF), pltpu.VMEM((n, n), FULL)],
        compiler_params=pltpu.CompilerParams(vmem_limit_bytes=VMEM_LIMIT),
        cost_estimate=pl.CostEstimate(flops=112 * n**3, bytes_accessed=24 * 2**20, transcendentals=0),
    )(ids, shape, raw, own, low, left, w)


def on_device(matrix, upper_inverse, lower_inverse, structure):
    p = lax.axis_index("prow")
    q = lax.axis_index("pcol")
    z, core = p // 4, lax.rem(q, 2)
    n = matrix.shape[1]
    part = n // 8
    own = jnp.transpose(matrix[0], (1, 0, 2))
    ids = jnp.stack([p, q]).astype(jnp.int32)

    piece = own[:, :part]
    came = {}
    for s in (1, 4, 5, 3, 6, 2, 7):
        to = [(i, i + 4 * s) for i in range(4)]
        came[s] = lax.ppermute(own[:, s * part : (s + 1) * part], "prow", to)
    row, came[1] = lax.optimization_barrier((own[0], came[1]))
    row_above, row_below = shift(row, "y-"), shift(row, "y+")
    for s in came:
        piece = jnp.where(z == s, came[s], piece)

    raw = lax.all_gather(piece, "prow")

    first = lax.ppermute(piece[0, : part // 2], "pcol", [(i, 2 * i) for i in range(4)])
    second = lax.ppermute(piece[0, part // 2 :], "pcol", [(i, 2 * i + 1) for i in range(4)])
    corner = jnp.where(core == 0, first, second)
    corner = [corner, shift(corner, "x-"), shift(shift(corner, "x-"), "x-"), shift(corner, "x+")]
    gap = lax.rem(q // 2 - p % 4 + 4, 4)
    corner = jnp.stack([jnp.where(i < gap, corner[i], corner[i + 1]) for i in range(3)])
    corner, row_above, row_below = lax.optimization_barrier((corner, row_above, row_below))
    corner = jnp.stack(around_eight(corner))
    above, below = shift(corner, "y-"), shift(corner, "y+")
    row_far = [shift(row_below[: n // 2], "y+"), shift(row_above[n // 2 :], "y-")]
    row = jnp.stack([own[0], row_above, jnp.concatenate(row_far, axis=0), row_below])
    row = [row, shift(row, "c")]
    above, below, row = lax.optimization_barrier((above, below, row))
    far = jnp.concatenate([shift(below[:4], "y+"), shift(above[4:], "y-")], axis=0)
    corner = [corner, above, far, below]
    corner = corner + [shift(block, "c") for block in corner]

    low, left = factor(ids, structure, corner, row, upper_inverse, lower_inverse)
    out = columns(ids, structure, raw, own, low, left, lower_inverse)
    return out[None]


def solution(mesh):
    return jax.shard_map(
        on_device,
        mesh=mesh,
        in_specs=(P(None, "prow", None, "pcol"), P(), P(), P()),
        out_specs=P(None, "prow", None, "pcol"),
        check_vma=False,
    )
```

time: 186 us -> 169 us (0.909); the launches traced: 185 us -> 166 us
  local copies, waits for them, and re-layouts: 12.4 us -> 4.36 us
  waiting for transfers between devices: 68.8 us -> 64.4 us
  starting transfers between devices: 54.2 us -> 51.2 us
  Pallas kernels: 33.2 us -> 30.3 us
    broadcast_in_dim x1 -> x0, local copies, waits for them, and re-layouts: 6.9 us -> none  [on_device(): return jnp.transpose(out, (1, 0, 2))[None]]
    all_gather x1, waiting for transfers between devices: 2.25 us -> 9.1 us  [on_device(): raw = lax.all_gather(piece, 'prow')]
    ppermute x2 -> x5, waiting for transfers between devices: 6.82 us -> 1.65 us  [shift(): return lax.ppermute(block, 'pcol', [(i, i ^ 1) for i in range(8)])]
    ppermute x8, waiting for transfers between devices: 33.9 us -> 29.6 us  [shift(): lax.ppermute(block, 'pcol', [(i, (i + 2 * move) % 8) for i in range(8)])]
    ppermute x2, waiting for transfers between devices: 4.49 us -> 0.48 us  [the longest x1 0.48 us: on_device(): lax.ppermute(piece[0, :part // 2], 'pcol', [(i, 2 * i) for i in range(4)])]
    pallas_call x1 -> x2, Pallas kernels: 33.2 us -> 30.3 us  [the longest x1 19.5 us: columns(): pl.pallas_call(column_kernel, grid=(4,), out_shape=jax.ShapeDtypeStruct((...]
    ppermute x8, starting transfers between devices: 14.9 us -> 13 us  [shift(): lax.ppermute(block, 'prow', [(i, (i + 4 * move) % 32) for i in range(32)])]
  transfers between devices with their start and end apart: 31 -> 34, of which waited for: 18 -> 21; matrix products, arithmetic and copies ran while one was open for 2% -> 1% of each run, Pallas kernels for 0% -> 6%
where the time goes in v3:
time: 169 us; the launch traced here: 166 us
  waiting for transfers between devices  64.4 us (38%)
  starting transfers between devices  51.2 us (30%)
  Pallas kernels  30.3 us (18%)
  between operations  13.7 us (8%)
  local copies, waits for them, and re-layouts  4.36 us (3%)
  other arithmetic  1.89 us (1%)
    ppermute x8, waiting for transfers between devices, shift(): lax.ppermute(block, 'pcol', [(i, (i + 2 * move) % 8) for i in range(8)])  29.6 us
    pallas_call x1, Pallas kernels, columns(): pl.pallas_call(column_kernel, grid=(4,), out_shape=jax.ShapeDtypeStruct((...  19.5 us
    ppermute x7, starting transfers between devices, on_device(): came[s] = lax.ppermute(own[:, s * part:(s + 1) * part], 'prow', to)  18.4 us
    ppermute x8, starting transfers between devices, shift(): lax.ppermute(block, 'prow', [(i, (i + 4 * move) % 32) for i in range(32)])  13 us
    ppermute x8, waiting for transfers between devices, shift(): lax.ppermute(block, 'prow', [(i, (i + 4 * move) % 32) for i in range(32)])  12.1 us
    pallas_call x1, Pallas kernels, factor(): pl.pallas_call(factor_kernel, out_shape=(jax.ShapeDtypeStruct((3, n, 3 *...  10.8 us
    ppermute x8, starting transfers between devices, shift(): lax.ppermute(block, 'pcol', [(i, (i + 2 * move) % 8) for i in range(8)])  10.6 us
    all_gather x1, waiting for transfers between devices, on_device(): raw = lax.all_gather(piece, 'prow')  9.1 us
  transfers between devices with their start and end apart: 34, of which 21 were waited for; matrix products, arithmetic and copies ran while one was open for 1% of the time, Pallas kernels for 6%

profile of v3, /device:TPU:16, one launch (start us, length us, event | category | flops | bytes accessed | tf_op | source)
XLA Modules:
  0.0 165.8 jit_solution(12444275885658763654)
XLA Ops:
  6.5 2.0 %copy.8 = bf16[1,512,4,512]{3,1,2,0:T(8,128)(2,1)S(1)} copy(bf16[1,512,4,512]{3,2,1,0:T(4,128)(2,1)} %param.4) | data formatting | bytes 4194304 | tf_op args[0]
  8.5 1.3 fusion.8
  9.8 3.8 %collective-permute-start.6 = (bf16[4,64,512]{2,1,0:T(8,128)(2,1)S(1)}, bf16[4,64,512]{2,1,0:T(8,128)(2,1)S(1)}, u32[]{:S(2)}, u32[]{:S(2)}) collective-permute-start(bf16[4,64,512]{2,1,0:T(8,128)(2,1)S(1)} %get-tuple-element.29), channel_id=1, source_target_pairs={{0,32},{8,40},{16,48},{24,56},{1,33},{9,41},{17,49},{25,57},{2,34}... | collective-permute-start | bytes 786440 | tf_op jit(solution)/shard_map/ppermute | solution.py:208
  13.6 4.6 %collective-permute-start = (bf16[4,64,512]{2,1,0:T(8,128)(2,1)S(1)}, bf16[4,64,512]{2,1,0:T(8,128)(2,1)S(1)}, u32[]{:S(2)}, u32[]{:S(2)}) collective-permute-start(bf16[4,64,512]{2,1,0:T(8,128)(2,1)S(1)} %get-tuple-element.35), channel_id=1, source_target_pairs={{0,224},{8,232},{16,240},{24,248},{1,225},{9,233},{17,241},{25,249... | collective-permute-start | bytes 786440 | tf_op jit(solution)/shard_map/ppermute | solution.py:208
  18.3 2.0 %collective-permute-start.1 = (bf16[4,64,512]{2,1,0:T(8,128)(2,1)}, bf16[4,64,512]{2,1,0:T(8,128)(2,1)}, u32[]{:S(2)}, u32[]{:S(2)}) collective-permute-start(bf16[4,64,512]{2,1,0:T(8,128)(2,1)} %get-tuple-element.34), channel_id=1, source_target_pairs={{0,64},{8,72},{16,80},{24,88},{1,65},{9,73},{17,81},{25,89},{2,66}... | collective-permute-start | bytes 786440 | tf_op jit(solution)/shard_map/ppermute | solution.py:208
  20.2 2.0 %collective-permute-start.2 = (bf16[4,64,512]{2,1,0:T(8,128)(2,1)}, bf16[4,64,512]{2,1,0:T(8,128)(2,1)}, u32[]{:S(2)}, u32[]{:S(2)}) collective-permute-start(bf16[4,64,512]{2,1,0:T(8,128)(2,1)} %get-tuple-element.33), channel_id=1, source_target_pairs={{0,192},{8,200},{16,208},{24,216},{1,193},{9,201},{17,209},{25,217... | collective-permute-start | bytes 786440 | tf_op jit(solution)/shard_map/ppermute | solution.py:208
  22.3 2.0 %collective-permute-start.3 = (bf16[4,64,512]{2,1,0:T(8,128)(2,1)}, bf16[4,64,512]{2,1,0:T(8,128)(2,1)}, u32[]{:S(2)}, u32[]{:S(2)}) collective-permute-start(bf16[4,64,512]{2,1,0:T(8,128)(2,1)} %get-tuple-element.32), channel_id=1, source_target_pairs={{0,96},{8,104},{16,112},{24,120},{1,97},{9,105},{17,113},{25,121},... | collective-permute-start | bytes 786440 | tf_op jit(solution)/shard_map/ppermute | solution.py:208
  24.2 0.0 collective-permute-done.6
  24.2 2.0 %collective-permute-start.4 = (bf16[4,64,512]{2,1,0:T(8,128)(2,1)}, bf16[4,64,512]{2,1,0:T(8,128)(2,1)}, u32[]{:S(2)}, u32[]{:S(2)}) collective-permute-start(bf16[4,64,512]{2,1,0:T(8,128)(2,1)} %get-tuple-element.31), channel_id=1, source_target_pairs={{0,160},{8,168},{16,176},{24,184},{1,161},{9,169},{17,177},{25,185... | collective-permute-start | bytes 786440 | tf_op jit(solution)/shard_map/ppermute | solution.py:208
  26.2 0.0 collective-permute-done
  26.2 2.0 %collective-permute-start.5 = (bf16[4,64,512]{2,1,0:T(8,128)(2,1)S(1)}, bf16[4,64,512]{2,1,0:T(8,128)(2,1)}, u32[]{:S(2)}, u32[]{:S(2)}) collective-permute-start(bf16[4,64,512]{2,1,0:T(8,128)(2,1)S(1)} %get-tuple-element.30), channel_id=1, source_target_pairs={{0,128},{8,136},{16,144},{24,152},{1,129},{9,137},{17,145},{25,153... | collective-permute-start | bytes 786440 | tf_op jit(solution)/shard_map/ppermute | solution.py:208
  28.2 0.1 fusion.7
  28.3 0.0 collective-permute-done.1
  28.3 2.3 %collective-permute-done.2 = bf16[4,64,512]{2,1,0:T(8,128)(2,1)} collective-permute-done((bf16[4,64,512]{2,1,0:T(8,128)(2,1)}, bf16[4,64,512]{2,1,0:T(8,128)(2,1)}, u32[]{:S(2)}, u32[]{:S(2)}) %collective-permute-start.2) | collective-permute-done | bytes 262176 | tf_op jit(solution)/shard_map/ppermute | solution.py:208
  30.7 1.5 collective-permute-done.3
  32.2 2.9 %collective-permute-done.4 = bf16[4,64,512]{2,1,0:T(8,128)(2,1)} collective-permute-done((bf16[4,64,512]{2,1,0:T(8,128)(2,1)}, bf16[4,64,512]{2,1,0:T(8,128)(2,1)}, u32[]{:S(2)}, u32[]{:S(2)}) %collective-permute-start.4) | collective-permute-done | bytes 262176 | tf_op jit(solution)/shard_map/ppermute | solution.py:208
  35.1 1.4 collective-permute-done.5
  36.6 0.8 fusion.5
  37.4 0.0 all-gather.3.cloned.1.call-update
  37.4 0.8 slice_bitcast_fusion
  38.2 1.3 collective-permute-start.7
  39.5 0.7 collective-permute-start.8
  40.2 3.3 %collective-permute-start.12 = (bf16[512,512]{1,0:T(8,128)(2,1)S(1)}, bf16[512,512]{1,0:T(8,128)(2,1)S(1)}, u32[]{:S(2)}, u32[]{:S(2)}) collective-permute-start(bf16[512,512]{1,0:T(8,128)(2,1)S(1)} %get-tuple-element.17), channel_id=1, source_target_pairs={{0,6},{1,7},{2,0},{3,1},{4,2},{5,3},{6,4},{7,5},{8,14},{9,15},{10,... | collective-permute-start | bytes 1572872 | tf_op jit(solution)/shard_map/ppermute | solution.py:27
  43.5 0.0 collective-permute-start.13
  43.5 0.5 collective-permute-done.7
  44.0 2.8 %collective-permute-start.9 = (bf16[32,512]{1,0:T(8,128)(2,1)S(1)}, bf16[32,512]{1,0:T(8,128)(2,1)S(1)}, u32[]{:S(2)}, u32[]{:S(2)}) collective-permute-start(bf16[32,512]{1,0:T(8,128)(2,1)S(1)} %broadcast_select_fusion), channel_id=1, source_target_pairs={{0,24},{8,0},{16,8},{24,16},{32,56},{40,32},{48,40},{56,48},{64,88... | collective-permute-start | bytes 98312 | tf_op jit(solution)/shard_map/ppermute | solution.py:25
  46.8 1.6 collective-permute-done.9
  48.4 3.5 %collective-permute-start.10 = (bf16[32,512]{1,0:T(8,128)(2,1)S(1)}, bf16[32,512]{1,0:T(8,128)(2,1)S(1)}, u32[]{:S(2)}, u32[]{:S(2)}) collective-permute-start(bf16[32,512]{1,0:T(8,128)(2,1)S(1)} %collective-permute-done.9), channel_id=1, source_target_pairs={{0,24},{8,0},{16,8},{24,16},{32,56},{40,32},{48,40},{56,48},{64,88... | collective-permute-start | bytes 98312 | tf_op jit(solution)/shard_map/ppermute | solution.py:25
  52.0 0.2 collective-permute-done.11
  52.2 1.4 collective-permute-done.10
  53.6 1.8 %collective-permute-done.12 = bf16[512,512]{1,0:T(8,128)(2,1)S(1)} collective-permute-done((bf16[512,512]{1,0:T(8,128)(2,1)S(1)}, bf16[512,512]{1,0:T(8,128)(2,1)S(1)}, u32[]{:S(2)}, u32[]{:S(2)}) %collective-permute-start.12) | collective-permute-done | bytes 524320 | tf_op jit(solution)/shard_map/ppermute | solution.py:27
  55.4 2.7 %collective-permute-done.13 = bf16[512,512]{1,0:T(8,128)(2,1)S(1)} collective-permute-done((bf16[512,512]{1,0:T(8,128)(2,1)S(1)}, bf16[512,512]{1,0:T(8,128)(2,1)S(1)}, u32[]{:S(2)}, u32[]{:S(2)}) %collective-permute-start.13) | collective-permute-done | bytes 524320 | tf_op jit(solution)/shard_map/ppermute | solution.py:27
  58.1 0.1 collective-permute-start.24
  58.2 2.1 %collective-permute-start.25 = (bf16[256,512]{1,0:T(8,128)(2,1)S(1)}, bf16[256,512]{1,0:T(8,128)(2,1)S(1)}, u32[]{:S(2)}, u32[]{:S(2)}) collective-permute-start(bf16[256,512]{1,0:T(8,128)(2,1)S(1)} %slice.66), channel_id=1, source_target_pairs={{0,6},{1,7},{2,0},{3,1},{4,2},{5,3},{6,4},{7,5},{8,14},{9,15},{10,... | collective-permute-start | bytes 786440 | tf_op jit(solution)/shard_map/ppermute | solution.py:27
  60.3 3.2 %collective-permute-start.18 = (bf16[3,32,512]{2,1,0:T(8,128)(2,1)S(1)}, bf16[3,32,512]{2,1,0:T(8,128)(2,1)S(1)}, u32[]{:S(2)}, u32[]{:S(2)}) collective-permute-start(bf16[3,32,512]{2,1,0:T(8,128)(2,1)S(1)} %pad_maximum_fusion.1), channel_id=1, source_target_pairs={{0,224},{8,232},{16,240},{24,248},{32,0},{40,8},{48,16},{56,24},{6... | collective-permute-start | bytes 294920 | tf_op jit(solution)/shard_map/ppermute | solution.py:23
  63.6 4.0 %collective-permute-done.14 = bf16[3,32,512]{2,1,0:T(8,128)(2,1)S(1)} collective-permute-done((bf16[3,32,512]{2,1,0:T(8,128)(2,1)S(1)}, bf16[3,32,512]{2,1,0:T(8,128)(2,1)S(1)}, u32[]{:S(2)}, u32[]{:S(2)}) %collective-permute-start.14) | collective-permute-done | bytes 98336 | tf_op jit(solution)/shard_map/ppermute | solution.py:23
  67.6 0.0 collective-permute-start.15
  67.6 3.2 %collective-permute-start.19 = (bf16[3,32,512]{2,1,0:T(8,128)(2,1)S(1)}, bf16[3,32,512]{2,1,0:T(8,128)(2,1)S(1)}, u32[]{:S(2)}, u32[]{:S(2)}) collective-permute-start(bf16[3,32,512]{2,1,0:T(8,128)(2,1)S(1)} %collective-permute-done.18), channel_id=1, source_target_pairs={{0,224},{8,232},{16,240},{24,248},{32,0},{40,8},{48,16},{56,24},{6... | collective-permute-start | bytes 294920 | tf_op jit(solution)/shard_map/ppermute | solution.py:23
  70.9 0.3 pad_maximum_fusion.refs_8_
  71.2 0.0 copy-start.1
  71.2 0.1 collective-permute-start.26
  71.3 3.1 %collective-permute-done.15 = bf16[3,32,512]{2,1,0:T(8,128)(2,1)S(1)} collective-permute-done((bf16[3,32,512]{2,1,0:T(8,128)(2,1)S(1)}, bf16[3,32,512]{2,1,0:T(8,128)(2,1)S(1)}, u32[]{:S(2)}, u32[]{:S(2)}) %collective-permute-start.15) | collective-permute-done | bytes 98336 | tf_op jit(solution)/shard_map/ppermute | solution.py:23
  74.4 3.2 %collective-permute-start.20 = (bf16[3,32,512]{2,1,0:T(8,128)(2,1)S(1)}, bf16[3,32,512]{2,1,0:T(8,128)(2,1)S(1)}, u32[]{:S(2)}, u32[]{:S(2)}) collective-permute-start(bf16[3,32,512]{2,1,0:T(8,128)(2,1)S(1)} %collective-permute-done.19), channel_id=1, source_target_pairs={{0,224},{8,232},{16,240},{24,248},{32,0},{40,8},{48,16},{56,24},{6... | collective-permute-start | bytes 294920 | tf_op jit(solution)/shard_map/ppermute | solution.py:23
  77.6 2.8 %collective-permute-done.16 = bf16[3,32,512]{2,1,0:T(8,128)(2,1)S(1)} collective-permute-done((bf16[3,32,512]{2,1,0:T(8,128)(2,1)S(1)}, bf16[3,32,512]{2,1,0:T(8,128)(2,1)S(1)}, u32[]{:S(2)}, u32[]{:S(2)}) %collective-permute-start.16) | collective-permute-done | bytes 98336 | tf_op jit(solution)/shard_map/ppermute | solution.py:23
  80.4 3.3 %collective-permute-start.21 = (bf16[3,16,512]{2,1,0:T(8,128)(2,1)S(1)}, bf16[3,16,512]{2,1,0:T(8,128)(2,1)S(1)}, u32[]{:S(2)}, u32[]{:S(2)}) collective-permute-start(bf16[3,16,512]{2,1,0:T(8,128)(2,1)S(1)} %slice.81), channel_id=1, source_target_pairs={{0,224},{8,232},{16,240},{24,248},{32,0},{40,8},{48,16},{56,24},{6... | collective-permute-start | bytes 147464 | tf_op jit(solution)/shard_map/ppermute | solution.py:23
  83.7 2.0 %collective-permute-done.17 = bf16[3,16,512]{2,1,0:T(8,128)(2,1)S(1)} collective-permute-done((bf16[3,16,512]{2,1,0:T(8,128)(2,1)S(1)}, bf16[3,16,512]{2,1,0:T(8,128)(2,1)S(1)}, u32[]{:S(2)}, u32[]{:S(2)}) %collective-permute-start.17) | collective-permute-done | bytes 49184 | tf_op jit(solution)/shard_map/ppermute | solution.py:23
  85.7 0.2 collective-permute-done.21
  86.0 1.2 collective-permute-start.22
  87.1 1.2 collective-permute-start.23
  88.3 16.1 %collective-permute-done.22.refs_1_ = bf16[8,3,32,512]{3,2,1,0:T(8,128)(2,1)S(1)} collective-permute-done((bf16[8,3,32,512]{3,2,1,0:T(8,128)(2,1)S(1)}, bf16[8,3,32,512]{3,2,1,0:T(8,128)(2,1)S(1)}, u32[]{:S(2)}, u32[]{:S(2)}) %collective-permute-start.22) | collective-permute-done | bytes 786464 | tf_op jit(solution)/shard_map/ppermute | solution.py:27
  104.5 0.4 collective-permute-done.23.refs_3_
  104.9 2.7 %collective-permute-start.27 = (bf16[4,3,32,512]{3,2,1,0:T(8,128)(2,1)S(1)}, bf16[4,3,32,512]{3,2,1,0:T(8,128)(2,1)S(1)}, u32[]{:S(2)}, u32[]{:S(2)}) collective-permute-start(bf16[4,3,32,512]{3,2,1,0:T(8,128)(2,1)S(1)} %slice.67), channel_id=1, source_target_pairs={{0,2},{1,3},{2,4},{3,5},{4,6},{5,7},{6,0},{7,1},{8,10},{9,11},{10,... | collective-permute-start | bytes 1179656 | tf_op jit(solution)/shard_map/ppermute | solution.py:27
  107.6 0.1 collective-permute-start.28
  107.7 0.1 collective-permute-start.29
  107.8 0.5 collective-permute-start.30
  108.3 0.1 collective-permute-start.32
  108.4 5.4 %collective-permute-done.27 = bf16[4,3,32,512]{3,2,1,0:T(8,128)(2,1)S(1)} collective-permute-done((bf16[4,3,32,512]{3,2,1,0:T(8,128)(2,1)S(1)}, bf16[4,3,32,512]{3,2,1,0:T(8,128)(2,1)S(1)}, u32[]{:S(2)}, u32[]{:S(2)}) %collective-permute-start.27) | collective-permute-done | bytes 393248 | tf_op jit(solution)/shard_map/ppermute | solution.py:27
  113.8 3.2 %collective-permute-done.28 = bf16[4,3,32,512]{3,2,1,0:T(8,128)(2,1)S(1)} collective-permute-done((bf16[4,3,32,512]{3,2,1,0:T(8,128)(2,1)S(1)}, bf16[4,3,32,512]{3,2,1,0:T(8,128)(2,1)S(1)}, u32[]{:S(2)}, u32[]{:S(2)}) %collective-permute-start.28) | collective-permute-done | bytes 393248 | tf_op jit(solution)/shard_map/ppermute | solution.py:27
  117.1 0.1 collective-permute-start.31
  117.2 0.7 pad_add_fusion.ids
  117.9 1.6 collective-permute-done.31.refs_6_
  119.6 10.8 %shard_map.46 = (bf16[3,512,1536]{2,1,0:T(8,128)(2,1)}, bf16[512,2048]{1,0:T(8,128)(2,1)}) custom-call(s32[2]{0:T(128)} %pad_add_fusion.ids, s32[32,32]{1,0:T(8,128)} %shape.3, bf16[8,3,32,512]{3,2,1,0:T(8,128)(2,1)} %copy-done.7, bf16[8,3,32,512]{3,2,1,0:T(8,128)(2,1)} %copy-done.4, bf16[8,3,32,512]{3,2,1,0:T(8,128)(2,1)} %copy-done.6, ...), custom_call_target="tpu_custom_call" | custom-call | flops 8053063680 | bytes 18874368 | tf_op jit(solution)/shard_map/pallas_call | solution.py:157
  130.4 9.1 %all-gather.3.cloned.1.call-done = bf16[128,64,512]{2,1,0:T(8,128)(2,1)} async-done(((bf16[4,64,512]{2,1,0:T(8,128)(2,1)}), bf16[128,64,512]{2,1,0:T(8,128)(2,1)}) %all-gather.3.cloned.1.call-update) | async-done | bytes 8388624 | tf_op jit(solution)/shard_map/all_gather | solution.py:214
  139.5 19.5 %shard_map.47 = f32[512,4,512]{2,1,0:T(4,128)} custom-call(s32[2]{0:T(128)} %pad_add_fusion.ids, s32[32,32]{1,0:T(8,128)} %shape.3, bf16[32,4,64,512]{3,2,1,0:T(8,128)(2,1)} %bitcast.49, bf16[4,512,512]{2,1,0:T(8,128)(2,1)} %bitcast.46, bf16[3,512,1536]{2,1,0:T(8,128)(2,1)} %get-tuple-element.25.low, bf16[512,2048]{1,0:T(8,128)(2,1)} %get-tuple-element.26.left, ...), custom_call_target="tpu_custom_call" | custom-call | flops 15032385536 | bytes 25165824 | tf_op jit(solution)/shard_map/pallas_call | solution.py:175
  (58 shorter events, 0.4 us)
Async XLA Ops:
  6.5 133.0 %all-gather.3.cloned.1.call-start = ((), (), s32[]{:S(2)}) async-start(), calls=%async_computation | async-start | bytes 8650752 | tf_op jit(solution)/shard_map/all_gather | solution.py:214
  8.5 28.0 %copy-start = (bf16[1,512,4,512]{3,1,2,0:T(8,128)(2,1)}, bf16[1,512,4,512]{3,1,2,0:T(8,128)(2,1)S(1)}, u32[]{:S(2)}) copy-start(bf16[1,512,4,512]{3,1,2,0:T(8,128)(2,1)S(1)} %copy.8) | copy-start | bytes 6291460
  9.8 14.4 %collective-permute-start.6 = (bf16[4,64,512]{2,1,0:T(8,128)(2,1)S(1)}, bf16[4,64,512]{2,1,0:T(8,128)(2,1)S(1)}, u32[]{:S(2)}, u32[]{:S(2)}) collective-permute-start(bf16[4,64,512]{2,1,0:T(8,128)(2,1)S(1)} %get-tuple-element.29), channel_id=1, source_target_pairs={{0,32},{8,40},{16,48},{24,56},{1,33},{9,41},{17,49},{25,57},{2,34}... | collective-permute-start | bytes 786440 | tf_op jit(solution)/shard_map/ppermute | solution.py:208
  13.6 12.6 %collective-permute-start = (bf16[4,64,512]{2,1,0:T(8,128)(2,1)S(1)}, bf16[4,64,512]{2,1,0:T(8,128)(2,1)S(1)}, u32[]{:S(2)}, u32[]{:S(2)}) collective-permute-start(bf16[4,64,512]{2,1,0:T(8,128)(2,1)S(1)} %get-tuple-element.35), channel_id=1, source_target_pairs={{0,224},{8,232},{16,240},{24,248},{1,225},{9,233},{17,241},{25,249... | collective-permute-start | bytes 786440 | tf_op jit(solution)/shard_map/ppermute | solution.py:208
  18.3 10.0 %collective-permute-start.1 = (bf16[4,64,512]{2,1,0:T(8,128)(2,1)}, bf16[4,64,512]{2,1,0:T(8,128)(2,1)}, u32[]{:S(2)}, u32[]{:S(2)}) collective-permute-start(bf16[4,64,512]{2,1,0:T(8,128)(2,1)} %get-tuple-element.34), channel_id=1, source_target_pairs={{0,64},{8,72},{16,80},{24,88},{1,65},{9,73},{17,81},{25,89},{2,66}... | collective-permute-start | bytes 786440 | tf_op jit(solution)/shard_map/ppermute | solution.py:208
  20.2 10.4 %collective-permute-start.2 = (bf16[4,64,512]{2,1,0:T(8,128)(2,1)}, bf16[4,64,512]{2,1,0:T(8,128)(2,1)}, u32[]{:S(2)}, u32[]{:S(2)}) collective-permute-start(bf16[4,64,512]{2,1,0:T(8,128)(2,1)} %get-tuple-element.33), channel_id=1, source_target_pairs={{0,192},{8,200},{16,208},{24,216},{1,193},{9,201},{17,209},{25,217... | collective-permute-start | bytes 786440 | tf_op jit(solution)/shard_map/ppermute | solution.py:208
  22.3 9.9 %collective-permute-start.3 = (bf16[4,64,512]{2,1,0:T(8,128)(2,1)}, bf16[4,64,512]{2,1,0:T(8,128)(2,1)}, u32[]{:S(2)}, u32[]{:S(2)}) collective-permute-start(bf16[4,64,512]{2,1,0:T(8,128)(2,1)} %get-tuple-element.32), channel_id=1, source_target_pairs={{0,96},{8,104},{16,112},{24,120},{1,97},{9,105},{17,113},{25,121},... | collective-permute-start | bytes 786440 | tf_op jit(solution)/shard_map/ppermute | solution.py:208
  24.2 4.0 %copy-start.2 = (bf16[4,64,512]{2,1,0:T(8,128)(2,1)}, bf16[4,64,512]{2,1,0:T(8,128)(2,1)S(1)}, u32[]{:S(2)}) copy-start(bf16[4,64,512]{2,1,0:T(8,128)(2,1)S(1)} %collective-permute-done.6) | copy-start | bytes 786436
  24.2 10.9 %collective-permute-start.4 = (bf16[4,64,512]{2,1,0:T(8,128)(2,1)}, bf16[4,64,512]{2,1,0:T(8,128)(2,1)}, u32[]{:S(2)}, u32[]{:S(2)}) collective-permute-start(bf16[4,64,512]{2,1,0:T(8,128)(2,1)} %get-tuple-element.31), channel_id=1, source_target_pairs={{0,160},{8,168},{16,176},{24,184},{1,161},{9,169},{17,177},{25,185... | collective-permute-start | bytes 786440 | tf_op jit(solution)/shard_map/ppermute | solution.py:208
  26.2 2.0 %copy-start.3 = (bf16[4,64,512]{2,1,0:T(8,128)(2,1)}, bf16[4,64,512]{2,1,0:T(8,128)(2,1)S(1)}, u32[]{:S(2)}) copy-start(bf16[4,64,512]{2,1,0:T(8,128)(2,1)S(1)} %collective-permute-done) | copy-start | bytes 786436
  26.2 10.3 %collective-permute-start.5 = (bf16[4,64,512]{2,1,0:T(8,128)(2,1)S(1)}, bf16[4,64,512]{2,1,0:T(8,128)(2,1)}, u32[]{:S(2)}, u32[]{:S(2)}) collective-permute-start(bf16[4,64,512]{2,1,0:T(8,128)(2,1)S(1)} %get-tuple-element.30), channel_id=1, source_target_pairs={{0,128},{8,136},{16,144},{24,152},{1,129},{9,137},{17,145},{25,153... | collective-permute-start | bytes 786440 | tf_op jit(solution)/shard_map/ppermute | solution.py:208
  38.2 5.8 %collective-permute-start.7 = (bf16[32,512]{1,0:T(8,128)(2,1)S(1)}, bf16[32,512]{1,0:T(8,128)(2,1)S(1)}, u32[]{:S(2)}, u32[]{:S(2)}) collective-permute-start(bf16[32,512]{1,0:T(8,128)(2,1)S(1)} %get-tuple-element.37), channel_id=1, source_target_pairs={{0,0},{1,2},{2,4},{3,6},{8,8},{9,10},{10,12},{11,14},{16,16},{17,1... | collective-permute-start | bytes 98312 | tf_op jit(solution)/shard_map/ppermute | solution.py:216
  39.5 4.5 %collective-permute-start.8 = (bf16[32,512]{1,0:T(8,128)(2,1)S(1)}, bf16[32,512]{1,0:T(8,128)(2,1)S(1)}, u32[]{:S(2)}, u32[]{:S(2)}) collective-permute-start(bf16[32,512]{1,0:T(8,128)(2,1)S(1)} %get-tuple-element.36), channel_id=1, source_target_pairs={{0,1},{1,3},{2,5},{3,7},{8,9},{9,11},{10,13},{11,15},{16,17},{17,1... | collective-permute-start | bytes 98312 | tf_op jit(solution)/shard_map/ppermute | solution.py:217
  40.2 15.2 %collective-permute-start.12 = (bf16[512,512]{1,0:T(8,128)(2,1)S(1)}, bf16[512,512]{1,0:T(8,128)(2,1)S(1)}, u32[]{:S(2)}, u32[]{:S(2)}) collective-permute-start(bf16[512,512]{1,0:T(8,128)(2,1)S(1)} %get-tuple-element.17), channel_id=1, source_target_pairs={{0,6},{1,7},{2,0},{3,1},{4,2},{5,3},{6,4},{7,5},{8,14},{9,15},{10,... | collective-permute-start | bytes 1572872 | tf_op jit(solution)/shard_map/ppermute | solution.py:27
  43.5 14.6 %collective-permute-start.13 = (bf16[512,512]{1,0:T(8,128)(2,1)S(1)}, bf16[512,512]{1,0:T(8,128)(2,1)S(1)}, u32[]{:S(2)}, u32[]{:S(2)}) collective-permute-start(bf16[512,512]{1,0:T(8,128)(2,1)S(1)} %get-tuple-element.17), channel_id=1, source_target_pairs={{0,2},{1,3},{2,4},{3,5},{4,6},{5,7},{6,0},{7,1},{8,10},{9,11},{10,... | collective-permute-start | bytes 1572872 | tf_op jit(solution)/shard_map/ppermute | solution.py:27
  44.0 4.4 %collective-permute-start.9 = (bf16[32,512]{1,0:T(8,128)(2,1)S(1)}, bf16[32,512]{1,0:T(8,128)(2,1)S(1)}, u32[]{:S(2)}, u32[]{:S(2)}) collective-permute-start(bf16[32,512]{1,0:T(8,128)(2,1)S(1)} %broadcast_select_fusion), channel_id=1, source_target_pairs={{0,24},{8,0},{16,8},{24,16},{32,56},{40,32},{48,40},{56,48},{64,88... | collective-permute-start | bytes 98312 | tf_op jit(solution)/shard_map/ppermute | solution.py:25
  46.8 5.3 %collective-permute-start.11 = (bf16[32,512]{1,0:T(8,128)(2,1)S(1)}, bf16[32,512]{1,0:T(8,128)(2,1)S(1)}, u32[]{:S(2)}, u32[]{:S(2)}) collective-permute-start(bf16[32,512]{1,0:T(8,128)(2,1)S(1)} %broadcast_select_fusion), channel_id=1, source_target_pairs={{0,8},{8,16},{16,24},{24,0},{32,40},{40,48},{48,56},{56,32},{64,72... | collective-permute-start | bytes 98312 | tf_op jit(solution)/shard_map/ppermute | solution.py:25
  48.4 5.1 %collective-permute-start.10 = (bf16[32,512]{1,0:T(8,128)(2,1)S(1)}, bf16[32,512]{1,0:T(8,128)(2,1)S(1)}, u32[]{:S(2)}, u32[]{:S(2)}) collective-permute-start(bf16[32,512]{1,0:T(8,128)(2,1)S(1)} %collective-permute-done.9), channel_id=1, source_target_pairs={{0,24},{8,0},{16,8},{24,16},{32,56},{40,32},{48,40},{56,48},{64,88... | collective-permute-start | bytes 98312 | tf_op jit(solution)/shard_map/ppermute | solution.py:25
  58.1 12.7 %collective-permute-start.24 = (bf16[256,512]{1,0:T(8,128)(2,1)S(1)}, bf16[256,512]{1,0:T(8,128)(2,1)S(1)}, u32[]{:S(2)}, u32[]{:S(2)}) collective-permute-start(bf16[256,512]{1,0:T(8,128)(2,1)S(1)} %slice.65), channel_id=1, source_target_pairs={{0,2},{1,3},{2,4},{3,5},{4,6},{5,7},{6,0},{7,1},{8,10},{9,11},{10,... | collective-permute-start | bytes 786440 | tf_op jit(solution)/shard_map/ppermute | solution.py:27
  58.2 12.6 %collective-permute-start.25 = (bf16[256,512]{1,0:T(8,128)(2,1)S(1)}, bf16[256,512]{1,0:T(8,128)(2,1)S(1)}, u32[]{:S(2)}, u32[]{:S(2)}) collective-permute-start(bf16[256,512]{1,0:T(8,128)(2,1)S(1)} %slice.66), channel_id=1, source_target_pairs={{0,6},{1,7},{2,0},{3,1},{4,2},{5,3},{6,4},{7,5},{8,14},{9,15},{10,... | collective-permute-start | bytes 786440 | tf_op jit(solution)/shard_map/ppermute | solution.py:27
  60.3 7.3 %collective-permute-start.14 = (bf16[3,32,512]{2,1,0:T(8,128)(2,1)S(1)}, bf16[3,32,512]{2,1,0:T(8,128)(2,1)S(1)}, u32[]{:S(2)}, u32[]{:S(2)}) collective-permute-start(bf16[3,32,512]{2,1,0:T(8,128)(2,1)S(1)} %pad_maximum_fusion.1), channel_id=1, source_target_pairs={{0,32},{8,40},{16,48},{24,56},{32,64},{40,72},{48,80},{56,88},{64,... | collective-permute-start | bytes 294920 | tf_op jit(solution)/shard_map/ppermute | solution.py:23
  60.3 7.3 %collective-permute-start.18 = (bf16[3,32,512]{2,1,0:T(8,128)(2,1)S(1)}, bf16[3,32,512]{2,1,0:T(8,128)(2,1)S(1)}, u32[]{:S(2)}, u32[]{:S(2)}) collective-permute-start(bf16[3,32,512]{2,1,0:T(8,128)(2,1)S(1)} %pad_maximum_fusion.1), channel_id=1, source_target_pairs={{0,224},{8,232},{16,240},{24,248},{32,0},{40,8},{48,16},{56,24},{6... | collective-permute-start | bytes 294920 | tf_op jit(solution)/shard_map/ppermute | solution.py:23
  67.6 6.8 %collective-permute-start.15 = (bf16[3,32,512]{2,1,0:T(8,128)(2,1)S(1)}, bf16[3,32,512]{2,1,0:T(8,128)(2,1)S(1)}, u32[]{:S(2)}, u32[]{:S(2)}) collective-permute-start(bf16[3,32,512]{2,1,0:T(8,128)(2,1)S(1)} %collective-permute-done.14), channel_id=1, source_target_pairs={{0,32},{8,40},{16,48},{24,56},{32,64},{40,72},{48,80},{56,88},{64,... | collective-permute-start | bytes 294920 | tf_op jit(solution)/shard_map/ppermute | solution.py:23
  67.6 6.8 %collective-permute-start.19 = (bf16[3,32,512]{2,1,0:T(8,128)(2,1)S(1)}, bf16[3,32,512]{2,1,0:T(8,128)(2,1)S(1)}, u32[]{:S(2)}, u32[]{:S(2)}) collective-permute-start(bf16[3,32,512]{2,1,0:T(8,128)(2,1)S(1)} %collective-permute-done.18), channel_id=1, source_target_pairs={{0,224},{8,232},{16,240},{24,248},{32,0},{40,8},{48,16},{56,24},{6... | collective-permute-start | bytes 294920 | tf_op jit(solution)/shard_map/ppermute | solution.py:23
  71.2 45.9 %copy-start.1 = (bf16[4,512,512]{2,1,0:T(8,128)(2,1)}, bf16[4,512,512]{2,1,0:T(8,128)(2,1)S(1)}, u32[]{:S(2)}) copy-start(bf16[4,512,512]{2,1,0:T(8,128)(2,1)S(1)} %pad_maximum_fusion.refs_8_) | copy-start | bytes 6291460
  71.2 33.7 %collective-permute-start.26 = (bf16[4,512,512]{2,1,0:T(8,128)(2,1)S(1)}, bf16[4,512,512]{2,1,0:T(8,128)(2,1)S(1)}, u32[]{:S(2)}, u32[]{:S(2)}) collective-permute-start(bf16[4,512,512]{2,1,0:T(8,128)(2,1)S(1)} %pad_maximum_fusion.refs_8_), channel_id=1, source_target_pairs={{0,1},{1,0},{2,3},{3,2},{4,5},{5,4},{6,7},{7,6},{8,9},{9,8},{10,11... | collective-permute-start | bytes 6291464 | tf_op jit(solution)/shard_map/ppermute | solution.py:28
  74.4 6.0 %collective-permute-start.16 = (bf16[3,32,512]{2,1,0:T(8,128)(2,1)S(1)}, bf16[3,32,512]{2,1,0:T(8,128)(2,1)S(1)}, u32[]{:S(2)}, u32[]{:S(2)}) collective-permute-start(bf16[3,32,512]{2,1,0:T(8,128)(2,1)S(1)} %collective-permute-done.15), channel_id=1, source_target_pairs={{0,32},{8,40},{16,48},{24,56},{32,64},{40,72},{48,80},{56,88},{64,... | collective-permute-start | bytes 294920 | tf_op jit(solution)/shard_map/ppermute | solution.py:23
  74.4 6.0 %collective-permute-start.20 = (bf16[3,32,512]{2,1,0:T(8,128)(2,1)S(1)}, bf16[3,32,512]{2,1,0:T(8,128)(2,1)S(1)}, u32[]{:S(2)}, u32[]{:S(2)}) collective-permute-start(bf16[3,32,512]{2,1,0:T(8,128)(2,1)S(1)} %collective-permute-done.19), channel_id=1, source_target_pairs={{0,224},{8,232},{16,240},{24,248},{32,0},{40,8},{48,16},{56,24},{6... | collective-permute-start | bytes 294920 | tf_op jit(solution)/shard_map/ppermute | solution.py:23
  80.4 5.3 %collective-permute-start.17 = (bf16[3,16,512]{2,1,0:T(8,128)(2,1)S(1)}, bf16[3,16,512]{2,1,0:T(8,128)(2,1)S(1)}, u32[]{:S(2)}, u32[]{:S(2)}) collective-permute-start(bf16[3,16,512]{2,1,0:T(8,128)(2,1)S(1)} %slice.80), channel_id=1, source_target_pairs={{0,32},{8,40},{16,48},{24,56},{32,64},{40,72},{48,80},{56,88},{64,... | collective-permute-start | bytes 147464 | tf_op jit(solution)/shard_map/ppermute | solution.py:23
  80.4 5.5 %collective-permute-start.21 = (bf16[3,16,512]{2,1,0:T(8,128)(2,1)S(1)}, bf16[3,16,512]{2,1,0:T(8,128)(2,1)S(1)}, u32[]{:S(2)}, u32[]{:S(2)}) collective-permute-start(bf16[3,16,512]{2,1,0:T(8,128)(2,1)S(1)} %slice.81), channel_id=1, source_target_pairs={{0,224},{8,232},{16,240},{24,248},{32,0},{40,8},{48,16},{56,24},{6... | collective-permute-start | bytes 147464 | tf_op jit(solution)/shard_map/ppermute | solution.py:23
  86.0 33.6 %copy-start.7 = (bf16[8,3,32,512]{3,2,1,0:T(8,128)(2,1)}, bf16[8,3,32,512]{3,2,1,0:T(8,128)(2,1)S(1)}, u32[]{:S(2)}) copy-start(bf16[8,3,32,512]{3,2,1,0:T(8,128)(2,1)S(1)} %bitcast_dynamic-update-slice_fusion.refs_0_) | copy-start | bytes 2359300
  86.0 18.5 %collective-permute-start.22 = (bf16[8,3,32,512]{3,2,1,0:T(8,128)(2,1)S(1)}, bf16[8,3,32,512]{3,2,1,0:T(8,128)(2,1)S(1)}, u32[]{:S(2)}, u32[]{:S(2)}) collective-permute-start(bf16[8,3,32,512]{3,2,1,0:T(8,128)(2,1)S(1)} %bitcast_dynamic-update-slice_fusion.refs_0_), channel_id=1, source_target_pairs={{0,6},{1,7},{2,0},{3,1},{4,2},{5,3},{6,4},{7,5},{8,14},{9,15},{10,... | collective-permute-start | bytes 2359304 | tf_op jit(solution)/shard_map/ppermute | solution.py:27
  87.1 17.7 %collective-permute-start.23 = (bf16[8,3,32,512]{3,2,1,0:T(8,128)(2,1)S(1)}, bf16[8,3,32,512]{3,2,1,0:T(8,128)(2,1)S(1)}, u32[]{:S(2)}, u32[]{:S(2)}) collective-permute-start(bf16[8,3,32,512]{3,2,1,0:T(8,128)(2,1)S(1)} %bitcast_dynamic-update-slice_fusion.refs_0_), channel_id=1, source_target_pairs={{0,2},{1,3},{2,4},{3,5},{4,6},{5,7},{6,0},{7,1},{8,10},{9,11},{10,... | collective-permute-start | bytes 2359304 | tf_op jit(solution)/shard_map/ppermute | solution.py:27
  104.5 15.1 %copy-start.4 = (bf16[8,3,32,512]{3,2,1,0:T(8,128)(2,1)}, bf16[8,3,32,512]{3,2,1,0:T(8,128)(2,1)S(1)}, u32[]{:S(2)}) copy-start(bf16[8,3,32,512]{3,2,1,0:T(8,128)(2,1)S(1)} %collective-permute-done.22.refs_1_) | copy-start | bytes 2359300
  104.8 14.7 %copy-start.5 = (bf16[8,3,32,512]{3,2,1,0:T(8,128)(2,1)}, bf16[8,3,32,512]{3,2,1,0:T(8,128)(2,1)S(1)}, u32[]{:S(2)}) copy-start(bf16[8,3,32,512]{3,2,1,0:T(8,128)(2,1)S(1)} %collective-permute-done.23.refs_3_) | copy-start | bytes 2359300
  104.9 14.7 %copy-start.8 = (bf16[4,512,512]{2,1,0:T(8,128)(2,1)}, bf16[4,512,512]{2,1,0:T(8,128)(2,1)S(1)}, u32[]{:S(2)}) copy-start(bf16[4,512,512]{2,1,0:T(8,128)(2,1)S(1)} %collective-permute-done.26.refs_9_) | copy-start | bytes 6291460
  104.9 8.9 %collective-permute-start.27 = (bf16[4,3,32,512]{3,2,1,0:T(8,128)(2,1)S(1)}, bf16[4,3,32,512]{3,2,1,0:T(8,128)(2,1)S(1)}, u32[]{:S(2)}, u32[]{:S(2)}) collective-permute-start(bf16[4,3,32,512]{3,2,1,0:T(8,128)(2,1)S(1)} %slice.67), channel_id=1, source_target_pairs={{0,2},{1,3},{2,4},{3,5},{4,6},{5,7},{6,0},{7,1},{8,10},{9,11},{10,... | collective-permute-start | bytes 1179656 | tf_op jit(solution)/shard_map/ppermute | solution.py:27
  107.6 9.4 %collective-permute-start.28 = (bf16[4,3,32,512]{3,2,1,0:T(8,128)(2,1)S(1)}, bf16[4,3,32,512]{3,2,1,0:T(8,128)(2,1)S(1)}, u32[]{:S(2)}, u32[]{:S(2)}) collective-permute-start(bf16[4,3,32,512]{3,2,1,0:T(8,128)(2,1)S(1)} %slice.68), channel_id=1, source_target_pairs={{0,6},{1,7},{2,0},{3,1},{4,2},{5,3},{6,4},{7,5},{8,14},{9,15},{10,... | collective-permute-start | bytes 1179656 | tf_op jit(solution)/shard_map/ppermute | solution.py:27
  107.7 10.2 %collective-permute-start.29 = (bf16[8,3,32,512]{3,2,1,0:T(8,128)(2,1)S(1)}, bf16[8,3,32,512]{3,2,1,0:T(8,128)(2,1)S(1)}, u32[]{:S(2)}, u32[]{:S(2)}) collective-permute-start(bf16[8,3,32,512]{3,2,1,0:T(8,128)(2,1)S(1)} %bitcast_dynamic-update-slice_fusion.refs_0_), channel_id=1, source_target_pairs={{0,1},{1,0},{2,3},{3,2},{4,5},{5,4},{6,7},{7,6},{8,9},{9,8},{10,11... | collective-permute-start | bytes 2359304 | tf_op jit(solution)/shard_map/ppermute | solution.py:28
  107.8 10.1 %collective-permute-start.30 = (bf16[8,3,32,512]{3,2,1,0:T(8,128)(2,1)S(1)}, bf16[8,3,32,512]{3,2,1,0:T(8,128)(2,1)S(1)}, u32[]{:S(2)}, u32[]{:S(2)}) collective-permute-start(bf16[8,3,32,512]{3,2,1,0:T(8,128)(2,1)S(1)} %collective-permute-done.22.refs_1_), channel_id=1, source_target_pairs={{0,1},{1,0},{2,3},{3,2},{4,5},{5,4},{6,7},{7,6},{8,9},{9,8},{10,11... | collective-permute-start | bytes 2359304 | tf_op jit(solution)/shard_map/ppermute | solution.py:28
  108.3 9.6 %collective-permute-start.32 = (bf16[8,3,32,512]{3,2,1,0:T(8,128)(2,1)S(1)}, bf16[8,3,32,512]{3,2,1,0:T(8,128)(2,1)S(1)}, u32[]{:S(2)}, u32[]{:S(2)}) collective-permute-start(bf16[8,3,32,512]{3,2,1,0:T(8,128)(2,1)S(1)} %collective-permute-done.23.refs_3_), channel_id=1, source_target_pairs={{0,1},{1,0},{2,3},{3,2},{4,5},{5,4},{6,7},{7,6},{8,9},{9,8},{10,11... | collective-permute-start | bytes 2359304 | tf_op jit(solution)/shard_map/ppermute | solution.py:28
  117.0 2.5 %copy-start.6 = (bf16[8,3,32,512]{3,2,1,0:T(8,128)(2,1)}, bf16[8,3,32,512]{3,2,1,0:T(8,128)(2,1)S(1)}, u32[]{:S(2)}) copy-start(bf16[8,3,32,512]{3,2,1,0:T(8,128)(2,1)S(1)} %constant_dynamic-update-slice_fusion.refs_2_) | copy-start | bytes 2359300
  117.1 2.5 %collective-permute-start.31 = (bf16[8,3,32,512]{3,2,1,0:T(8,128)(2,1)S(1)}, bf16[8,3,32,512]{3,2,1,0:T(8,128)(2,1)}, u32[]{:S(2)}, u32[]{:S(2)}) collective-permute-start(bf16[8,3,32,512]{3,2,1,0:T(8,128)(2,1)S(1)} %constant_dynamic-update-slice_fusion.refs_2_), channel_id=1, source_target_pairs={{0,1},{1,0},{2,3},{3,2},{4,5},{5,4},{6,7},{7,6},{8,9},{9,8},{10,11... | collective-permute-start | bytes 2359304 | tf_op jit(solution)/shard_map/ppermute | solution.py:28
  117.9 1.7 %copy-start.9 = (bf16[8,3,32,512]{3,2,1,0:T(8,128)(2,1)}, bf16[8,3,32,512]{3,2,1,0:T(8,128)(2,1)S(1)}, u32[]{:S(2)}) copy-start(bf16[8,3,32,512]{3,2,1,0:T(8,128)(2,1)S(1)} %collective-permute-done.29.refs_4_) | copy-start | bytes 2359300
  117.9 1.7 %copy-start.10 = (bf16[8,3,32,512]{3,2,1,0:T(8,128)(2,1)}, bf16[8,3,32,512]{3,2,1,0:T(8,128)(2,1)S(1)}, u32[]{:S(2)}) copy-start(bf16[8,3,32,512]{3,2,1,0:T(8,128)(2,1)S(1)} %collective-permute-done.30.refs_5_) | copy-start | bytes 2359300
  117.9 1.7 %copy-start.11 = (bf16[8,3,32,512]{3,2,1,0:T(8,128)(2,1)}, bf16[8,3,32,512]{3,2,1,0:T(8,128)(2,1)S(1)}, u32[]{:S(2)}) copy-start(bf16[8,3,32,512]{3,2,1,0:T(8,128)(2,1)S(1)} %collective-permute-done.32.refs_7_) | copy-start | bytes 2359300
Sparse Core Ops, SparseCore 0:
  37.5 101.9 all-gather.2

commit v4 on v3

--- a/solution.py
+++ b/solution.py
@@ -163,7 +163,7 @@
         in_specs=[smem, smem] + [vmem] * 12,
         out_specs=(vmem, vmem),
         scratch_shapes=[pltpu.VMEM((3 * n, 4 * n), HALF)],
-        compiler_params=pltpu.CompilerParams(vmem_limit_bytes=VMEM_LIMIT),
+        compiler_params=pltpu.CompilerParams(vmem_limit_bytes=20 * 1024 * 1024),
         cost_estimate=pl.CostEstimate(flops=60 * n**3, bytes_accessed=18 * 2**20, transcendentals=0),
     )(ids, shape, *corner, *row, v, w)
 
@@ -201,15 +201,16 @@
     own = jnp.transpose(matrix[0], (1, 0, 2))
     ids = jnp.stack([p, q]).astype(jnp.int32)
 
-    piece = own[:, :part]
+    piece = matrix[0, :part]
     came = {}
     for s in (1, 4, 5, 3, 6, 2, 7):
         to = [(i, i + 4 * s) for i in range(4)]
-        came[s] = lax.ppermute(own[:, s * part : (s + 1) * part], "prow", to)
+        came[s] = lax.ppermute(matrix[0, s * part : (s + 1) * part], "prow", to)
     row, came[1] = lax.optimization_barrier((own[0], came[1]))
     row_above, row_below = shift(row, "y-"), shift(row, "y+")
     for s in came:
         piece = jnp.where(z == s, came[s], piece)
+    piece = jnp.transpose(piece, (1, 0, 2))
 
     raw = lax.all_gather(piece, "prow")
 

time: 169 us -> 170 us (level)
  Pallas kernels: 30.3 us -> 26.4 us
  local copies, waits for them, and re-layouts: 4.36 us -> 7.88 us
    pallas_call x1, Pallas kernels: 10.8 us -> 5.87 us  [factor(): pl.pallas_call(factor_kernel, out_shape=(jax.ShapeDtypeStruct((3, n, 3 *...]
    unnamed x32 -> x26, local copies, waits for them, and re-layouts: 2.12 us -> 5.66 us
  transfers between devices with their start and end apart: 34 -> 34, of which waited for: 21 -> 20; matrix products, arithmetic and copies ran while one was open for 1% -> 1% of each run, Pallas kernels for 6% -> 4%
where the time goes in v4:
time: 170 us; the launch traced here: 167 us
  waiting for transfers between devices  65.6 us (39%)
  starting transfers between devices  52 us (31%)
  Pallas kernels  26.4 us (16%)
  between operations  13.7 us (8%)
  local copies, waits for them, and re-layouts  7.88 us (5%)
    ppermute x8, waiting for transfers between devices, shift(): lax.ppermute(block, 'pcol', [(i, (i + 2 * move) % 8) for i in range(8)])  29.8 us
    pallas_call x1, Pallas kernels, columns(): pl.pallas_call(column_kernel, grid=(4,), out_shape=jax.ShapeDtypeStruct((...  20.6 us
    ppermute x7, starting transfers between devices, on_device(): came[s] = lax.ppermute(matrix[0, s * part:(s + 1) * part], 'prow', to)  18.5 us
    ppermute x8, starting transfers between devices, shift(): lax.ppermute(block, 'prow', [(i, (i + 4 * move) % 32) for i in range(32)])  13.2 us
    ppermute x8, waiting for transfers between devices, shift(): lax.ppermute(block, 'prow', [(i, (i + 4 * move) % 32) for i in range(32)])  11.9 us
    ppermute x8, starting transfers between devices, shift(): lax.ppermute(block, 'pcol', [(i, (i + 2 * move) % 8) for i in range(8)])  11.2 us
    all_gather x1, waiting for transfers between devices, on_device(): raw = lax.all_gather(piece, 'prow')  9.91 us
    ppermute x7, waiting for transfers between devices, on_device(): came[s] = lax.ppermute(matrix[0, s * part:(s + 1) * part], 'prow', to)  8.16 us
  transfers between devices with their start and end apart: 34, of which 20 were waited for; matrix products, arithmetic and copies ran while one was open for 1% of the time, Pallas kernels for 4%

profile of v4, /device:TPU:16, one launch (start us, length us, event | category | flops | bytes accessed | tf_op | source)
XLA Modules:
  0.0 166.9 jit_solution(3027569013616767042)
XLA Ops:
  6.5 2.0 %copy.25 = bf16[1,512,4,512]{3,1,2,0:T(8,128)(2,1)S(1)} copy(bf16[1,512,4,512]{3,2,1,0:T(4,128)(2,1)} %param.4) | data formatting | bytes 4194304 | tf_op args[0]
  8.5 1.2 slice_bitcast_fusion.1
  9.8 3.8 %collective-permute-start.6 = (bf16[64,4,512]{2,0,1:T(8,128)(2,1)S(1)}, bf16[64,4,512]{2,0,1:T(8,128)(2,1)S(1)}, u32[]{:S(2)}, u32[]{:S(2)}) collective-permute-start(bf16[64,4,512]{2,0,1:T(8,128)(2,1)S(1)} %get-tuple-element.29), channel_id=1, source_target_pairs={{0,32},{8,40},{16,48},{24,56},{1,33},{9,41},{17,49},{25,57},{2,34}... | collective-permute-start | bytes 786440 | tf_op jit(solution)/shard_map/ppermute | solution.py:208
  13.6 4.6 %collective-permute-start = (bf16[64,4,512]{2,0,1:T(8,128)(2,1)S(1)}, bf16[64,4,512]{2,0,1:T(8,128)(2,1)S(1)}, u32[]{:S(2)}, u32[]{:S(2)}) collective-permute-start(bf16[64,4,512]{2,0,1:T(8,128)(2,1)S(1)} %get-tuple-element.35), channel_id=1, source_target_pairs={{0,224},{8,232},{16,240},{24,248},{1,225},{9,233},{17,241},{25,249... | collective-permute-start | bytes 786440 | tf_op jit(solution)/shard_map/ppermute | solution.py:208
  18.2 2.0 %collective-permute-start.1 = (bf16[64,4,512]{2,0,1:T(8,128)(2,1)}, bf16[64,4,512]{2,0,1:T(8,128)(2,1)}, u32[]{:S(2)}, u32[]{:S(2)}) collective-permute-start(bf16[64,4,512]{2,0,1:T(8,128)(2,1)} %get-tuple-element.34), channel_id=1, source_target_pairs={{0,64},{8,72},{16,80},{24,88},{1,65},{9,73},{17,81},{25,89},{2,66}... | collective-permute-start | bytes 786440 | tf_op jit(solution)/shard_map/ppermute | solution.py:208
  20.2 2.0 %collective-permute-start.2 = (bf16[64,4,512]{2,0,1:T(8,128)(2,1)}, bf16[64,4,512]{2,0,1:T(8,128)(2,1)}, u32[]{:S(2)}, u32[]{:S(2)}) collective-permute-start(bf16[64,4,512]{2,0,1:T(8,128)(2,1)} %get-tuple-element.33), channel_id=1, source_target_pairs={{0,192},{8,200},{16,208},{24,216},{1,193},{9,201},{17,209},{25,217... | collective-permute-start | bytes 786440 | tf_op jit(solution)/shard_map/ppermute | solution.py:208
  22.3 2.0 %collective-permute-start.3 = (bf16[64,4,512]{2,0,1:T(8,128)(2,1)}, bf16[64,4,512]{2,0,1:T(8,128)(2,1)}, u32[]{:S(2)}, u32[]{:S(2)}) collective-permute-start(bf16[64,4,512]{2,0,1:T(8,128)(2,1)} %get-tuple-element.32), channel_id=1, source_target_pairs={{0,96},{8,104},{16,112},{24,120},{1,97},{9,105},{17,113},{25,121},... | collective-permute-start | bytes 786440 | tf_op jit(solution)/shard_map/ppermute | solution.py:208
  24.3 0.0 collective-permute-done.6
  24.3 2.0 %collective-permute-start.4 = (bf16[64,4,512]{2,0,1:T(8,128)(2,1)}, bf16[64,4,512]{2,0,1:T(8,128)(2,1)}, u32[]{:S(2)}, u32[]{:S(2)}) collective-permute-start(bf16[64,4,512]{2,0,1:T(8,128)(2,1)} %get-tuple-element.31), channel_id=1, source_target_pairs={{0,160},{8,168},{16,176},{24,184},{1,161},{9,169},{17,177},{25,185... | collective-permute-start | bytes 786440 | tf_op jit(solution)/shard_map/ppermute | solution.py:208
  26.3 0.0 collective-permute-done
  26.3 2.0 %collective-permute-start.5 = (bf16[64,4,512]{2,0,1:T(8,128)(2,1)S(1)}, bf16[64,4,512]{2,0,1:T(8,128)(2,1)}, u32[]{:S(2)}, u32[]{:S(2)}) collective-permute-start(bf16[64,4,512]{2,0,1:T(8,128)(2,1)S(1)} %get-tuple-element.30), channel_id=1, source_target_pairs={{0,128},{8,136},{16,144},{24,152},{1,129},{9,137},{17,145},{25,153... | collective-permute-start | bytes 786440 | tf_op jit(solution)/shard_map/ppermute | solution.py:208
  28.3 0.1 fusion.9
  28.4 0.0 collective-permute-done.1
  28.4 2.3 %collective-permute-done.2 = bf16[64,4,512]{2,0,1:T(8,128)(2,1)} collective-permute-done((bf16[64,4,512]{2,0,1:T(8,128)(2,1)}, bf16[64,4,512]{2,0,1:T(8,128)(2,1)}, u32[]{:S(2)}, u32[]{:S(2)}) %collective-permute-start.2) | collective-permute-done | bytes 262176 | tf_op jit(solution)/shard_map/ppermute | solution.py:208
  30.6 1.5 collective-permute-done.3
  32.2 2.9 %collective-permute-done.4 = bf16[64,4,512]{2,0,1:T(8,128)(2,1)} collective-permute-done((bf16[64,4,512]{2,0,1:T(8,128)(2,1)}, bf16[64,4,512]{2,0,1:T(8,128)(2,1)}, u32[]{:S(2)}, u32[]{:S(2)}) %collective-permute-start.4) | collective-permute-done | bytes 262176 | tf_op jit(solution)/shard_map/ppermute | solution.py:208
  35.1 1.4 collective-permute-done.5
  36.5 0.8 fusion.7
  37.4 0.0 all-gather.3.cloned.1.call-update
  37.4 0.8 slice_bitcast_fusion.8
  38.2 1.3 collective-permute-start.7
  39.5 0.7 collective-permute-start.8
  40.1 3.3 %collective-permute-start.12 = (bf16[512,512]{1,0:T(8,128)(2,1)S(1)}, bf16[512,512]{1,0:T(8,128)(2,1)S(1)}, u32[]{:S(2)}, u32[]{:S(2)}) collective-permute-start(bf16[512,512]{1,0:T(8,128)(2,1)S(1)} %get-tuple-element.17), channel_id=1, source_target_pairs={{0,6},{1,7},{2,0},{3,1},{4,2},{5,3},{6,4},{7,5},{8,14},{9,15},{10,... | collective-permute-start | bytes 1572872 | tf_op jit(solution)/shard_map/ppermute | solution.py:27
  43.5 0.5 collective-permute-done.7
  44.0 2.8 %collective-permute-start.9 = (bf16[32,512]{1,0:T(8,128)(2,1)S(1)}, bf16[32,512]{1,0:T(8,128)(2,1)S(1)}, u32[]{:S(2)}, u32[]{:S(2)}) collective-permute-start(bf16[32,512]{1,0:T(8,128)(2,1)S(1)} %broadcast_select_fusion), channel_id=1, source_target_pairs={{0,24},{8,0},{16,8},{24,16},{32,56},{40,32},{48,40},{56,48},{64,88... | collective-permute-start | bytes 98312 | tf_op jit(solution)/shard_map/ppermute | solution.py:25
  46.8 1.6 collective-permute-done.9
  48.4 3.5 %collective-permute-start.10 = (bf16[32,512]{1,0:T(8,128)(2,1)S(1)}, bf16[32,512]{1,0:T(8,128)(2,1)S(1)}, u32[]{:S(2)}, u32[]{:S(2)}) collective-permute-start(bf16[32,512]{1,0:T(8,128)(2,1)S(1)} %collective-permute-done.9), channel_id=1, source_target_pairs={{0,24},{8,0},{16,8},{24,16},{32,56},{40,32},{48,40},{56,48},{64,88... | collective-permute-start | bytes 98312 | tf_op jit(solution)/shard_map/ppermute | solution.py:25
  51.9 0.2 collective-permute-done.11
  52.1 1.4 collective-permute-done.10
  53.6 1.8 %collective-permute-done.12 = bf16[512,512]{1,0:T(8,128)(2,1)S(1)} collective-permute-done((bf16[512,512]{1,0:T(8,128)(2,1)S(1)}, bf16[512,512]{1,0:T(8,128)(2,1)S(1)}, u32[]{:S(2)}, u32[]{:S(2)}) %collective-permute-start.12) | collective-permute-done | bytes 524320 | tf_op jit(solution)/shard_map/ppermute | solution.py:27
  55.4 2.7 %collective-permute-done.13 = bf16[512,512]{1,0:T(8,128)(2,1)S(1)} collective-permute-done((bf16[512,512]{1,0:T(8,128)(2,1)S(1)}, bf16[512,512]{1,0:T(8,128)(2,1)S(1)}, u32[]{:S(2)}, u32[]{:S(2)}) %collective-permute-start.13) | collective-permute-done | bytes 524320 | tf_op jit(solution)/shard_map/ppermute | solution.py:27
  58.1 0.1 collective-permute-start.24
  58.2 2.1 %collective-permute-start.25 = (bf16[256,512]{1,0:T(8,128)(2,1)S(1)}, bf16[256,512]{1,0:T(8,128)(2,1)S(1)}, u32[]{:S(2)}, u32[]{:S(2)}) collective-permute-start(bf16[256,512]{1,0:T(8,128)(2,1)S(1)} %slice.66), channel_id=1, source_target_pairs={{0,6},{1,7},{2,0},{3,1},{4,2},{5,3},{6,4},{7,5},{8,14},{9,15},{10,... | collective-permute-start | bytes 786440 | tf_op jit(solution)/shard_map/ppermute | solution.py:27
  60.3 3.2 %collective-permute-start.18 = (bf16[3,32,512]{2,1,0:T(8,128)(2,1)S(1)}, bf16[3,32,512]{2,1,0:T(8,128)(2,1)S(1)}, u32[]{:S(2)}, u32[]{:S(2)}) collective-permute-start(bf16[3,32,512]{2,1,0:T(8,128)(2,1)S(1)} %pad_maximum_fusion.1), channel_id=1, source_target_pairs={{0,224},{8,232},{16,240},{24,248},{32,0},{40,8},{48,16},{56,24},{6... | collective-permute-start | bytes 294920 | tf_op jit(solution)/shard_map/ppermute | solution.py:23
  63.5 4.0 %collective-permute-done.14 = bf16[3,32,512]{2,1,0:T(8,128)(2,1)S(1)} collective-permute-done((bf16[3,32,512]{2,1,0:T(8,128)(2,1)S(1)}, bf16[3,32,512]{2,1,0:T(8,128)(2,1)S(1)}, u32[]{:S(2)}, u32[]{:S(2)}) %collective-permute-start.14) | collective-permute-done | bytes 98336 | tf_op jit(solution)/shard_map/ppermute | solution.py:23
  67.6 3.2 %collective-permute-start.19 = (bf16[3,32,512]{2,1,0:T(8,128)(2,1)S(1)}, bf16[3,32,512]{2,1,0:T(8,128)(2,1)S(1)}, u32[]{:S(2)}, u32[]{:S(2)}) collective-permute-start(bf16[3,32,512]{2,1,0:T(8,128)(2,1)S(1)} %collective-permute-done.18), channel_id=1, source_target_pairs={{0,224},{8,232},{16,240},{24,248},{32,0},{40,8},{48,16},{56,24},{6... | collective-permute-start | bytes 294920 | tf_op jit(solution)/shard_map/ppermute | solution.py:23
  70.9 0.3 pad_maximum_fusion.refs_8_
  71.1 0.1 collective-permute-start.26
  71.3 3.1 %collective-permute-done.15 = bf16[3,32,512]{2,1,0:T(8,128)(2,1)S(1)} collective-permute-done((bf16[3,32,512]{2,1,0:T(8,128)(2,1)S(1)}, bf16[3,32,512]{2,1,0:T(8,128)(2,1)S(1)}, u32[]{:S(2)}, u32[]{:S(2)}) %collective-permute-start.15) | collective-permute-done | bytes 98336 | tf_op jit(solution)/shard_map/ppermute | solution.py:23
  74.4 3.3 %collective-permute-start.20 = (bf16[3,32,512]{2,1,0:T(8,128)(2,1)S(1)}, bf16[3,32,512]{2,1,0:T(8,128)(2,1)S(1)}, u32[]{:S(2)}, u32[]{:S(2)}) collective-permute-start(bf16[3,32,512]{2,1,0:T(8,128)(2,1)S(1)} %collective-permute-done.19), channel_id=1, source_target_pairs={{0,224},{8,232},{16,240},{24,248},{32,0},{40,8},{48,16},{56,24},{6... | collective-permute-start | bytes 294920 | tf_op jit(solution)/shard_map/ppermute | solution.py:23
  77.7 2.6 %collective-permute-done.16 = bf16[3,32,512]{2,1,0:T(8,128)(2,1)S(1)} collective-permute-done((bf16[3,32,512]{2,1,0:T(8,128)(2,1)S(1)}, bf16[3,32,512]{2,1,0:T(8,128)(2,1)S(1)}, u32[]{:S(2)}, u32[]{:S(2)}) %collective-permute-start.16) | collective-permute-done | bytes 98336 | tf_op jit(solution)/shard_map/ppermute | solution.py:23
  80.4 0.0 copy-start.2
  80.4 0.1 collective-permute-start.17
  80.5 3.3 %collective-permute-start.21 = (bf16[3,16,512]{2,1,0:T(8,128)(2,1)S(1)}, bf16[3,16,512]{2,1,0:T(8,128)(2,1)S(1)}, u32[]{:S(2)}, u32[]{:S(2)}) collective-permute-start(bf16[3,16,512]{2,1,0:T(8,128)(2,1)S(1)} %slice.81), channel_id=1, source_target_pairs={{0,224},{8,232},{16,240},{24,248},{32,0},{40,8},{48,16},{56,24},{6... | collective-permute-start | bytes 147464 | tf_op jit(solution)/shard_map/ppermute | solution.py:23
  83.8 2.0 %collective-permute-done.17 = bf16[3,16,512]{2,1,0:T(8,128)(2,1)S(1)} collective-permute-done((bf16[3,16,512]{2,1,0:T(8,128)(2,1)S(1)}, bf16[3,16,512]{2,1,0:T(8,128)(2,1)S(1)}, u32[]{:S(2)}, u32[]{:S(2)}) %collective-permute-start.17) | collective-permute-done | bytes 49184 | tf_op jit(solution)/shard_map/ppermute | solution.py:23
  85.8 0.1 collective-permute-done.21
  85.9 1.2 collective-permute-start.22
  87.2 1.3 collective-permute-start.23
  88.5 16.4 %collective-permute-done.22.refs_1_ = bf16[8,3,32,512]{3,2,1,0:T(8,128)(2,1)S(1)} collective-permute-done((bf16[8,3,32,512]{3,2,1,0:T(8,128)(2,1)S(1)}, bf16[8,3,32,512]{3,2,1,0:T(8,128)(2,1)S(1)}, u32[]{:S(2)}, u32[]{:S(2)}) %collective-permute-start.22) | collective-permute-done | bytes 786464 | tf_op jit(solution)/shard_map/ppermute | solution.py:27
  104.9 3.0 %collective-permute-start.27 = (bf16[4,3,32,512]{3,2,1,0:T(8,128)(2,1)S(1)}, bf16[4,3,32,512]{3,2,1,0:T(8,128)(2,1)S(1)}, u32[]{:S(2)}, u32[]{:S(2)}) collective-permute-start(bf16[4,3,32,512]{3,2,1,0:T(8,128)(2,1)S(1)} %slice.67), channel_id=1, source_target_pairs={{0,2},{1,3},{2,4},{3,5},{4,6},{5,7},{6,0},{7,1},{8,10},{9,11},{10,... | collective-permute-start | bytes 1179656 | tf_op jit(solution)/shard_map/ppermute | solution.py:27
  108.0 0.1 collective-permute-start.28
  108.1 0.1 collective-permute-start.29
  108.2 0.5 collective-permute-start.30
  108.7 0.1 collective-permute-start.32
  108.8 5.7 %collective-permute-done.27 = bf16[4,3,32,512]{3,2,1,0:T(8,128)(2,1)S(1)} collective-permute-done((bf16[4,3,32,512]{3,2,1,0:T(8,128)(2,1)S(1)}, bf16[4,3,32,512]{3,2,1,0:T(8,128)(2,1)S(1)}, u32[]{:S(2)}, u32[]{:S(2)}) %collective-permute-start.27) | collective-permute-done | bytes 393248 | tf_op jit(solution)/shard_map/ppermute | solution.py:27
  114.5 3.2 %collective-permute-done.28 = bf16[4,3,32,512]{3,2,1,0:T(8,128)(2,1)S(1)} collective-permute-done((bf16[4,3,32,512]{3,2,1,0:T(8,128)(2,1)S(1)}, bf16[4,3,32,512]{3,2,1,0:T(8,128)(2,1)S(1)}, u32[]{:S(2)}, u32[]{:S(2)}) %collective-permute-start.28) | collective-permute-done | bytes 393248 | tf_op jit(solution)/shard_map/ppermute | solution.py:27
  117.7 0.1 collective-permute-start.31
  117.8 0.1 pad_add_fusion.ids
  117.9 2.2 %collective-permute-done.31.refs_6_ = bf16[8,3,32,512]{3,2,1,0:T(8,128)(2,1)S(1)} collective-permute-done((bf16[8,3,32,512]{3,2,1,0:T(8,128)(2,1)S(1)}, bf16[8,3,32,512]{3,2,1,0:T(8,128)(2,1)S(1)}, u32[]{:S(2)}, u32[]{:S(2)}) %collective-permute-start.31) | collective-permute-done | bytes 786464 | tf_op jit(solution)/shard_map/ppermute | solution.py:28
  120.1 5.9 %shard_map.46 = (bf16[3,512,1536]{2,1,0:T(8,128)(2,1)S(1)}, bf16[512,2048]{1,0:T(8,128)(2,1)S(1)}) custom-call(s32[2]{0:T(128)S(1)} %pad_add_fusion.ids, s32[32,32]{1,0:T(8,128)S(1)} %copy-done.2, bf16[8,3,32,512]{3,2,1,0:T(8,128)(2,1)S(1)} %bitcast_dynamic-update-slice_fusion.refs_0_, bf16[8,3,32,512]{3,2,1,0:T(8,128)(2,1)S(1)} %collective-permute-done.22.refs_1_, ...), custom_call_target="tpu_custom_call" | custom-call | flops 8053063680 | bytes 18874368 | tf_op jit(solution)/shard_map/pallas_call | solution.py:157
  126.0 2.2 %copy-done.4 = bf16[3,512,1536]{2,1,0:T(8,128)(2,1)} copy-done((bf16[3,512,1536]{2,1,0:T(8,128)(2,1)}, bf16[3,512,1536]{2,1,0:T(8,128)(2,1)S(1)}, u32[]{:S(2)}) %copy-start.4) | copy-done | bytes 4718616
  128.2 1.3 copy-done.5
  129.6 9.9 %all-gather.3.cloned.1.call-done = bf16[128,64,512]{2,1,0:T(8,128)(2,1)} async-done(((bf16[4,64,512]{2,1,0:T(8,128)(2,1)}), bf16[128,64,512]{2,1,0:T(8,128)(2,1)}) %all-gather.3.cloned.1.call-update) | async-done | bytes 8388624 | tf_op jit(solution)/shard_map/all_gather | solution.py:215
  139.5 20.6 %shard_map.47 = f32[512,4,512]{2,1,0:T(4,128)} custom-call(s32[2]{0:T(128)} %copy-done.3, s32[32,32]{1,0:T(8,128)} %shape.3, bf16[32,4,64,512]{3,2,1,0:T(8,128)(2,1)} %bitcast.81, bf16[4,512,512]{2,1,0:T(8,128)(2,1)} %bitcast.78, bf16[3,512,1536]{2,1,0:T(8,128)(2,1)} %copy-done.4, bf16[512,2048]{1,0:T(8,128)(2,1)} %copy-done.5, bf16[4,512,512]{2,1,0:T(8,128)(2,1)} %w.1), custom_call_target="tpu_custom_call" | custom-call | flops 15032385536 | bytes 25165824 | tf_op jit(solution)/shard_map/pallas_call | solution.py:175
  (52 shorter events, 0.4 us)
Async XLA Ops:
  6.5 132.9 %all-gather.3.cloned.1.call-start = ((), (), s32[]{:S(2)}) async-start(), calls=%async_computation | async-start | bytes 8650752 | tf_op jit(solution)/shard_map/all_gather | solution.py:215
  8.5 28.0 %copy-start.6 = (bf16[1,512,4,512]{3,1,2,0:T(8,128)(2,1)}, bf16[1,512,4,512]{3,1,2,0:T(8,128)(2,1)S(1)}, u32[]{:S(2)}) copy-start(bf16[1,512,4,512]{3,1,2,0:T(8,128)(2,1)S(1)} %copy.25) | copy-start | bytes 6291460
  9.8 14.5 %collective-permute-start.6 = (bf16[64,4,512]{2,0,1:T(8,128)(2,1)S(1)}, bf16[64,4,512]{2,0,1:T(8,128)(2,1)S(1)}, u32[]{:S(2)}, u32[]{:S(2)}) collective-permute-start(bf16[64,4,512]{2,0,1:T(8,128)(2,1)S(1)} %get-tuple-element.29), channel_id=1, source_target_pairs={{0,32},{8,40},{16,48},{24,56},{1,33},{9,41},{17,49},{25,57},{2,34}... | collective-permute-start | bytes 786440 | tf_op jit(solution)/shard_map/ppermute | solution.py:208
  13.6 12.7 %collective-permute-start = (bf16[64,4,512]{2,0,1:T(8,128)(2,1)S(1)}, bf16[64,4,512]{2,0,1:T(8,128)(2,1)S(1)}, u32[]{:S(2)}, u32[]{:S(2)}) collective-permute-start(bf16[64,4,512]{2,0,1:T(8,128)(2,1)S(1)} %get-tuple-element.35), channel_id=1, source_target_pairs={{0,224},{8,232},{16,240},{24,248},{1,225},{9,233},{17,241},{25,249... | collective-permute-start | bytes 786440 | tf_op jit(solution)/shard_map/ppermute | solution.py:208
  18.2 10.1 %collective-permute-start.1 = (bf16[64,4,512]{2,0,1:T(8,128)(2,1)}, bf16[64,4,512]{2,0,1:T(8,128)(2,1)}, u32[]{:S(2)}, u32[]{:S(2)}) collective-permute-start(bf16[64,4,512]{2,0,1:T(8,128)(2,1)} %get-tuple-element.34), channel_id=1, source_target_pairs={{0,64},{8,72},{16,80},{24,88},{1,65},{9,73},{17,81},{25,89},{2,66}... | collective-permute-start | bytes 786440 | tf_op jit(solution)/shard_map/ppermute | solution.py:208
  20.2 10.4 %collective-permute-start.2 = (bf16[64,4,512]{2,0,1:T(8,128)(2,1)}, bf16[64,4,512]{2,0,1:T(8,128)(2,1)}, u32[]{:S(2)}, u32[]{:S(2)}) collective-permute-start(bf16[64,4,512]{2,0,1:T(8,128)(2,1)} %get-tuple-element.33), channel_id=1, source_target_pairs={{0,192},{8,200},{16,208},{24,216},{1,193},{9,201},{17,209},{25,217... | collective-permute-start | bytes 786440 | tf_op jit(solution)/shard_map/ppermute | solution.py:208
  22.3 9.9 %collective-permute-start.3 = (bf16[64,4,512]{2,0,1:T(8,128)(2,1)}, bf16[64,4,512]{2,0,1:T(8,128)(2,1)}, u32[]{:S(2)}, u32[]{:S(2)}) collective-permute-start(bf16[64,4,512]{2,0,1:T(8,128)(2,1)} %get-tuple-element.32), channel_id=1, source_target_pairs={{0,96},{8,104},{16,112},{24,120},{1,97},{9,105},{17,113},{25,121},... | collective-permute-start | bytes 786440 | tf_op jit(solution)/shard_map/ppermute | solution.py:208
  24.3 4.0 %copy-start.7 = (bf16[64,4,512]{2,0,1:T(8,128)(2,1)}, bf16[64,4,512]{2,0,1:T(8,128)(2,1)S(1)}, u32[]{:S(2)}) copy-start(bf16[64,4,512]{2,0,1:T(8,128)(2,1)S(1)} %collective-permute-done.6) | copy-start | bytes 786436
  24.3 10.8 %collective-permute-start.4 = (bf16[64,4,512]{2,0,1:T(8,128)(2,1)}, bf16[64,4,512]{2,0,1:T(8,128)(2,1)}, u32[]{:S(2)}, u32[]{:S(2)}) collective-permute-start(bf16[64,4,512]{2,0,1:T(8,128)(2,1)} %get-tuple-element.31), channel_id=1, source_target_pairs={{0,160},{8,168},{16,176},{24,184},{1,161},{9,169},{17,177},{25,185... | collective-permute-start | bytes 786440 | tf_op jit(solution)/shard_map/ppermute | solution.py:208
  26.3 2.0 %copy-start.8 = (bf16[64,4,512]{2,0,1:T(8,128)(2,1)}, bf16[64,4,512]{2,0,1:T(8,128)(2,1)S(1)}, u32[]{:S(2)}) copy-start(bf16[64,4,512]{2,0,1:T(8,128)(2,1)S(1)} %collective-permute-done) | copy-start | bytes 786436
  26.3 10.3 %collective-permute-start.5 = (bf16[64,4,512]{2,0,1:T(8,128)(2,1)S(1)}, bf16[64,4,512]{2,0,1:T(8,128)(2,1)}, u32[]{:S(2)}, u32[]{:S(2)}) collective-permute-start(bf16[64,4,512]{2,0,1:T(8,128)(2,1)S(1)} %get-tuple-element.30), channel_id=1, source_target_pairs={{0,128},{8,136},{16,144},{24,152},{1,129},{9,137},{17,145},{25,153... | collective-permute-start | bytes 786440 | tf_op jit(solution)/shard_map/ppermute | solution.py:208
  38.2 5.8 %collective-permute-start.7 = (bf16[32,512]{1,0:T(8,128)(2,1)S(1)}, bf16[32,512]{1,0:T(8,128)(2,1)S(1)}, u32[]{:S(2)}, u32[]{:S(2)}) collective-permute-start(bf16[32,512]{1,0:T(8,128)(2,1)S(1)} %get-tuple-element.39), channel_id=1, source_target_pairs={{0,0},{1,2},{2,4},{3,6},{8,8},{9,10},{10,12},{11,14},{16,16},{17,1... | collective-permute-start | bytes 98312 | tf_op jit(solution)/shard_map/ppermute | solution.py:217
  39.5 4.5 %collective-permute-start.8 = (bf16[32,512]{1,0:T(8,128)(2,1)S(1)}, bf16[32,512]{1,0:T(8,128)(2,1)S(1)}, u32[]{:S(2)}, u32[]{:S(2)}) collective-permute-start(bf16[32,512]{1,0:T(8,128)(2,1)S(1)} %get-tuple-element.38), channel_id=1, source_target_pairs={{0,1},{1,3},{2,5},{3,7},{8,9},{9,11},{10,13},{11,15},{16,17},{17,1... | collective-permute-start | bytes 98312 | tf_op jit(solution)/shard_map/ppermute | solution.py:218
  40.1 15.2 %collective-permute-start.12 = (bf16[512,512]{1,0:T(8,128)(2,1)S(1)}, bf16[512,512]{1,0:T(8,128)(2,1)S(1)}, u32[]{:S(2)}, u32[]{:S(2)}) collective-permute-start(bf16[512,512]{1,0:T(8,128)(2,1)S(1)} %get-tuple-element.17), channel_id=1, source_target_pairs={{0,6},{1,7},{2,0},{3,1},{4,2},{5,3},{6,4},{7,5},{8,14},{9,15},{10,... | collective-permute-start | bytes 1572872 | tf_op jit(solution)/shard_map/ppermute | solution.py:27
  43.5 14.6 %collective-permute-start.13 = (bf16[512,512]{1,0:T(8,128)(2,1)S(1)}, bf16[512,512]{1,0:T(8,128)(2,1)S(1)}, u32[]{:S(2)}, u32[]{:S(2)}) collective-permute-start(bf16[512,512]{1,0:T(8,128)(2,1)S(1)} %get-tuple-element.17), channel_id=1, source_target_pairs={{0,2},{1,3},{2,4},{3,5},{4,6},{5,7},{6,0},{7,1},{8,10},{9,11},{10,... | collective-permute-start | bytes 1572872 | tf_op jit(solution)/shard_map/ppermute | solution.py:27
  44.0 4.4 %collective-permute-start.9 = (bf16[32,512]{1,0:T(8,128)(2,1)S(1)}, bf16[32,512]{1,0:T(8,128)(2,1)S(1)}, u32[]{:S(2)}, u32[]{:S(2)}) collective-permute-start(bf16[32,512]{1,0:T(8,128)(2,1)S(1)} %broadcast_select_fusion), channel_id=1, source_target_pairs={{0,24},{8,0},{16,8},{24,16},{32,56},{40,32},{48,40},{56,48},{64,88... | collective-permute-start | bytes 98312 | tf_op jit(solution)/shard_map/ppermute | solution.py:25
  46.8 5.3 %collective-permute-start.11 = (bf16[32,512]{1,0:T(8,128)(2,1)S(1)}, bf16[32,512]{1,0:T(8,128)(2,1)S(1)}, u32[]{:S(2)}, u32[]{:S(2)}) collective-permute-start(bf16[32,512]{1,0:T(8,128)(2,1)S(1)} %broadcast_select_fusion), channel_id=1, source_target_pairs={{0,8},{8,16},{16,24},{24,0},{32,40},{40,48},{48,56},{56,32},{64,72... | collective-permute-start | bytes 98312 | tf_op jit(solution)/shard_map/ppermute | solution.py:25
  48.4 5.1 %collective-permute-start.10 = (bf16[32,512]{1,0:T(8,128)(2,1)S(1)}, bf16[32,512]{1,0:T(8,128)(2,1)S(1)}, u32[]{:S(2)}, u32[]{:S(2)}) collective-permute-start(bf16[32,512]{1,0:T(8,128)(2,1)S(1)} %collective-permute-done.9), channel_id=1, source_target_pairs={{0,24},{8,0},{16,8},{24,16},{32,56},{40,32},{48,40},{56,48},{64,88... | collective-permute-start | bytes 98312 | tf_op jit(solution)/shard_map/ppermute | solution.py:25
  58.1 12.7 %collective-permute-start.24 = (bf16[256,512]{1,0:T(8,128)(2,1)S(1)}, bf16[256,512]{1,0:T(8,128)(2,1)S(1)}, u32[]{:S(2)}, u32[]{:S(2)}) collective-permute-start(bf16[256,512]{1,0:T(8,128)(2,1)S(1)} %slice.65), channel_id=1, source_target_pairs={{0,2},{1,3},{2,4},{3,5},{4,6},{5,7},{6,0},{7,1},{8,10},{9,11},{10,... | collective-permute-start | bytes 786440 | tf_op jit(solution)/shard_map/ppermute | solution.py:27
  58.2 12.6 %collective-permute-start.25 = (bf16[256,512]{1,0:T(8,128)(2,1)S(1)}, bf16[256,512]{1,0:T(8,128)(2,1)S(1)}, u32[]{:S(2)}, u32[]{:S(2)}) collective-permute-start(bf16[256,512]{1,0:T(8,128)(2,1)S(1)} %slice.66), channel_id=1, source_target_pairs={{0,6},{1,7},{2,0},{3,1},{4,2},{5,3},{6,4},{7,5},{8,14},{9,15},{10,... | collective-permute-start | bytes 786440 | tf_op jit(solution)/shard_map/ppermute | solution.py:27
  60.3 7.3 %collective-permute-start.14 = (bf16[3,32,512]{2,1,0:T(8,128)(2,1)S(1)}, bf16[3,32,512]{2,1,0:T(8,128)(2,1)S(1)}, u32[]{:S(2)}, u32[]{:S(2)}) collective-permute-start(bf16[3,32,512]{2,1,0:T(8,128)(2,1)S(1)} %pad_maximum_fusion.1), channel_id=1, source_target_pairs={{0,32},{8,40},{16,48},{24,56},{32,64},{40,72},{48,80},{56,88},{64,... | collective-permute-start | bytes 294920 | tf_op jit(solution)/shard_map/ppermute | solution.py:23
  60.3 7.3 %collective-permute-start.18 = (bf16[3,32,512]{2,1,0:T(8,128)(2,1)S(1)}, bf16[3,32,512]{2,1,0:T(8,128)(2,1)S(1)}, u32[]{:S(2)}, u32[]{:S(2)}) collective-permute-start(bf16[3,32,512]{2,1,0:T(8,128)(2,1)S(1)} %pad_maximum_fusion.1), channel_id=1, source_target_pairs={{0,224},{8,232},{16,240},{24,248},{32,0},{40,8},{48,16},{56,24},{6... | collective-permute-start | bytes 294920 | tf_op jit(solution)/shard_map/ppermute | solution.py:23
  67.6 6.8 %collective-permute-start.15 = (bf16[3,32,512]{2,1,0:T(8,128)(2,1)S(1)}, bf16[3,32,512]{2,1,0:T(8,128)(2,1)S(1)}, u32[]{:S(2)}, u32[]{:S(2)}) collective-permute-start(bf16[3,32,512]{2,1,0:T(8,128)(2,1)S(1)} %collective-permute-done.14), channel_id=1, source_target_pairs={{0,32},{8,40},{16,48},{24,56},{32,64},{40,72},{48,80},{56,88},{64,... | collective-permute-start | bytes 294920 | tf_op jit(solution)/shard_map/ppermute | solution.py:23
  67.6 6.8 %collective-permute-start.19 = (bf16[3,32,512]{2,1,0:T(8,128)(2,1)S(1)}, bf16[3,32,512]{2,1,0:T(8,128)(2,1)S(1)}, u32[]{:S(2)}, u32[]{:S(2)}) collective-permute-start(bf16[3,32,512]{2,1,0:T(8,128)(2,1)S(1)} %collective-permute-done.18), channel_id=1, source_target_pairs={{0,224},{8,232},{16,240},{24,248},{32,0},{40,8},{48,16},{56,24},{6... | collective-permute-start | bytes 294920 | tf_op jit(solution)/shard_map/ppermute | solution.py:23
  71.1 33.8 %collective-permute-start.26 = (bf16[4,512,512]{2,1,0:T(8,128)(2,1)S(1)}, bf16[4,512,512]{2,1,0:T(8,128)(2,1)S(1)}, u32[]{:S(2)}, u32[]{:S(2)}) collective-permute-start(bf16[4,512,512]{2,1,0:T(8,128)(2,1)S(1)} %pad_maximum_fusion.refs_8_), channel_id=1, source_target_pairs={{0,1},{1,0},{2,3},{3,2},{4,5},{5,4},{6,7},{7,6},{8,9},{9,8},{10,11... | collective-permute-start | bytes 6291464 | tf_op jit(solution)/shard_map/ppermute | solution.py:28
  74.4 6.0 %collective-permute-start.16 = (bf16[3,32,512]{2,1,0:T(8,128)(2,1)S(1)}, bf16[3,32,512]{2,1,0:T(8,128)(2,1)S(1)}, u32[]{:S(2)}, u32[]{:S(2)}) collective-permute-start(bf16[3,32,512]{2,1,0:T(8,128)(2,1)S(1)} %collective-permute-done.15), channel_id=1, source_target_pairs={{0,32},{8,40},{16,48},{24,56},{32,64},{40,72},{48,80},{56,88},{64,... | collective-permute-start | bytes 294920 | tf_op jit(solution)/shard_map/ppermute | solution.py:23
  74.4 6.1 %collective-permute-start.20 = (bf16[3,32,512]{2,1,0:T(8,128)(2,1)S(1)}, bf16[3,32,512]{2,1,0:T(8,128)(2,1)S(1)}, u32[]{:S(2)}, u32[]{:S(2)}) collective-permute-start(bf16[3,32,512]{2,1,0:T(8,128)(2,1)S(1)} %collective-permute-done.19), channel_id=1, source_target_pairs={{0,224},{8,232},{16,240},{24,248},{32,0},{40,8},{48,16},{56,24},{6... | collective-permute-start | bytes 294920 | tf_op jit(solution)/shard_map/ppermute | solution.py:23
  80.4 39.7 %copy-start = (bf16[4,512,512]{2,1,0:T(8,128)(2,1)S(1)}, bf16[4,512,512]{2,1,0:T(8,128)(2,1)}, u32[]{:S(2)}) copy-start(bf16[4,512,512]{2,1,0:T(8,128)(2,1)} %refs_10_.1) | copy-start | bytes 6291460
  80.4 39.7 %copy-start.1 = (bf16[4,512,512]{2,1,0:T(8,128)(2,1)S(1)}, bf16[4,512,512]{2,1,0:T(8,128)(2,1)}, u32[]{:S(2)}) copy-start(bf16[4,512,512]{2,1,0:T(8,128)(2,1)} %w.1) | copy-start | bytes 6291460
  80.4 39.7 %copy-start.2 = (s32[32,32]{1,0:T(8,128)S(1)}, s32[32,32]{1,0:T(8,128)}, u32[]{:S(2)}) copy-start(s32[32,32]{1,0:T(8,128)} %shape.3) | copy-start | bytes 12292
  80.4 5.4 %collective-permute-start.17 = (bf16[3,16,512]{2,1,0:T(8,128)(2,1)S(1)}, bf16[3,16,512]{2,1,0:T(8,128)(2,1)S(1)}, u32[]{:S(2)}, u32[]{:S(2)}) collective-permute-start(bf16[3,16,512]{2,1,0:T(8,128)(2,1)S(1)} %slice.80), channel_id=1, source_target_pairs={{0,32},{8,40},{16,48},{24,56},{32,64},{40,72},{48,80},{56,88},{64,... | collective-permute-start | bytes 147464 | tf_op jit(solution)/shard_map/ppermute | solution.py:23
  80.5 5.4 %collective-permute-start.21 = (bf16[3,16,512]{2,1,0:T(8,128)(2,1)S(1)}, bf16[3,16,512]{2,1,0:T(8,128)(2,1)S(1)}, u32[]{:S(2)}, u32[]{:S(2)}) collective-permute-start(bf16[3,16,512]{2,1,0:T(8,128)(2,1)S(1)} %slice.81), channel_id=1, source_target_pairs={{0,224},{8,232},{16,240},{24,248},{32,0},{40,8},{48,16},{56,24},{6... | collective-permute-start | bytes 147464 | tf_op jit(solution)/shard_map/ppermute | solution.py:23
  85.9 18.9 %collective-permute-start.22 = (bf16[8,3,32,512]{3,2,1,0:T(8,128)(2,1)S(1)}, bf16[8,3,32,512]{3,2,1,0:T(8,128)(2,1)S(1)}, u32[]{:S(2)}, u32[]{:S(2)}) collective-permute-start(bf16[8,3,32,512]{3,2,1,0:T(8,128)(2,1)S(1)} %bitcast_dynamic-update-slice_fusion.refs_0_), channel_id=1, source_target_pairs={{0,6},{1,7},{2,0},{3,1},{4,2},{5,3},{6,4},{7,5},{8,14},{9,15},{10,... | collective-permute-start | bytes 2359304 | tf_op jit(solution)/shard_map/ppermute | solution.py:27
  87.2 17.7 %collective-permute-start.23 = (bf16[8,3,32,512]{3,2,1,0:T(8,128)(2,1)S(1)}, bf16[8,3,32,512]{3,2,1,0:T(8,128)(2,1)S(1)}, u32[]{:S(2)}, u32[]{:S(2)}) collective-permute-start(bf16[8,3,32,512]{3,2,1,0:T(8,128)(2,1)S(1)} %bitcast_dynamic-update-slice_fusion.refs_0_), channel_id=1, source_target_pairs={{0,2},{1,3},{2,4},{3,5},{4,6},{5,7},{6,0},{7,1},{8,10},{9,11},{10,... | collective-permute-start | bytes 2359304 | tf_op jit(solution)/shard_map/ppermute | solution.py:27
  104.9 9.5 %collective-permute-start.27 = (bf16[4,3,32,512]{3,2,1,0:T(8,128)(2,1)S(1)}, bf16[4,3,32,512]{3,2,1,0:T(8,128)(2,1)S(1)}, u32[]{:S(2)}, u32[]{:S(2)}) collective-permute-start(bf16[4,3,32,512]{3,2,1,0:T(8,128)(2,1)S(1)} %slice.67), channel_id=1, source_target_pairs={{0,2},{1,3},{2,4},{3,5},{4,6},{5,7},{6,0},{7,1},{8,10},{9,11},{10,... | collective-permute-start | bytes 1179656 | tf_op jit(solution)/shard_map/ppermute | solution.py:27
  108.0 9.7 %collective-permute-start.28 = (bf16[4,3,32,512]{3,2,1,0:T(8,128)(2,1)S(1)}, bf16[4,3,32,512]{3,2,1,0:T(8,128)(2,1)S(1)}, u32[]{:S(2)}, u32[]{:S(2)}) collective-permute-start(bf16[4,3,32,512]{3,2,1,0:T(8,128)(2,1)S(1)} %slice.68), channel_id=1, source_target_pairs={{0,6},{1,7},{2,0},{3,1},{4,2},{5,3},{6,4},{7,5},{8,14},{9,15},{10,... | collective-permute-start | bytes 1179656 | tf_op jit(solution)/shard_map/ppermute | solution.py:27
  108.1 9.8 %collective-permute-start.29 = (bf16[8,3,32,512]{3,2,1,0:T(8,128)(2,1)S(1)}, bf16[8,3,32,512]{3,2,1,0:T(8,128)(2,1)S(1)}, u32[]{:S(2)}, u32[]{:S(2)}) collective-permute-start(bf16[8,3,32,512]{3,2,1,0:T(8,128)(2,1)S(1)} %bitcast_dynamic-update-slice_fusion.refs_0_), channel_id=1, source_target_pairs={{0,1},{1,0},{2,3},{3,2},{4,5},{5,4},{6,7},{7,6},{8,9},{9,8},{10,11... | collective-permute-start | bytes 2359304 | tf_op jit(solution)/shard_map/ppermute | solution.py:28
  108.2 9.7 %collective-permute-start.30 = (bf16[8,3,32,512]{3,2,1,0:T(8,128)(2,1)S(1)}, bf16[8,3,32,512]{3,2,1,0:T(8,128)(2,1)S(1)}, u32[]{:S(2)}, u32[]{:S(2)}) collective-permute-start(bf16[8,3,32,512]{3,2,1,0:T(8,128)(2,1)S(1)} %collective-permute-done.22.refs_1_), channel_id=1, source_target_pairs={{0,1},{1,0},{2,3},{3,2},{4,5},{5,4},{6,7},{7,6},{8,9},{9,8},{10,11... | collective-permute-start | bytes 2359304 | tf_op jit(solution)/shard_map/ppermute | solution.py:28
  108.7 9.2 %collective-permute-start.32 = (bf16[8,3,32,512]{3,2,1,0:T(8,128)(2,1)S(1)}, bf16[8,3,32,512]{3,2,1,0:T(8,128)(2,1)S(1)}, u32[]{:S(2)}, u32[]{:S(2)}) collective-permute-start(bf16[8,3,32,512]{3,2,1,0:T(8,128)(2,1)S(1)} %collective-permute-done.23.refs_3_), channel_id=1, source_target_pairs={{0,1},{1,0},{2,3},{3,2},{4,5},{5,4},{6,7},{7,6},{8,9},{9,8},{10,11... | collective-permute-start | bytes 2359304 | tf_op jit(solution)/shard_map/ppermute | solution.py:28
  117.7 2.4 %collective-permute-start.31 = (bf16[8,3,32,512]{3,2,1,0:T(8,128)(2,1)S(1)}, bf16[8,3,32,512]{3,2,1,0:T(8,128)(2,1)S(1)}, u32[]{:S(2)}, u32[]{:S(2)}) collective-permute-start(bf16[8,3,32,512]{3,2,1,0:T(8,128)(2,1)S(1)} %constant_dynamic-update-slice_fusion.refs_2_), channel_id=1, source_target_pairs={{0,1},{1,0},{2,3},{3,2},{4,5},{5,4},{6,7},{7,6},{8,9},{9,8},{10,11... | collective-permute-start | bytes 2359304 | tf_op jit(solution)/shard_map/ppermute | solution.py:28
  117.9 8.1 %copy-start.3 = (s32[2]{0:T(128)}, s32[2]{0:T(128)S(1)}, u32[]{:S(2)}) copy-start(s32[2]{0:T(128)S(1)} %pad_add_fusion.ids) | copy-start | bytes 28
  126.0 2.2 %copy-start.4 = (bf16[3,512,1536]{2,1,0:T(8,128)(2,1)}, bf16[3,512,1536]{2,1,0:T(8,128)(2,1)S(1)}, u32[]{:S(2)}) copy-start(bf16[3,512,1536]{2,1,0:T(8,128)(2,1)S(1)} %get-tuple-element.25.low) | copy-start | bytes 14155780
  128.2 1.3 copy-start.5
Sparse Core Ops, SparseCore 0:
  37.5 101.9 all-gather.2
